TPU v7x, 32 devices: a whole 2x2x4 slice. The times are simulated.
32 devices in a mesh: task: 4 (over y, x), batch: 8 (over z, core).
Axes of the slice: x: 2, y: 2, z: 4, core: 2. Of those that a mesh axis runs over, the one named last changes fastest.
Arguments:
- images: bfloat16 [32, 18, 24, 512], P(('task', 'batch')), may hold values from -6 to 6
- image_small: int32 [32], P(('task', 'batch')), may hold values from 0 to 1, as said below
- pool_index: int32 [32, 9, 12], P(('task', 'batch')), may hold values from 0 to 3
- row_slot: int32 [9216], replicated, may hold values from 0 to 9215, each once
- trunk_weight: float32 [9216, 512], P('batch'), may hold values from -0.09375 to 0.09375
- trunk_mean_grad: float32 [9216, 512], P('batch'), may hold values from -5.173322 to 5.173322
- trunk_mean_square: float32 [9216, 512], P('batch'), may hold values from 7.32672 to 116.1216
- trunk_statistic: float32 [2, 512, 512], replicated, as said below
- trunk_basis: float32 [2, 512, 512], replicated, as said below
- head_weight: float32 [4, 5632, 512], P('task', 'batch'), may hold values from -0.15625 to 0.15625
- head_mean_grad: float32 [4, 5632, 512], P('task', 'batch'), may hold values from -5.173322 to 5.173322
- head_mean_square: float32 [4, 5632, 512], P('task', 'batch'), may hold values from 7.32672 to 116.1216
- head_statistic: float32 [4, 3, 512, 512], P('task'), as said below
- head_basis: float32 [4, 3, 512, 512], P('task'), as said below
- trunk_gain: float32 [2, 512], replicated, may hold values from 0.5 to 1.5
- trunk_offset: float32 [2, 512], replicated, may hold values from -1.2 to 1.2
- trunk_norm_mean_grad: float32 [2, 2, 512], replicated, may hold values from -5.173322 to 5.173322
- trunk_norm_mean_square: float32 [2, 2, 512], replicated, may hold values from 7.32672 to 116.1216
- head_gain: float32 [4, 3, 512], P('task'), may hold values from 0.5 to 1.5
- head_offset: float32 [4, 3, 512], P('task'), may hold values from -1.2 to 1.2
- head_norm_mean_grad: float32 [4, 3, 2, 512], P('task'), may hold values from -5.173322 to 5.173322
- head_norm_mean_square: float32 [4, 3, 2, 512], P('task'), may hold values from 7.32672 to 116.1216
- cotangent: bfloat16 [4, 4, 8, 9, 12, 512], P('task', None, 'batch'), may hold values from -6 to 6
Outputs:
- task_features: bfloat16 [4, 4, 8, 9, 12, 512], P('task', None, 'batch')
- input_grad: float32 [32, 18, 24, 512], P(('task', 'batch'))
- trunk_weight_new: float32 [9216, 512], P('batch')
- trunk_mean_grad_new: float32 [9216, 512], P('batch')
- trunk_mean_square_new: float32 [9216, 512], P('batch')
- trunk_statistic_new: float32 [2, 512, 512], replicated
- trunk_basis_new: float32 [2, 512, 512], replicated
- head_weight_new: float32 [4, 5632, 512], P('task', 'batch')
- head_mean_grad_new: float32 [4, 5632, 512], P('task', 'batch')
- head_mean_square_new: float32 [4, 5632, 512], P('task', 'batch')
- head_statistic_new: float32 [4, 3, 512, 512], P('task')
- head_basis_new: float32 [4, 3, 512, 512], P('task')
- trunk_norm_new: float32 [2, 2, 512], replicated
- trunk_norm_mean_grad_new: float32 [2, 2, 512], replicated
- trunk_norm_mean_square_new: float32 [2, 2, 512], replicated
- head_norm_new: float32 [4, 3, 2, 512], P('task')
- head_norm_mean_grad_new: float32 [4, 3, 2, 512], P('task')
- head_norm_mean_square_new: float32 [4, 3, 2, 512], P('task')
Inputs may be any that keep to these rules, and one draw needn't show every extreme that they name: `image_small`: 1 marks a 144x192 image whose valid region is its first 9 rows and 12 columns; 0 marks a 288x384 image, valid everywhere. `pool_index`: which cell of a 2x2 window receives the value: 2 times the row offset plus the column offset. A permutation: row r of the stacked trunk kernels is held at row row_slot[r] of the slot-ordered arrays. `trunk_statistic`: each matrix is symmetric with a dominant positive diagonal. `head_statistic`: each matrix is symmetric with a dominant positive diagonal. `trunk_basis`: each matrix is orthogonal. `head_basis`: each matrix is orthogonal.
All inputs are finite; a program needn't handle non-finite values.
Results may differ from a plain program's by a relative error of at most 0.023.
Values may be sent and summed in bfloat16 or wider, within the bound.
A program may use at most 320 MiB of HBM per device.

v0:
```python
import functools

import jax
import jax.numpy as jnp
from jax import lax
from jax.experimental import pallas as pl
from jax.experimental.pallas import tpu as pltpu
from jax.sharding import PartitionSpec as P

STEP = 10


EPS = 1e-05
ADAM_EPS = 1e-08
BETA_ONE = 0.95
BETA_TWO = 0.95
STAT_DECAY = 0.95
LEARN_MATRIX = 0.02
LEARN_NORM = 0.5
DECAY_MATRIX = 0.01
BF = jnp.bfloat16
F32 = jnp.float32
MESH = pl.DeviceIdType.MESH
MIB = 1 << 20

VMEM_SPEC = pl.BlockSpec(memory_space=pltpu.VMEM)
SMEM_SPEC = pl.BlockSpec(memory_space=pltpu.SMEM)


def run(body, outs, specs, args, scratch=(), vmem=40, flops=0):
    size = sum(o.size * o.dtype.itemsize for o in outs) + sum(a.size * a.dtype.itemsize for a in args)
    return pl.pallas_call(
        body,
        out_shape=tuple(outs),
        in_specs=[SMEM_SPEC if s == "s" else VMEM_SPEC for s in specs],
        out_specs=tuple(VMEM_SPEC for _ in outs),
        scratch_shapes=list(scratch),
        compiler_params=pltpu.CompilerParams(vmem_limit_bytes=vmem * MIB),
        cost_estimate=pl.CostEstimate(flops=flops, bytes_accessed=size, transcendentals=0),
    )(*args)


def shape(dims, kind):
    return jax.ShapeDtypeStruct(tuple(dims), kind)


def dot(a, b):
    return jnp.dot(a, b, preferred_element_type=F32)


def dot_nt(a, b):
    return lax.dot_general(a, b, (((1,), (1,)), ((), ())), preferred_element_type=F32)


def dot_tn(a, b):
    return lax.dot_general(a, b, (((0,), (0,)), ((), ())), preferred_element_type=F32)


def split(a):
    high = a.astype(BF)
    return high, (a - high.astype(F32)).astype(BF)


def dot3(kind, a, b):
    dims = {dot: (1, 0), dot_nt: (1, 1), dot_tn: (0, 0)}[kind]
    a_high, a_low = split(a)
    b_high, b_low = split(b)
    return kind(
        jnp.concatenate([a_high, a_high, a_low], axis=dims[0]),
        jnp.concatenate([b_high, b_low, b_high], axis=dims[1]),
    )


def places(height, breadth):
    index = lax.broadcasted_iota(jnp.int32, (height * breadth, 1), 0)
    row = lax.div(index, breadth)
    return row, index - row * breadth


def valid_rows(kind, height, breadth):
    row, col = places(height, breadth)
    shrunk = kind > 0
    row_limit = jnp.where(shrunk, height // 2, height)
    col_limit = jnp.where(shrunk, breadth // 2, breadth)
    return jnp.where((row < row_limit) & (col < col_limit), 1.0, 0.0).astype(F32)


def move(values, rows):
    gap = jnp.zeros((abs(rows),) + values.shape[1:], values.dtype)
    if rows > 0:
        return jnp.concatenate([gap, values[:-rows]], axis=0)
    return jnp.concatenate([values[-rows:], gap], axis=0)


def from_left(values, col):
    return jnp.where(col > 0, pltpu.roll(values, 1, 0), 0.0)


def from_right(values, col, breadth):
    return jnp.where(col < breadth - 1, pltpu.roll(values, values.shape[0] - 1, 0), 0.0)


def gather_taps(tap, breadth, col):
    lines = [move(tap(b), breadth) + tap(3 + b) + move(tap(6 + b), -breadth) for b in range(3)]
    return lines[1] + from_left(lines[0], col) + from_right(lines[2], col, breadth)


def spread_taps(values, breadth, col):
    lines = [from_right(values, col, breadth), values, from_left(values, col)]
    return [
        move(lines[b], breadth * (a - 1)) if a != 1 else lines[b] for a in range(3) for b in range(3)
    ]


def window_sum(values, row, col, breadth):
    count = values.shape[0]
    pair = values + jnp.where(
        col % 2 == 0, pltpu.roll(values, count - 1, 0), pltpu.roll(values, 1, 0)
    )
    return pair + jnp.where(row % 2 == 0, move(pair, -breadth), move(pair, breadth))


def silu_back(scaled):
    sig = jax.nn.sigmoid(scaled)
    return sig * (1.0 + scaled * (1.0 - sig))


def col_sum(values):
    return jnp.sum(values, axis=0, keepdims=True)


def put_sums(ref, rows):
    width = ref.shape[1]
    rows = list(rows) + [jnp.zeros((1, width), F32)] * (8 - len(rows))
    ref[...] = jnp.concatenate(rows, axis=0)


def each_image(geometry, body, start):
    number, height, breadth = geometry
    pixels = height * breadth

    def step(image, carry):
        return body(image, pl.ds(pl.multiple_of(image * pixels, 16), pixels), carry)

    return lax.fori_loop(0, number, step, start)


def zero_rows(count, width):
    return (jnp.zeros((1, width), F32),) * count


def greet(axes):
    barrier = pltpu.get_barrier_semaphore()
    for axis, size in axes:
        me = lax.axis_index(axis)
        for step in range(1, size):
            pl.semaphore_signal(
                barrier, inc=1, device_id={axis: lax.rem(me + step, size)}, device_id_type=MESH
            )
    pl.semaphore_wait(barrier, sum(size - 1 for _, size in axes))


def remote(source, target, sends, receives, peer, axis):
    return pltpu.make_async_remote_copy(
        src_ref=source,
        dst_ref=target,
        send_sem=sends,
        recv_sem=receives,
        device_id={axis: peer},
        device_id_type=MESH,
    )


def pack(rows):
    parts = [row[:, i : i + 128] for row in rows for i in range(0, row.shape[1], 128)]
    parts += [jnp.zeros((1, 128), F32)] * (8 - len(parts))
    return jnp.concatenate(parts, axis=0)


def unpack(tile, count, width):
    per = width // 128
    return [
        jnp.concatenate([tile[k * per + i : k * per + i + 1, :] for i in range(per)], axis=1)
        for k in range(count)
    ]


def total_rows(k, axis, size, rows, mine, slots, sends, receives, meanwhile=None):
    me = lax.axis_index(axis)
    tile = pack(rows)
    mine[k] = tile
    slots[k, me] = tile
    for step in range(1, size):
        peer = lax.rem(me + step, size)
        remote(mine.at[k], slots.at[k, me], sends.at[k, step], receives.at[k, me], peer, axis).start()
    if meanwhile:
        meanwhile()
    for step in range(1, size):
        peer = lax.rem(me + size - step, size)
        remote(
            mine.at[k], slots.at[k, peer], sends.at[k, step], receives.at[k, peer], peer, axis
        ).wait_recv()
    total = slots[k, 0]
    for peer in range(1, size):
        total = total + slots[k, peer]
    for step in range(1, size):
        peer = lax.rem(me + step, size)
        remote(
            mine.at[k], slots.at[k, me], sends.at[k, step], receives.at[k, me], peer, axis
        ).wait_send()
    return unpack(total, len(rows), rows[0].shape[1])


def total_scratch(count, size):
    return [
        pltpu.VMEM((count, 8, 128), F32),
        pltpu.VMEM((count, size, 8, 128), F32),
        pltpu.SemaphoreType.DMA((count, size)),
        pltpu.SemaphoreType.DMA((count, size)),
    ]


def columns_of(place, width):
    return pl.ds(pl.multiple_of(place * width, 128), width)


SPECS = {"s": SMEM_SPEC, "v": VMEM_SPEC, "h": pl.BlockSpec(memory_space=pltpu.HBM)}


def exchange_kernel(body, outs, specs, args, scratch, identity, vmem, flops=0, places_out=None):
    size = sum(o.size * o.dtype.itemsize for o in outs) + sum(a.size * a.dtype.itemsize for a in args)
    return pl.pallas_call(
        body,
        out_shape=tuple(outs),
        in_specs=[SPECS[s] for s in specs],
        out_specs=tuple(SPECS[s] for s in places_out or "v" * len(outs)),
        scratch_shapes=list(scratch),
        compiler_params=pltpu.CompilerParams(
            vmem_limit_bytes=vmem * MIB, collective_id=identity, has_side_effects=True
        ),
        cost_estimate=pl.CostEstimate(flops=flops, bytes_accessed=size, transcendentals=0),
    )(*args)


def info_rows(infos, i):
    return infos[pl.ds(pl.multiple_of(i * 8, 8), 8), :]


def valid_of(infos, i, height, breadth):
    return valid_rows(info_rows(infos, i)[1:2, 0:1], height, breadth)


def chosen_cells(narrow, infos, i):
    return (narrow * info_rows(infos, i)[0:1, : narrow.shape[1]]).astype(BF)


def norm_with(values, totals, scale):
    total, squares, count = totals
    center = total / count
    inverse = lax.rsqrt(squares / count - center * center + EPS)
    normal = (values - center) * inverse
    return normal, inverse, normal * scale[0] + scale[1]


def norm_back_with(upstream, normal, inverse, count, sums, scale, valid):
    return scale[0] * inverse * (upstream - sums[0] / count - normal * (sums[1] / count)) * valid


def silu(values):
    return values * jax.nn.sigmoid(values)


def window_count(height, breadth):
    return -(-(height * breadth // 4) // 16) * 16


def pool_choice(height, breadth, windows, flipped):
    pixels = height * breadth
    dims = (windows, pixels) if flipped else (pixels, windows)
    pixel = lax.broadcasted_iota(jnp.int32, dims, 1 if flipped else 0)
    window = lax.broadcasted_iota(jnp.int32, dims, 0 if flipped else 1)
    row = lax.div(pixel, breadth)
    col = pixel - row * breadth
    home = lax.div(row, 2) * (breadth // 2) + lax.div(col, 2)
    return jnp.where(home == window, 1.0, 0.0).astype(F32)


def rows_of(ref, first, count):
    return [ref[first + k : first + k + 1, :] for k in range(count)]


def window_rows(i, windows):
    return pl.ds(pl.multiple_of(i * windows, 16), windows)


def trunk_forward_body(
    geometry, tasks, batches,
    index, infos, x, kernel_slots, scales,
    enc_totals, dec_totals, features, *rest,
):
    kept, (enc_pre, dec_pre, spread), rest = rest[:6], rest[6:9], rest[9:]
    (
        enc_taps, dec_taps, wide, tap,
        work, pooled, pooled_all, part, pool_sends, pool_receives, sends, receives,
    mine, slots, total_sends, total_receives, saved,
    ) = rest
    number, height, breadth = geometry
    width = enc_pre.shape[1]
    windows = window_count(height, breadth)
    task = lax.axis_index("task")
    _, col = places(height, breadth)
    choice = pool_choice(height, breadth, windows, True)
    narrow = choice.astype(BF)

    sources = (x, enc_taps, dec_taps, enc_pre, dec_pre, spread)
    saves = [pltpu.make_async_copy(a, b, saved.at[k]) for k, (a, b) in enumerate(zip(sources, kept))]
    saves[0].start()
    channels = x.shape[1]

    def widen(i, carry):
        rows = pl.ds(pl.multiple_of(i * channels, 16), channels)
        wide[rows, :] = kernel_slots[rows, :].astype(F32)
        return carry

    def fetch(taps, first, begin, end):
        group = 32
        for p in range(begin, end):

            def some(i, carry):
                base = i * group
                for u in range(group):
                    slot = index[(first + p) * channels + base + u]
                    tap[pl.ds(base + u, 1), :] = wide[pl.ds(slot, 1), :]
                return carry

            lax.fori_loop(0, channels // group, some, 0)
            taps[:, p * width : (p + 1) * width] = tap[...].astype(BF)

    lax.fori_loop(0, wide.shape[0] // channels, widen, 0)
    fetch(enc_taps, 0, 0, 9)
    saves[1].start()

    def conv(x, taps, pre):
        def image(i, rows, carry):
            valid = valid_of(infos, i, height, breadth)
            work[...] = dot(x[rows, :], taps[...])
            out = gather_taps(lambda p: work[:, p * width : (p + 1) * width], breadth, col)
            pre[rows, :] = out
            kept = out * valid
            return (
                carry[0] + col_sum(kept),
                carry[1] + col_sum(kept * out),
                carry[2] + jnp.broadcast_to(col_sum(valid), (1, width)),
            )

        return each_image(geometry, image, zero_rows(3, width))

    def total(k, rows, meanwhile=None):
        return total_rows(
            k, "batch", batches, list(rows), mine, slots, total_sends, total_receives, meanwhile
        )

    sums = conv(x, enc_taps, enc_pre)
    saves[3].start()
    greet((("task", tasks), ("batch", batches)))
    totals = total(0, sums, lambda: fetch(dec_taps, 9, 0, 4))
    put_sums(enc_totals, totals)
    scale = rows_of(scales, 0, 2)

    def peer_of(step, incoming):
        return lax.rem(task + (tasks - step if incoming else step), tasks)

    def pool_copy(i, step, incoming=False):
        rows = window_rows(i, windows)
        peer = peer_of(step, incoming)
        target = pooled_all.at[rows, columns_of(peer if incoming else task, width)]
        return remote(
            pooled.at[rows, :], target, pool_sends.at[i, step], pool_receives.at[i, step], peer, "task"
        )

    def pool(i, rows, carry):
        valid = valid_of(infos, i, height, breadth)
        _, _, scaled = norm_with(enc_pre[rows, :], totals, scale)
        high, low = split(silu(scaled) * valid)
        mean = ((dot(narrow, high) + dot(narrow, low)) * 0.25).astype(BF)
        here = window_rows(i, windows)
        pooled[here, :] = mean
        pooled_all[here, columns_of(task, width)] = mean
        for step in range(1, tasks):
            pool_copy(i, step).start()
        return carry

    each_image(geometry, pool, 0)
    fetch(dec_taps, 9, 4, 9)
    saves[2].start()

    def unpool(i, rows, carry):
        for step in range(1, tasks):
            pool_copy(i, step, True).wait_recv()
        wide = dot_tn(chosen_cells(choice, infos, i), pooled_all[window_rows(i, windows), :])
        spread[rows, :] = wide.astype(BF)
        return carry

    each_image(geometry, unpool, 0)
    saves[5].start()
    sums = conv(spread, dec_taps, dec_pre)
    saves[4].start()
    totals = total(1, sums)
    put_sums(dec_totals, totals)
    scale = rows_of(scales, 2, 2)

    def feature_copy(i, rows, step, incoming=False):
        peer = peer_of(step, incoming)
        target = features.at[rows, columns_of(peer if incoming else task, width)]
        return remote(
            part.at[rows, :], target, sends.at[i, step], receives.at[i, step], peer, "task"
        )

    def finish(i, rows, carry):
        valid = valid_of(infos, i, height, breadth)
        _, _, scaled = norm_with(dec_pre[rows, :], totals, scale)
        low = (silu(scaled) * valid).astype(BF)
        part[rows, :] = low
        features[rows, columns_of(task, width)] = low
        for step in range(1, tasks):
            feature_copy(i, rows, step).start()
        return carry

    each_image(geometry, finish, 0)

    def settle(i, rows, carry):
        for step in range(1, tasks):
            feature_copy(i, rows, step, True).wait_recv()
            feature_copy(i, rows, step).wait_send()
            pool_copy(i, step).wait_send()
        return carry

    each_image(geometry, settle, 0)
    for copy in saves:
        copy.wait()


def trunk_forward(geometry, tasks, batches, index, infos, x, kernel_slots, scales):
    number, height, breadth = geometry
    pixels = height * breadth
    channels = x.shape[1]
    width = channels // tasks
    windows = window_count(height, breadth)
    tall = shape((x.shape[0], width), F32)
    taps = shape((channels, 9 * width), BF)
    outs = [
        shape((8, width), F32), shape((8, width), F32), shape(x.shape, BF),
        shape(x.shape, BF), taps, taps,
        tall, tall, shape(x.shape, BF),
    ]
    return exchange_kernel(
        functools.partial(trunk_forward_body, geometry, tasks, batches),
        outs,
        "svvvv",
        (index, infos, x, kernel_slots, scales),
        [
            pltpu.VMEM(tall.shape, F32),
            pltpu.VMEM(tall.shape, F32),
            pltpu.VMEM(x.shape, BF),
            pltpu.VMEM(taps.shape, BF),
            pltpu.VMEM(taps.shape, BF),
            pltpu.VMEM(kernel_slots.shape, F32),
            pltpu.VMEM((channels, width), F32),
            pltpu.VMEM((pixels, 9 * width), F32),
            pltpu.VMEM((number * windows, width), BF),
            pltpu.VMEM((number * windows, channels), BF),
            pltpu.VMEM((x.shape[0], width), BF),
        ]
        + [pltpu.SemaphoreType.DMA((number, tasks))] * 4
        + total_scratch(2, batches)
        + [pltpu.SemaphoreType.DMA((6,))],
        1,
        60,
        flops=4 * x.size * taps.shape[1],
        places_out="vvvhhhhhh",
    )


def head_body(
    geometry, tasks, batches, summing,
    infos, features, weights, cotangent, scales, counts,
    task_out, upstream, norm_sums, *rest,
):
    grads_out, rest = rest[0], rest[1:]
    (
        grads, pre_one, pre_two, pre_three, hidden, gated, nine, work, lower, out, arrived,
        sends, receives, mine, slots, total_sends, total_receives, loaded,
    ) = rest[:18]
    number, height, breadth = geometry
    channels = features.shape[1]
    width = channels // tasks
    windows = task_out.shape[1]
    task = lax.axis_index("task")
    half = work.shape[2]
    _, col = places(height, breadth)
    widen = pool_choice(height, breadth, windows, False).astype(BF)
    narrow = pool_choice(height, breadth, windows, True).astype(BF)
    count = jnp.broadcast_to(counts[2:3, 0:1], (1, channels))
    cuts = (pl.ds(0, 2 * channels), pl.ds(2 * channels, 9 * channels))
    loads = [
        pltpu.make_async_copy(weights.at[cut, :], grads.at[cut, :], loaded.at[k])
        for k, cut in enumerate(cuts)
    ]
    for copy in loads:
        copy.start()
    first = grads.at[pl.ds(0, channels), :]
    second = grads.at[pl.ds(channels, channels), :]

    def kernel_rows(p):
        return pl.ds((2 + p) * channels, channels)

    def total(k, rows, meanwhile=None):
        return total_rows(
            k, "batch", batches, list(rows), mine, slots, total_sends, total_receives, meanwhile
        )

    if summing:
        near, near_sends, near_receives = rest[18:]
        place, core, chips = pair_place(batches)
        block = near.shape[1]

        def near_copy(chip):
            return remote(
                block_rows(grads, 2 * chip + 1 - core, block), near.at[chip],
                near_sends.at[chip], near_receives.at[chip], 2 * place + 1 - core, "batch",
            )

    def put_stats(pre, rows, value, valid, carry):
        pre[rows, :] = value
        kept = value * valid
        return carry[0] + col_sum(kept), carry[1] + col_sum(kept * value)

    nothing = zero_rows(2, channels)
    scale_one, scale_two, scale_three = (rows_of(scales, 2 * k, 2) for k in range(3))

    loads[0].wait()

    def first_step(i, rows, carry):
        valid = valid_of(infos, i, height, breadth)
        return put_stats(pre_one, rows, dot(features[rows, :], first[...]), valid, carry)

    sums = each_image(geometry, first_step, nothing)
    greet((("task", tasks), ("batch", batches)))
    totals_one = total(0, sums) + [count]

    def second_step(i, rows, carry):
        valid = valid_of(infos, i, height, breadth)
        _, _, scaled = norm_with(pre_one[rows, :], totals_one, scale_one)
        low = (silu(scaled) * valid).astype(BF)
        hidden[rows, :] = low
        return put_stats(pre_two, rows, dot(low, second[...]), valid, carry)

    sums = each_image(geometry, second_step, nothing)
    totals_two = total(1, sums) + [count]

    def third_step(i, rows, carry):
        valid = valid_of(infos, i, height, breadth)
        _, _, scaled = norm_with(pre_two[rows, :], totals_two, scale_two)
        low = (jax.nn.sigmoid(scaled) * features[rows, :].astype(F32)).astype(BF)
        gated[rows, :] = low
        parts = []
        for j in range(channels // half):
            cut = slice(j * half, (j + 1) * half)
            for p in range(9):
                work[p] = dot(low, grads[kernel_rows(p), cut])
            parts.append(gather_taps(lambda p: work[p], breadth, col))
        return put_stats(pre_three, rows, jnp.concatenate(parts, axis=1), valid, carry)

    loads[1].wait()
    sums = each_image(geometry, third_step, nothing)
    totals_three = total(2, sums) + [count]

    def out_step(i, rows, carry):
        valid = valid_of(infos, i, height, breadth)
        normal, _, scaled = norm_with(pre_three[rows, :], totals_three, scale_three)
        high, low = split(silu(scaled) * valid)
        mean = (dot(narrow, high) + dot(narrow, low)) * 0.25
        task_out[i] = mean.astype(BF)
        dy = silu_back(scaled) * dot(widen, cotangent[i]) * 0.25 * valid
        lower[rows, :] = dy
        return carry[0] + col_sum(dy), carry[1] + col_sum(dy * normal)

    sums = each_image(geometry, out_step, nothing)
    sums_three = total(3, sums)

    def third_back(i, rows, carry):
        valid = valid_of(infos, i, height, breadth)
        normal, inverse, _ = norm_with(pre_three[rows, :], totals_three, scale_three)
        dz = norm_back_with(lower[rows, :], normal, inverse, count, sums_three, scale_three, valid)
        for p, moved in enumerate(spread_taps(dz, breadth, col)):
            nine[p, rows, :] = moved.astype(BF)
        flow = None
        for p in range(9):
            piece = dot_nt(nine[p, rows, :], grads[kernel_rows(p), :])
            flow = piece if flow is None else flow + piece
        lower[rows, :] = flow
        normal, _, scaled = norm_with(pre_two[rows, :], totals_two, scale_two)
        gate = jax.nn.sigmoid(scaled)
        dy = flow * features[rows, :].astype(F32) * gate * (1.0 - gate) * valid
        pre_three[rows, :] = dy
        return carry[0] + col_sum(dy), carry[1] + col_sum(dy * normal)

    sums = each_image(geometry, third_back, nothing)

    def taps(begin, end):
        def tap(p, carry):
            rows = pl.ds(pl.multiple_of((2 + p) * channels, channels), channels)
            grads[rows, :] = dot_tn(gated[...], nine[p]).astype(BF)
            return carry

        lax.fori_loop(begin, end, tap, 0)

    sums_two = total(4, sums, lambda: taps(0, 4))

    def second_back(i, rows, carry):
        valid = valid_of(infos, i, height, breadth)
        normal, inverse, scaled = norm_with(pre_two[rows, :], totals_two, scale_two)
        dz = norm_back_with(
            pre_three[rows, :], normal, inverse, count, sums_two, scale_two, valid
        ).astype(BF)
        out[rows, :] = dz
        lower[rows, :] = lower[rows, :] * jax.nn.sigmoid(scaled)
        normal, _, scaled = norm_with(pre_one[rows, :], totals_one, scale_one)
        dy = silu_back(scaled) * dot_nt(dz, second[...]) * valid
        pre_three[rows, :] = dy
        return carry[0] + col_sum(dy), carry[1] + col_sum(dy * normal)

    sums = each_image(geometry, second_back, nothing)

    def weight_rows():
        grads[pl.ds(channels, channels), :] = dot_tn(hidden[...], out[...]).astype(BF)
        taps(4, 9)
        if summing:
            for chip in range(1, chips):
                near_copy(chip).start()

    sums_one = total(5, sums, weight_rows)

    def flow_copy(i, rows, step, incoming=False):
        peer = lax.rem(task + (tasks - step if incoming else step), tasks)
        return remote(
            out.at[rows, columns_of(peer, width)], arrived.at[step - 1, rows, :],
            sends.at[i, step], receives.at[i, step], peer, "task",
        )

    def first_back(i, rows, carry):
        valid = valid_of(infos, i, height, breadth)
        normal, inverse, _ = norm_with(pre_one[rows, :], totals_one, scale_one)
        dz = norm_back_with(
            pre_three[rows, :], normal, inverse, count, sums_one, scale_one, valid
        ).astype(BF)
        hidden[rows, :] = dz
        flow = (lower[rows, :] + dot_nt(dz, first[...])) * valid
        out[rows, :] = flow.astype(BF)
        for step in range(1, tasks):
            flow_copy(i, rows, step).start()
        return carry

    each_image(geometry, first_back, 0)
    grads[pl.ds(0, channels), :] = dot_tn(features[...], hidden[...]).astype(BF)
    if summing:
        near_copy(0).start()
        for chip in (*range(1, chips), 0):
            near_copy(chip).wait_recv()
            own = block_rows(grads, 2 * chip + core, block)[...].astype(F32)
            grads_out[chip] = (own + near[chip].astype(F32)).astype(BF)
    else:
        grads_out[...] = grads[...]
    put_sums(norm_sums, sums_one + sums_two + sums_three)

    def settle(i, rows, carry):
        for step in range(1, tasks):
            flow_copy(i, rows, step, True).wait_recv()
        flow = out[rows, columns_of(task, width)].astype(F32)
        for step in range(1, tasks):
            flow = flow + arrived[step - 1, rows, :].astype(F32)
        upstream[rows, :] = flow
        for step in range(1, tasks):
            flow_copy(i, rows, step).wait_send()
        return carry

    each_image(geometry, settle, 0)
    if summing:
        for chip in range(chips):
            near_copy(chip).wait_send()


def head(geometry, tasks, batches, infos, features, weights, cotangent, scales, counts):
    number, height, breadth = geometry
    pixels = height * breadth
    total, channels = features.shape
    width = channels // tasks
    block = weights.shape[0] // batches
    chips = batches // 2
    summing = block % 16 == 0
    outs = [
        shape((number, pixels // 4, channels), BF),
        shape((total, width), F32),
        shape((8, channels), F32),
        shape((chips, block, channels) if summing else weights.shape, BF),
    ]
    scratch = []
    if summing:
        scratch = [pltpu.VMEM((chips, block, channels), BF)]
        scratch += [pltpu.SemaphoreType.DMA((chips,))] * 2
    pooled, upstream, sums, grads = exchange_kernel(
        functools.partial(head_body, geometry, tasks, batches, summing),
        outs,
        "vvhvvv",
        (infos, features, weights, cotangent, scales, counts),
        [
            pltpu.VMEM(weights.shape, BF),
            pltpu.VMEM(features.shape, F32),
            pltpu.VMEM(features.shape, F32),
            pltpu.VMEM(features.shape, F32),
            pltpu.VMEM(features.shape, BF),
            pltpu.VMEM(features.shape, BF),
            pltpu.VMEM((9,) + features.shape, BF),
            pltpu.VMEM((9, pixels, min(channels, 256)), F32),
            pltpu.VMEM(features.shape, F32),
            pltpu.VMEM(features.shape, BF),
            pltpu.VMEM((tasks - 1, total, width), BF),
        ]
        + [pltpu.SemaphoreType.DMA((number, tasks))] * 2
        + total_scratch(6, batches)
        + [pltpu.SemaphoreType.DMA((2,))]
        + scratch,
        2,
        61,
        flops=6 * total * channels * weights.shape[0],
    )
    if summing:
        owned = lax.psum_scatter(
            grads.reshape(chips * block, channels), "batch", scatter_dimension=0,
            axis_index_groups=[list(range(core, batches, 2)) for core in range(2)], tiled=True,
        )
    else:
        owned = lax.psum_scatter(grads, "batch", scatter_dimension=0, tiled=True)
    return pooled, upstream, sums, owned


def trunk_backward_body(
    geometry, tasks, batches,
    infos, upstream, enc_totals, dec_totals, scales, *rest,
):
    kept, rest = rest[:6], rest[6:]
    (enc_grad, dec_grad, flow_out, norm_sums), rest = rest[:4], rest[4:]
    (x, enc_taps, dec_taps, enc_pre, dec_pre, spread), rest = rest[:6], rest[6:]
    (
        nine, change, packed, arrived, pooled, sends, receives,
        mine, slots, total_sends, total_receives, loaded,
    ) = rest
    targets = (x, enc_taps, dec_taps, enc_pre, dec_pre, spread)
    loads = [pltpu.make_async_copy(a, b, loaded.at[k]) for k, (a, b) in enumerate(zip(kept, targets))]
    for k in (4, 2, 5, 3, 1, 0):
        loads[k].start()
    number, height, breadth = geometry
    channels = x.shape[1]
    width = enc_pre.shape[1]
    windows = window_count(height, breadth)
    task = lax.axis_index("task")
    _, col = places(height, breadth)
    widen = pool_choice(height, breadth, windows, False).astype(BF)
    narrow = pool_choice(height, breadth, windows, True)
    nothing = zero_rows(2, width)

    def total(k, rows):
        return total_rows(
            k, "batch", batches, list(rows), mine, slots, total_sends, total_receives
        )

    def change_of(pre, totals, scale, flow):
        def image(i, rows, carry):
            valid = valid_of(infos, i, height, breadth)
            normal, _, scaled = norm_with(pre[rows, :], totals, scale)
            dy = silu_back(scaled) * flow(i, rows) * valid
            change[rows, :] = dy
            return carry[0] + col_sum(dy), carry[1] + col_sum(dy * normal)

        return each_image(geometry, image, nothing)

    def back(pre, totals, scale, sums, taps, put):
        def image(i, rows, carry):
            valid = valid_of(infos, i, height, breadth)
            normal, inverse, _ = norm_with(pre[rows, :], totals, scale)
            dz = norm_back_with(change[rows, :], normal, inverse, totals[2], sums, scale, valid)
            for p, moved in enumerate(spread_taps(dz, breadth, col)):
                nine[rows, p * width : (p + 1) * width] = moved.astype(BF)
            put(i, rows, dot_nt(nine[rows, :], taps[...]) * valid)
            return carry

        each_image(geometry, image, 0)

    totals = rows_of(dec_totals, 0, 3)
    scale = rows_of(scales, 2, 2)
    loads[4].wait()
    sums = change_of(dec_pre, totals, scale, lambda i, rows: upstream[rows, :])
    greet((("task", tasks), ("batch", batches)))
    dec_sums = total(0, sums)

    def copy_of(i, step, incoming=False):
        rows = window_rows(i, windows)
        peer = lax.rem(task + (tasks - step if incoming else step), tasks)
        return remote(
            packed.at[rows, columns_of(peer, width)], arrived.at[step - 1, rows, :],
            sends.at[i, step], receives.at[i, step], peer, "task",
        )

    def put_packed(i, rows, flow):
        chosen = chosen_cells(narrow, infos, i)
        packed[window_rows(i, windows), :] = dot(chosen, flow.astype(BF)).astype(BF)
        for step in range(1, tasks):
            copy_of(i, step).start()

    loads[2].wait()
    back(dec_pre, totals, scale, dec_sums, dec_taps, put_packed)
    loads[5].wait()
    dec_grad[...] = dot_tn(spread[...], nine[...])

    def collect(i, carry):
        for step in range(1, tasks):
            copy_of(i, step, True).wait_recv()
        rows = window_rows(i, windows)
        flow = packed[rows, columns_of(task, width)].astype(F32)
        for step in range(1, tasks):
            flow = flow + arrived[step - 1, rows, :].astype(F32)
        pooled[rows, :] = flow
        for step in range(1, tasks):
            copy_of(i, step).wait_send()
        return carry

    lax.fori_loop(0, number, collect, 0)

    def widened(i, rows):
        high, low = split(pooled[window_rows(i, windows), :])
        return (dot(widen, high) + dot(widen, low)) * 0.25

    totals = rows_of(enc_totals, 0, 3)
    scale = rows_of(scales, 0, 2)
    loads[3].wait()
    sums = change_of(enc_pre, totals, scale, widened)
    enc_sums = total(1, sums)

    def put_flow(i, rows, flow):
        flow_out[rows, :] = flow.astype(BF)

    loads[1].wait()
    back(enc_pre, totals, scale, enc_sums, enc_taps, put_flow)
    loads[0].wait()
    enc_grad[...] = dot_tn(x[...], nine[...])
    put_sums(norm_sums, enc_sums + dec_sums)


def trunk_backward(
    geometry, tasks, batches, infos, upstream, enc_totals, dec_totals, scales, kept
):
    number, height, breadth = geometry
    x, enc_taps, dec_taps = kept[:3]
    total, channels = x.shape
    width = channels // tasks
    windows = window_count(height, breadth)
    outs = [
        shape(enc_taps.shape, F32),
        shape(dec_taps.shape, F32),
        shape(x.shape, BF),
        shape((8, width), F32),
    ]
    return exchange_kernel(
        functools.partial(trunk_backward_body, geometry, tasks, batches),
        outs,
        "vvvvvhhhhhh",
        (infos, upstream, enc_totals, dec_totals, scales, *kept),
        [pltpu.VMEM(a.shape, a.dtype) for a in kept]
        + [
            pltpu.VMEM((total, 9 * width), BF),
            pltpu.VMEM((total, width), F32),
            pltpu.VMEM((number * windows, channels), BF),
            pltpu.VMEM((tasks - 1, number * windows, width), BF),
            pltpu.VMEM((number * windows, width), F32),
        ]
        + [pltpu.SemaphoreType.DMA((number, tasks))] * 2
        + total_scratch(2, batches)
        + [pltpu.SemaphoreType.DMA((6,))],
        3,
        60,
        flops=8 * x.size * enc_taps.shape[1],
    )


def to_slots_body(index, enc, dec, slots, wide):
    count = slots.shape[0]
    channels = enc.shape[0]
    width = slots.shape[1]
    step = 1024
    group = 32
    for p in range(18):
        source = enc if p < 9 else dec
        q = p % 9

        def place(i, carry):
            base = pl.multiple_of(i * group, group)
            values = source[pl.ds(base, group), q * width : (q + 1) * width]
            for u in range(group):
                wide[pl.ds(index[p * channels + base + u], 1), :] = values[u : u + 1, :]
            return carry

        lax.fori_loop(0, channels // group, place, 0)

    def narrow(i, carry):
        rows = pl.ds(pl.multiple_of(i * step, step), step)
        slots[rows, :] = wide[rows, :].astype(BF)
        return carry

    lax.fori_loop(0, count // step, narrow, 0)


def to_slots(index, enc, dec):
    width = enc.shape[1] // 9
    dims = (index.shape[0], width)
    return run(
        to_slots_body, [shape(dims, BF)], "svv", (index, enc, dec), [pltpu.VMEM(dims, F32)], vmem=60
    )[0]


def adam(gradient, moment_one, moment_two):
    new_one = BETA_ONE * moment_one + (1.0 - BETA_ONE) * gradient
    new_two = BETA_TWO * moment_two + (1.0 - BETA_TWO) * gradient * gradient
    direction = (
        new_one / (1.0 - BETA_ONE**STEP) / (jnp.sqrt(new_two / (1.0 - BETA_TWO**STEP)) + ADAM_EPS)
    )
    return new_one, new_two, direction


def pair_place(batches):
    me = lax.axis_index("batch")
    place = lax.div(me, 2)
    return place, me - 2 * place, batches // 2


def greet_pairs(tasks, batches):
    place, core, chips = pair_place(batches)
    task = lax.axis_index("task")
    barrier = pltpu.get_barrier_semaphore()

    def signal(device):
        pl.semaphore_signal(barrier, inc=1, device_id=device, device_id_type=MESH)

    for step in range(1, tasks):
        signal({"task": lax.rem(task + step, tasks)})
    signal({"batch": 2 * place + 1 - core})
    for step in range(1, chips):
        signal({"batch": 2 * lax.rem(place + step, chips) + core})
    pl.semaphore_wait(barrier, tasks - 1 + chips)


def block_rows(ref, index, count):
    return ref.at[pl.ds(pl.multiple_of(index * count, 8), count), :]


SMALL = 128 * 128


def far_first(chips):
    return sorted(range(chips), key=lambda step: -min(step, chips - step))


def pair_sum(batches, rows_of_block, own_block, near, paired, far, sems):
    place, core, chips = pair_place(batches)
    count = near.shape[1]
    near_send, near_receive, far_send, far_receive = sems
    other = 2 * place + 1 - core
    ring = chips == 4 and count % 32 == 0 and near.shape[2] * count > SMALL
    half = count // 2
    halves = (pl.ds(0, half), pl.ds(half, half))

    def near_copy(step):
        chip = lax.rem(place + step, chips)
        return remote(rows_of_block(2 * chip + 1 - core), near.at[step],
                      near_send.at[step], near_receive.at[step], other, "batch")

    def far_copy(step, incoming=False):
        chip = lax.rem(place + (chips - step if incoming else step), chips)
        return remote(paired.at[step], far.at[step], far_send.at[step], far_receive.at[step],
                      2 * chip + core, "batch")

    def ring_copy(which, way):
        chip = lax.rem(place + (1 if way == 0 else chips - 1), chips)
        if which == 0:
            source, target = paired.at[2, halves[way], :], far.at[2 + way, halves[0], :]
        else:
            cut = halves[way] if which == 2 else halves[1 - way]
            source, target = paired.at[1 if way == 0 else 3, cut, :], far.at[way, cut, :]
        k = 2 * which + way
        return remote(source, target, far_send.at[k], far_receive.at[k], 2 * chip + core, "batch")

    def start():
        for step in far_first(chips):
            near_copy(step).start()

    def middle():
        for step in far_first(chips):
            near_copy(step).wait_recv()
            if step:
                paired[step] = (own_block(step) + near[step].astype(F32)).astype(paired.dtype)
                if not ring:
                    far_copy(step).start()
                elif step == 2:
                    ring_copy(0, 0).start()
                    ring_copy(0, 1).start()
                else:
                    ring_copy(1, 0 if step == 1 else 1).start()

    def relay():
        if not ring:
            return
        for way in range(2):
            ring_copy(0, way).wait_recv()
            step = 1 if way == 0 else 3
            total = paired[step, halves[way], :].astype(F32) + far[2 + way, halves[0], :].astype(F32)
            paired[step, halves[way], :] = total.astype(paired.dtype)
            ring_copy(2, way).start()

    def end():
        total = own_block(0) + near[0].astype(F32)
        if ring:
            for way in range(2):
                ring_copy(1, way).wait_recv()
                ring_copy(2, way).wait_recv()
                total = total + far[way].astype(F32)
            for k in range(3):
                for way in range(2):
                    ring_copy(k, way).wait_send()
        else:
            for step in range(1, chips):
                far_copy(step, True).wait_recv()
                total = total + far[step].astype(F32)
            for step in range(1, chips):
                far_copy(step).wait_send()
        for step in range(chips):
            near_copy(step).wait_send()
        return total

    return start, middle, relay, end


def blocks_in(source, batches, count):
    place, core, chips = pair_place(batches)

    def own(step):
        chip = lax.rem(place + step, chips)
        return block_rows(source, 2 * chip + core, count)[...].astype(F32)

    return (lambda index: block_rows(source, index, count)), own


def pair_scratch(batches, rows, width, kind):
    chips = batches // 2
    return [pltpu.VMEM((chips, rows // batches, width), kind)] * 3 + [
        pltpu.SemaphoreType.DMA((max(chips, 6),))
    ] * 4


def chip_spread(batches, block, sends, receives):
    place, core, chips = pair_place(batches)
    count, width = block(place).shape
    ring = chips == 4 and count % 32 == 0 and width * count > SMALL
    half = count // 2

    def copy(step, incoming=False):
        peer = lax.rem(place + (chips - step if incoming else step), chips)
        ref = block(peer if incoming else place)
        return remote(ref, ref, sends.at[step], receives.at[step], 2 * peer + core, "batch")

    def pass_on(way, incoming=False):
        step = 1 if way == 0 else chips - 1
        peer = lax.rem(place + (chips - step if incoming else step), chips)
        home = lax.rem(place + (2 if incoming else chips - step), chips)
        ref = block(home).at[pl.ds(way * half, half), :]
        k = 2 if way == 0 else 0
        return remote(ref, ref, sends.at[k], receives.at[k], 2 * peer + core, "batch")

    steps = (1, chips - 1) if ring else tuple(range(1, chips))

    def start():
        for step in steps:
            copy(step).start()

    def relay():
        if ring:
            for way, step in enumerate(steps):
                copy(step, True).wait_recv()
                pass_on(way).start()

    def settle():
        if ring:
            for way in range(2):
                pass_on(way, True).wait_recv()
        else:
            for step in steps:
                copy(step, True).wait_recv()

    def drain():
        for step in steps:
            copy(step).wait_send()
        if ring:
            for way in range(2):
                pass_on(way).wait_send()

    return start, relay, settle, drain


def arrive_body(
    tasks, batches, geometry,
    image_raw, info, index, weight, head_weight,
    slots, x, infos, owners, head_low,
    image, head_raw, head_loaded, raw, raw_loaded, x_send, x_receive, info_send, info_receive,
    chip_send, chip_receive, pair_send, pair_receive, own,
):
    task = lax.axis_index("task")
    place, core, chips = pair_place(batches)
    count, width = raw.shape
    load = pltpu.make_async_copy(weight.at[:, columns_of(task, width)], raw, raw_loaded)
    load.start()
    head_load = pltpu.make_async_copy(head_weight, head_raw, head_loaded)
    head_load.start()
    number, height, breadth = geometry
    pixels = height * breadth
    for n in range(number):
        valid = valid_rows(info[8 * n + 1 : 8 * n + 2, 0:1], height, breadth)
        rows = slice(n * pixels, (n + 1) * pixels)
        image[rows, :] = (image_raw[rows, :].astype(F32) * valid).astype(BF)
    greet_pairs(tasks, batches)

    def task_copy(source, target, sends, receives, step, incoming=False):
        peer = lax.rem(task + (tasks - step if incoming else step), tasks)
        home = peer if incoming else task
        return remote(source, block_rows(target, home, source.shape[0]), sends.at[step],
                      receives.at[step], peer, "task")

    def moves(step, incoming=False):
        return (
            task_copy(info, infos, info_send, info_receive, step, incoming),
            task_copy(image, x, x_send, x_receive, step, incoming),
        )

    def block(chip):
        return block_rows(slots, 2 * chip + core, count)

    def pair_copy(hop, incoming=False):
        chip = lax.rem(place + chips - hop, chips)
        ref = block_rows(slots, 2 * chip + (1 - core if incoming else core), count)
        return remote(ref, ref, pair_send.at[hop], pair_receive.at[hop], 2 * place + 1 - core, "batch")

    start, relay, settle, drain = chip_spread(batches, block, chip_send, chip_receive)
    ring = chips == 4 and count % 32 == 0 and width * count > SMALL
    load.wait()
    block(place)[...] = raw[...].astype(BF)
    start()
    pair_copy(0).start()
    for step in range(1, tasks):
        for copy in moves(step):
            copy.start()
    locals_ = [
        pltpu.make_async_copy(image, block_rows(x, task, image.shape[0]), own.at[0]),
        pltpu.make_async_copy(info, block_rows(infos, task, info.shape[0]), own.at[1]),
    ]
    for copy in locals_:
        copy.start()
    mine = lax.broadcasted_iota(jnp.int32, (count, 1), 0) + lax.axis_index("batch") * count
    found = jnp.zeros((count, 128), F32)
    for k in range(index.shape[0] // 2, index.shape[0]):
        found = jnp.where(index[k : k + 1, :] == mine, 1.0, found)
    found = jnp.max(found, axis=1, keepdims=True)
    owners[:, 0:1] = 1.0 - found
    owners[:, 1:2] = found
    head_load.wait()
    head_low[...] = head_raw[...].astype(BF)
    relay()
    if ring:
        pair_copy(1).start()
        pair_copy(3).start()
        settle()
        pair_copy(2).start()
    else:
        settle()
        for hop in range(1, chips):
            pair_copy(hop).start()
    for copy in locals_:
        copy.wait()
    for step in range(1, tasks):
        for copy in moves(step, True):
            copy.wait_recv()
    for hop in range(chips):
        pair_copy(hop, True).wait_recv()
    for step in range(1, tasks):
        for copy in moves(step):
            copy.wait_send()
    for hop in range(chips):
        pair_copy(hop).wait_send()
    drain()


def arrive(tasks, batches, geometry, image, info, index, weight, head_weight):
    count, channels = weight.shape
    width = channels // tasks
    chips = batches // 2
    return exchange_kernel(
        functools.partial(arrive_body, tasks, batches, geometry),
        [
            shape((count * batches, width), BF),
            shape((image.shape[0] * tasks, channels), BF),
            shape((info.shape[0] * tasks, info.shape[1]), F32),
            shape((count, 2), F32),
            shape(head_weight.shape, BF),
        ],
        "vvvhh",
        (image, info, index.reshape(-1, 128), weight, head_weight),
        [
            pltpu.VMEM(image.shape, BF),
            pltpu.VMEM(head_weight.shape, F32),
            pltpu.SemaphoreType.DMA,
            pltpu.VMEM((count, width), F32),
            pltpu.SemaphoreType.DMA,
        ]
        + [pltpu.SemaphoreType.DMA((tasks,))] * 4
        + [pltpu.SemaphoreType.DMA((max(chips, 4),))] * 4
        + [pltpu.SemaphoreType.DMA((2,))],
        4,
        60,
        flops=20000 * MIB,
    )


def soap_rows(cuts, grad, owners, state, low, first, begin=0, end=None):
    total = grad.shape[0]

    def chunk(i, carry):
        rows = pl.ds(pl.multiple_of(i * (total // cuts), 8), total // cuts)
        values = grad[rows, :].astype(F32)
        marks = owners(i * (total // cuts), total // cuts)
        count = len(marks)
        rotated = None
        for m in range(count):
            part = dot((values * marks[m]).astype(BF), low[first + m])
            rotated = part if rotated is None else rotated + part
        new_one, new_two, direction = adam(rotated, state[1, rows, :], state[2, rows, :])
        state[1, rows, :] = new_one
        state[2, rows, :] = new_two
        stepped = None
        for m in range(count):
            part = dot_nt((direction * marks[m]).astype(BF), low[first + m])
            stepped = part if stepped is None else stepped + part
        old = state[0, rows, :]
        state[0, rows, :] = old - LEARN_MATRIX * (stepped + DECAY_MATRIX * old)
        return carry

    lax.fori_loop(begin, cuts if end is None else end, chunk, 0)


def factor_rows(values, identity, turn):
    size, width = values.shape
    sub = lax.broadcasted_iota(jnp.int32, (size, width), 0)
    rolled = pltpu.roll(values, turn, 1)
    columns = [jnp.broadcast_to(rolled[:, j : j + 1], (size, width)) for j in range(size)]
    scale = jnp.zeros((size, width), F32)
    for j in range(size):
        root = lax.rsqrt(columns[j][j : j + 1, :])
        scale = jnp.where(sub == j, root, scale)
        lower = jnp.where(sub > j, columns[j] * root, 0.0)
        values = values - lower * (values[j : j + 1, :] * root)
        identity = identity - lower * (identity[j : j + 1, :] * root)
        for i in range(j + 1, size):
            columns[i] = columns[i] - lower * (columns[i][j : j + 1, :] * root)
    return values * scale, identity * scale


GROUP = 16
PANEL = 128


def renew_panel(k, product, made, tables, inverses):
    count, size = product.shape[0], product.shape[1]
    here = slice(k * PANEL, (k + 1) * PANEL)
    row = lax.broadcasted_iota(jnp.int32, (PANEL, PANEL), 0)
    col = lax.broadcasted_iota(jnp.int32, (PANEL, PANEL), 1)
    unit = jnp.where(row == col, 1.0, 0.0).astype(F32)
    for n in range(count):
        tables[n][:, :PANEL] = dot3(dot_tn, product[n, :, here], product[n, :, here])
        tables[n][:, PANEL:] = unit

    def group(q, carry):
        rows = pl.ds(pl.multiple_of(q * GROUP, GROUP), GROUP)
        turn = lax.rem(PANEL - q * GROUP, PANEL)
        done = [
            factor_rows(tables[n][rows, :PANEL], tables[n][rows, PANEL:], turn)
            for n in range(count)
        ]
        for n in range(count):
            upper, inverse = done[n]
            inverses[n][rows, :] = inverse
            both = jnp.concatenate([upper, inverse], axis=1)
            tables[n][...] = tables[n][...] - dot3(dot_tn, upper, both)
        return carry

    lax.fori_loop(0, PANEL // GROUP, group, 0)
    for n in range(count):
        turned = dot3(dot_nt, product[n, :, here], inverses[n][...])
        made[n, :, here] = turned
        if k < size // PANEL - 1:
            rest = slice((k + 1) * PANEL, size)
            product[n, :, rest] = product[n, :, rest] - dot3(
                dot, turned, dot3(dot_tn, turned, product[n, :, rest])
            )


def tail_body(
    tasks, batches, cuts,
    slots, flow, sums, owners, head_grad,
    weight, one, two, head_weight, head_one, head_two, basis, head_basis,
    input_grad, norm_sums, state_new, head_state_new, grams, head_grams,
    grad, part, state, head_state, mine, head_mine, bases, low,
    flow_in, flow_send, flow_receive, send, receive, sum_send, sum_receive,
    *rest,
):
    row_scratch, gram_scratch, head_scratch = rest[:7], rest[7:14], rest[14:21]
    chip_send, chip_receive, task_send, task_receive, pair_send, pair_receive, load, save = rest[21:]
    task = lax.axis_index("task")
    place, core, chips = pair_place(batches)
    width = part.shape[1]
    channels = grad.shape[1]
    pixels = input_grad.shape[0]
    trunk_total = basis.shape[0]
    head_total = head_basis.shape[0]
    count, head_count = mine.shape[0] // batches, head_mine.shape[0] // batches

    def trunk_marks(start, size):
        rows = pl.ds(pl.multiple_of(start, 8), size)
        return [owners[rows, m : m + 1] for m in range(trunk_total)]

    def head_marks(start, size):
        index = lax.broadcasted_iota(jnp.int32, (size, 1), 0) + start
        index = index + lax.axis_index("batch") * head_grad.shape[0]
        owner = jnp.minimum(lax.div(index, channels), head_total - 1)
        return [jnp.where(owner == m, 1.0, 0.0).astype(F32) for m in range(head_total)]

    def put_grams(target, rows, columns, marks):
        for m, mark in enumerate(marks):
            held = (rows[...].astype(F32) * mark).astype(BF)
            target[m * channels : (m + 1) * channels, :] = dot_tn(held, columns[...]).astype(
                target.dtype
            )

    def peer_of(step, incoming):
        return lax.rem(task + (tasks - step if incoming else step), tasks)

    def flow_copy(step, incoming=False):
        peer = peer_of(step, incoming)
        return remote(block_rows(flow, peer, pixels), flow_in.at[step - 1], flow_send.at[step],
                      flow_receive.at[step], peer, "task")

    def sum_copy(step, incoming=False):
        peer = peer_of(step, incoming)
        home = peer if incoming else task
        return remote(sums, norm_sums.at[:, columns_of(home, width)], sum_send.at[step],
                      sum_receive.at[step], peer, "task")

    def part_copy(step, incoming=False):
        peer = peer_of(step, incoming)
        home = peer if incoming else task
        return remote(part, grad.at[:, columns_of(home, width)], send.at[step], receive.at[step],
                      peer, "task")

    def trunk_block(chip, home, which):
        rows = pl.ds(pl.multiple_of((2 * chip + which) * count, 8), count)
        return grams.at[rows, columns_of(home, width)]

    def head_block(chip, which):
        return block_rows(head_grams, 2 * chip + which, head_count)

    def task_copy(step, hop, incoming=False):
        peer = peer_of(step, incoming)
        chip = lax.rem(place + chips - hop, chips)
        block = trunk_block(chip, peer if incoming else task, core)
        return remote(block, block, task_send.at[step, hop], task_receive.at[step, hop], peer, "task")

    def pair_copy(kind, hop, incoming=False):
        chip = lax.rem(place + chips - hop, chips)
        which = 1 - core if incoming else core
        home = lax.rem(task + tasks - kind, tasks)
        block = head_block(chip, which) if kind == tasks else trunk_block(chip, home, which)
        return remote(block, block, pair_send.at[kind, hop], pair_receive.at[kind, hop],
                      2 * place + 1 - core, "batch")

    def sum_of(source, scratch):
        near, paired, far, *sems = scratch
        return pair_sum(
            batches, *blocks_in(source, batches, near.shape[1]), near, paired, far, sems
        )

    moves = [
        (basis, bases.at[pl.ds(0, trunk_total)]),
        (head_basis, bases.at[pl.ds(trunk_total, head_total)]),
        (head_weight, head_state.at[0]),
        (head_one, head_state.at[1]),
        (head_two, head_state.at[2]),
        (weight, state.at[0]),
        (one, state.at[1]),
        (two, state.at[2]),
    ]
    loads = [pltpu.make_async_copy(a, b, load.at[k]) for k, (a, b) in enumerate(moves)]
    for copy in loads:
        copy.start()
    saves = [
        pltpu.make_async_copy(state, state_new, save.at[0]),
        pltpu.make_async_copy(head_state, head_state_new, save.at[1]),
    ]

    greet_pairs(tasks, batches)
    row_start, row_middle, row_relay, row_end = sum_of(slots, row_scratch)
    row_start()
    for step in range(1, tasks):
        sum_copy(step).start()
        flow_copy(step).start()
    norm_sums[:, columns_of(task, width)] = sums[...]
    row_middle()
    put_grams(head_mine, head_grad, head_grad, head_marks(0, head_grad.shape[0]))
    head_start, head_middle, head_relay, head_end = sum_of(head_mine, head_scratch)
    head_start()
    row_relay()
    head_middle()
    for copy in loads[:5]:
        copy.wait()
    for m in range(trunk_total + head_total):
        low[m] = bases[m].astype(BF)
    total = row_end().astype(BF)
    part[...] = total
    for step in range(1, tasks):
        part_copy(step).start()
    grad[:, columns_of(task, width)] = total
    head_relay()

    soap_rows(cuts, head_grad, head_marks, head_state, low, trunk_total)
    saves[1].start()
    total = block_rows(flow, task, pixels)[...].astype(F32)
    for step in range(1, tasks):
        flow_copy(step, True).wait_recv()
        total = total + flow_in[step - 1].astype(F32)
    input_grad[...] = total
    head_block(place, core)[...] = head_end().astype(head_grams.dtype)
    trunk_spread = chip_spread(
        batches, lambda chip: trunk_block(chip, task, core), chip_send.at[0], chip_receive.at[0]
    )
    head_spread = chip_spread(
        batches, lambda chip: head_block(chip, core), chip_send.at[1], chip_receive.at[1]
    )
    head_spread[0]()
    pair_copy(tasks, 0).start()
    for step in range(1, tasks):
        part_copy(step, True).wait_recv()

    put_grams(mine, grad, part, trunk_marks(0, grad.shape[0]))
    start, middle, relay, end = sum_of(mine, gram_scratch)
    start()
    middle()
    head_spread[1]()
    for copy in loads[5:]:
        copy.wait()
    relay()
    soap_rows(cuts, grad, trunk_marks, state, low, 0, 0, cuts // 2)
    trunk_block(place, task, core)[...] = end().astype(grams.dtype)
    trunk_spread[0]()
    for step in range(1, tasks):
        task_copy(step, 0).start()
    pair_copy(0, 0).start()
    soap_rows(cuts, grad, trunk_marks, state, low, 0, cuts // 2, cuts)
    saves[0].start()
    trunk_spread[1]()
    trunk_spread[2]()
    for hop in range(1, chips):
        for step in range(1, tasks):
            task_copy(step, hop).start()
        pair_copy(0, hop).start()
    head_spread[2]()
    for hop in range(1, chips):
        pair_copy(tasks, hop).start()
    for hop in range(chips):
        for step in range(1, tasks):
            task_copy(step, hop, True).wait_recv()
            pair_copy(step, hop).start()
    for hop in range(chips):
        for kind in range(tasks + 1):
            pair_copy(kind, hop, True).wait_recv()
    for step in range(1, tasks):
        sum_copy(step, True).wait_recv()

    for copy in saves:
        copy.wait()
    for step in range(1, tasks):
        sum_copy(step).wait_send()
        part_copy(step).wait_send()
        flow_copy(step).wait_send()
    for hop in range(chips):
        for kind in range(tasks + 1):
            pair_copy(kind, hop).wait_send()
        for step in range(1, tasks):
            task_copy(step, hop).wait_send()
    trunk_spread[3]()
    head_spread[3]()


def renew_body(
    state, head_state, grams, head_grams, stat, head_stat, basis, head_basis,
    weight_new, one_new, two_new, head_weight_new, head_one_new, head_two_new,
    stat_new, head_stat_new, basis_new, head_basis_new,
    stats, product, made, held, head_held, load, save, *work,
):
    trunk_total, head_total = stat.shape[0], head_stat.shape[0]
    channels = stat.shape[1]
    count = trunk_total + head_total
    tables, inverses = work[:count], work[count:]
    loads = [
        pltpu.make_async_copy(state, held, load.at[0]),
        pltpu.make_async_copy(head_state, head_held, load.at[1]),
    ]
    for copy in loads:
        copy.start()
    sources = [held.at[k] for k in range(3)] + [head_held.at[k] for k in range(3)]
    targets = [weight_new, one_new, two_new, head_weight_new, head_one_new, head_two_new]
    saves = [pltpu.make_async_copy(a, b, save.at[k]) for k, (a, b) in enumerate(zip(sources, targets))]
    for m in range(count):
        first = m < trunk_total
        place = m if first else m - trunk_total
        gram = (grams if first else head_grams)[place * channels : (place + 1) * channels, :]
        old = (stat if first else head_stat)[place]
        stats[m] = STAT_DECAY * old + (1.0 - STAT_DECAY) * gram.astype(F32)
        product[m] = dot3(dot, stats[m], (basis if first else head_basis)[place])
    groups = ((0, trunk_total, stat_new, basis_new), (trunk_total, head_total, head_stat_new, head_basis_new))
    for begin, size, out, _ in groups:
        copy = pltpu.make_async_copy(stats.at[pl.ds(begin, size)], out, save.at[len(saves)])
        copy.start()
        saves.append(copy)
    for copy in loads:
        copy.wait()
    for copy in saves[:6]:
        copy.start()
    for k in range(channels // PANEL):
        renew_panel(k, product, made, tables, inverses)
        cut = pl.ds(k * PANEL, PANEL)
        for begin, size, _, out in groups:
            copy = pltpu.make_async_copy(
                made.at[pl.ds(begin, size), :, cut], out.at[:, :, cut], save.at[len(saves)]
            )
            copy.start()
            saves.append(copy)
    for copy in saves:
        copy.wait()


def finish(tasks, batches, local_grads, rows, matrices):
    slots, flow, sums, owners, head_grad = local_grads
    stat, head_stat, basis, head_basis = matrices
    total, channels = rows[0].shape
    width = channels // tasks
    trunk_total, head_total = basis.shape[0], head_basis.shape[0]
    gram_rows, head_rows = trunk_total * channels, head_total * channels
    chips = batches // 2
    kind = BF if gram_rows % (16 * batches) == 0 else F32
    head_kind = BF if head_rows % (16 * batches) == 0 else F32
    cuts = 4 if total % 64 == 0 and head_grad.shape[0] % 64 == 0 else 1
    square = (trunk_total + head_total, channels, channels)
    pixels = flow.shape[0] // tasks
    input_grad, norm_sums, *made = exchange_kernel(
        functools.partial(tail_body, tasks, batches, cuts),
        [
            shape((pixels, channels), F32),
            shape((8, channels), F32),
            shape((3, total, channels), F32),
            shape((3,) + head_grad.shape, F32),
            shape((gram_rows, channels), kind),
            shape((head_rows, channels), head_kind),
        ],
        "vvvvvhhhhhhhh",
        (*local_grads, *rows, basis, head_basis),
        [
            pltpu.VMEM((total, channels), BF),
            pltpu.VMEM((total, width), BF),
            pltpu.VMEM((3, total, channels), F32),
            pltpu.VMEM((3,) + head_grad.shape, F32),
            pltpu.VMEM((gram_rows, width), kind),
            pltpu.VMEM((head_rows, channels), head_kind),
            pltpu.VMEM(square, F32),
            pltpu.VMEM(square, BF),
            pltpu.VMEM((tasks - 1, pixels, channels), BF),
        ]
        + [pltpu.SemaphoreType.DMA((tasks,))] * 6
        + pair_scratch(batches, slots.shape[0], width, BF)
        + pair_scratch(batches, gram_rows, width, kind)
        + pair_scratch(batches, head_rows, channels, head_kind)
        + [pltpu.SemaphoreType.DMA((2, max(chips, 4)))] * 2
        + [pltpu.SemaphoreType.DMA((tasks, chips))] * 2
        + [pltpu.SemaphoreType.DMA((tasks + 1, chips))] * 2
        + [pltpu.SemaphoreType.DMA((8,)), pltpu.SemaphoreType.DMA((2,))],
        5,
        60,
        flops=50000 * MIB,
        places_out="vvhhvv",
    )
    outs = [shape(a.shape, F32) for a in (*rows, *matrices)]
    hbm = pl.BlockSpec(memory_space=pltpu.HBM)
    count = trunk_total + head_total
    results = pl.pallas_call(
        renew_body,
        out_shape=tuple(outs),
        in_specs=[hbm] * 2 + [VMEM_SPEC] * 6,
        out_specs=tuple(hbm for _ in outs),
        scratch_shapes=[pltpu.VMEM(square, F32)] * 3
        + [pltpu.VMEM(made[0].shape, F32), pltpu.VMEM(made[1].shape, F32)]
        + [pltpu.SemaphoreType.DMA((2,))]
        + [pltpu.SemaphoreType.DMA((8 + 2 * (channels // PANEL),))]
        + [pltpu.VMEM((PANEL, 2 * PANEL), F32)] * count
        + [pltpu.VMEM((PANEL, PANEL), F32)] * count,
        compiler_params=pltpu.CompilerParams(vmem_limit_bytes=60 * MIB),
        cost_estimate=pl.CostEstimate(
            flops=60000 * MIB, bytes_accessed=64 * MIB, transcendentals=0
        ),
    )(*made, *matrices)
    return input_grad, norm_sums, results


def local(
    tasks,
    batches,
    images,
    image_small,
    pool_index,
    row_slot,
    trunk_weight,
    trunk_mean_grad,
    trunk_mean_square,
    trunk_statistic,
    trunk_basis,
    head_weight,
    head_mean_grad,
    head_mean_square,
    head_statistic,
    head_basis,
    trunk_gain,
    trunk_offset,
    trunk_norm_mean_grad,
    trunk_norm_mean_square,
    head_gain,
    head_offset,
    head_norm_mean_grad,
    head_norm_mean_square,
    cotangent,
):
    number, height, breadth, channels = images.shape
    pixels = height * breadth
    shown = tasks * number
    geometry = (shown, height, breadth)
    task = lax.axis_index("task")
    width = channels // tasks

    def quarter(values):
        return lax.dynamic_slice_in_dim(values, task * width, width, values.ndim - 1)

    def inside(flags):
        row_limit = jnp.where(flags > 0, height // 2, height)[:, None, None]
        col_limit = jnp.where(flags > 0, breadth // 2, breadth)[:, None, None]
        return (jnp.arange(height, dtype=jnp.int32)[None, :, None] < row_limit) & (
            jnp.arange(breadth, dtype=jnp.int32)[None, None, :] < col_limit
        )

    cell = 2 * jnp.arange(2, dtype=jnp.int32)[:, None, None] + jnp.arange(2, dtype=jnp.int32)
    cells = pool_index.reshape(number, height // 2, 1, breadth // 2, 1)
    valid = inside(image_small)
    chosen = ((cells == cell).reshape(number, height, breadth) & valid).reshape(number, pixels)
    info = jnp.zeros((8 * number, channels), F32)
    info = info.at[::8, :pixels].set(chosen.astype(F32))
    info = info.at[1::8, 0].set(image_small.astype(F32))
    slots, x, infos, trunk_owners, head_low = arrive(
        tasks, batches, (number, height, breadth), images.reshape(number * pixels, channels),
        info, row_slot, trunk_weight, head_weight[0],
    )
    head_rows = lax.all_gather(head_low, "batch", axis=0, tiled=True)

    scales = quarter(jnp.stack([trunk_gain, trunk_offset], axis=1)).reshape(4, width)
    enc_totals, dec_totals, features, *kept = trunk_forward(
        geometry, tasks, batches, row_slot, infos, x, slots, scales
    )
    head_scales = jnp.stack([head_gain[0], head_offset[0]], axis=1).reshape(6, channels)
    pooled, upstream, head_sums, head_owned = head(
        geometry, tasks, batches, infos, features, head_rows,
        cotangent.reshape(shown, pixels // 4, channels), head_scales, enc_totals,
    )
    task_features = pooled.reshape(cotangent.shape)
    enc_grad, dec_grad, flow, trunk_sums = trunk_backward(
        geometry, tasks, batches, infos, upstream, enc_totals, dec_totals, scales, kept
    )
    input_grad, norm_sums, results = finish(
        tasks, batches,
        (to_slots(row_slot, enc_grad, dec_grad), flow, trunk_sums, trunk_owners, head_owned),
        (trunk_weight, trunk_mean_grad, trunk_mean_square,
         head_weight[0], head_mean_grad[0], head_mean_square[0]),
        (trunk_statistic, head_statistic[0], trunk_basis, head_basis[0]),
    )
    input_grad = input_grad.reshape(images.shape)
    (
        trunk_weight_new, trunk_one_new, trunk_two_new,
        head_weight_new, head_one_new, head_two_new,
        trunk_stat_new, head_stat_new, trunk_basis_new, head_basis_new,
    ) = results

    trunk_norm = jnp.stack([trunk_gain, trunk_offset], axis=1)
    trunk_norm_grad = norm_sums[:4].reshape(2, 2, channels)[:, ::-1]
    trunk_norm_one, trunk_norm_two, trunk_direction = adam(
        trunk_norm_grad, trunk_norm_mean_grad, trunk_norm_mean_square
    )
    head_norm = jnp.stack([head_gain, head_offset], axis=2)
    head_norm_grad = head_sums[:6].reshape(1, 3, 2, channels)[:, :, ::-1]
    head_norm_one, head_norm_two, head_direction = adam(
        head_norm_grad, head_norm_mean_grad, head_norm_mean_square
    )
    return (
        task_features,
        input_grad,
        trunk_weight_new,
        trunk_one_new,
        trunk_two_new,
        trunk_stat_new,
        trunk_basis_new,
        head_weight_new[None],
        head_one_new[None],
        head_two_new[None],
        head_stat_new[None],
        head_basis_new[None],
        trunk_norm - LEARN_NORM * trunk_direction,
        trunk_norm_one,
        trunk_norm_two,
        head_norm - LEARN_NORM * head_direction,
        head_norm_one,
        head_norm_two,
    )


def solution(mesh):
    placed = (
        P(("task", "batch"), None, None, None),
        P(("task", "batch")),
        P(("task", "batch"), None, None),
        P(),
        P("batch", None),
        P("batch", None),
        P("batch", None),
        P(),
        P(),
        P("task", "batch", None),
        P("task", "batch", None),
        P("task", "batch", None),
        P("task", None, None, None),
        P("task", None, None, None),
        P(),
        P(),
        P(),
        P(),
        P("task", None, None),
        P("task", None, None),
        P("task", None, None, None),
        P("task", None, None, None),
        P("task", None, "batch", None, None, None),
    )
    return jax.shard_map(
        functools.partial(local, mesh.shape["task"], mesh.shape["batch"]),
        mesh=mesh,
        in_specs=placed,
        out_specs=(
            P("task", None, "batch", None, None, None),
            P(("task", "batch"), None, None, None),
            P("batch", None),
            P("batch", None),
            P("batch", None),
            P(),
            P(),
            P("task", "batch", None),
            P("task", "batch", None),
            P("task", "batch", None),
            P("task", None, None, None),
            P("task", None, None, None),
            P(),
            P(),
            P(),
            P("task", None, None, None),
            P("task", None, None, None),
            P("task", None, None, None),
        ),
        check_vma=False,
    )
```

profile of v0, /device:TPU:0, one launch (start us, length us, event | category | flops | bytes accessed | tf_op | source)
XLA Modules:
  0.0 391.6 jit_solution(16538381445831468563)
XLA Ops:
  7.2 0.0 all-gather.2.cloned.1.call-start
  7.2 0.1 iota_add_fusion
  7.3 0.7 copy.62
  8.0 0.1 broadcast_compare_fusion
  8.1 0.1 eq.36
  8.9 0.1 and.51
  9.0 0.1 and.52
  9.1 0.1 and.54
  9.3 0.1 scatter.14.info
  9.3 0.0 copy-start.8
  9.4 0.6 copy-done.8
  10.0 0.0 copy-start.5
  10.0 0.0 copy-start.6
  10.0 0.0 copy-start.2
  10.0 0.0 copy-start.3
  10.0 0.0 copy-start.4
  10.0 31.2 %shard_map.358 = (bf16[9216,128]{1,0:T(8,128)(2,1)}, bf16[1728,512]{1,0:T(8,128)(2,1)}, f32[32,512]{1,0:T(8,128)}, f32[1152,2]{1,0:T(8,128)}, bf16[704,512]{1,0:T(8,128)(2,1)}) custom-call(bf16[432,512]{1,0:T(8,128)(2,1)} %bitcast.56, f32[8,512]{1,0:T(8,128)} %copy-done.8, s32[72,128]{1,0:T(8,128)} %bitcast.36, f32[1152,512]{1,0:T(8,128)} %weight.3, ...), custom_call_target="tpu_custom_call" | custom-call | flops 20971520000 | bytes 9221120 | tf_op jit(solution)/shard_map/pallas_call | solution.py:232
  41.2 0.0 all-gather.2.cloned.1.call-update
  41.2 0.2 reduce-scatter.2.cloned.1.call-start
  41.5 0.0 copy-done.5
  41.5 0.0 copy-done.6
  41.5 0.6 copy.43
  42.1 0.0 copy-done.2
  42.1 0.8 copy.44.cotangent
  42.9 0.0 copy-done.3
  42.9 0.0 copy-done.4
  42.9 0.6 reshape.259.scales
  43.6 55.3 %shard_map.359 = (f32[8,128]{1,0:T(8,128)}, f32[8,128]{1,0:T(8,128)}, bf16[1728,512]{1,0:T(8,128)(2,1)}, bf16[1728,512]{1,0:T(8,128)(2,1)}, bf16[512,1152]{1,0:T...) custom-call(s32[9216]{0:T(1024)} %index.3, ...), custom_call_target="tpu_custom_call" | custom-call | flops 4076863488 | bytes 13678592 | tf_op jit(solution)/shard_map/pallas_call | solution.py:232
  98.9 4.1 %all-gather.2.cloned.1.call-done.weights = bf16[5632,512]{1,0:T(8,128)(2,1)} async-done(((bf16[704,512]{1,0:T(8,128)(2,1)}), bf16[5632,512]{1,0:T(8,128)(2,1)}) %all-gather.2.cloned.1.call-update) | async-done | bytes 5767184 | tf_op jit(solution)/shard_map/all_gather | solution.py:1690
  103.0 89.4 %shard_map.360 = (bf16[4,108,512]{2,1,0:T(8,128)(2,1)}, f32[1728,128]{1,0:T(8,128)}, f32[8,512]{1,0:T(8,128)}, bf16[4,704,512]{2,1,0:T(8,128)(2,1)}) custom-call(f32[32,512]{1,0:T(8,128)} %get-tuple-element.80.infos, bf16[1728,512]{1,0:T(8,128)(2,1)} %get-tuple-element.83.features, bf16[5632,512]{1,0:T(8,128)(2,1)} %all-gather.2.cloned.1.call-done.weights, ...), custom_call_target="tpu_custom_call" | custom-call | flops 29896998912 | bytes 12288000 | tf_op jit(solution)/shard_map/pallas_call | solution.py:232
  192.4 0.0 copy-start.1
  192.4 0.0 copy-start.7
  192.4 0.0 reduce-scatter.2.cloned.1.call-update
  192.5 1.0 copy-done.1
  193.4 1.1 copy.45
  194.6 0.0 copy-done.7
  194.6 0.2 rev.7
  194.7 31.4 %shard_map.361 = (f32[512,1152]{1,0:T(8,128)}, f32[512,1152]{1,0:T(8,128)}, bf16[1728,512]{1,0:T(8,128)(2,1)}, f32[8,128]{1,0:T(8,128)}) custom-call(f32[32,512]{1,0:T(8,128)} %get-tuple-element.80.infos, f32[1728,128]{1,0:T(8,128)} %get-tuple-element.87.upstream, f32[8,128]{1,0:T(8,128)} %get-tuple-element.85.counts.enc_totals, ...), custom_call_target="tpu_custom_call" | custom-call | flops 8153726976 | bytes 15120384 | tf_op jit(solution)/shard_map/pallas_call | solution.py:232
  226.1 0.0 copy-start.9
  226.1 0.0 copy-start.10
  226.1 13.0 %shard_map.362.slots = bf16[9216,128]{1,0:T(8,128)(2,1)} custom-call(s32[9216]{0:T(1024)} %index.3, f32[512,1152]{1,0:T(8,128)} %get-tuple-element.95.enc, f32[512,1152]{1,0:T(8,128)} %get-tuple-element.96.dec), custom_call_target="tpu_custom_call" | custom-call | bytes 7114752 | tf_op jit(solution)/shard_map/pallas_call | solution.py:32
  239.2 0.0 copy-done.9
  239.2 0.0 copy-done.10
  239.2 0.7 maximum_subtract_fusion
  239.8 9.1 %reduce-scatter.2.cloned.1.call-done.head_grad = bf16[704,512]{1,0:T(8,128)(2,1)} async-done(((bf16[2816,512]{1,0:T(8,128)(2,1)}), bf16[704,512]{1,0:T(8,128)(2,1)}) %reduce-scatter.2.cloned.1.call-update) | async-done | bytes 720912 | tf_op jit(solution)/shard_map/reduce_scatter | solution.py:738
  248.9 0.0 copy-start.11
  248.9 0.0 copy-start.12
  248.9 70.4 %shard_map.363 = (f32[432,512]{1,0:T(8,128)}, f32[8,512]{1,0:T(8,128)}, f32[3,1152,512]{2,1,0:T(8,128)}, f32[3,704,512]{2,1,0:T(8,128)}, bf16[1024,512]{1,0:T(8,128)(2,1)}, /*index=5*/bf16[1536,512]{1,0:T(8,128)(2,1)}) custom-call(bf16[9216,128]{1,0:T(8,128)(2,1)} %shard_map.362.slots, bf16[1728,512]{1,0:T(8,128)(2,1)} %get-tuple-element.97.flow, ...), custom_call_target="tpu_custom_call" | custom-call | flops 52428800000 | bytes 36434944 | tf_op jit(solution)/shard_map/pallas_call | solution.py:232
  319.3 0.7 slice.41
  320.0 0.0 copy-done.11
  320.1 0.0 copy-done.12
  320.1 0.6 copy.49
  320.7 0.6 copy.50
  321.3 0.6 copy.51
  321.9 0.0 copy-start
  321.9 61.7 %shard_map.364 = (f32[1152,512]{1,0:T(8,128)}, f32[1152,512]{1,0:T(8,128)}, f32[1152,512]{1,0:T(8,128)}, f32[704,512]{1,0:T(8,128)}, f32[704,512]{1,0:T(8,128)},...) custom-call(f32[3,1152,512]{2,1,0:T(8,128)} %get-tuple-element.102.s, ...), custom_call_target="tpu_custom_call" | custom-call | flops 62914560000 | bytes 67108864 | tf_op jit(solution)/shard_map/pallas_call | solution.py:1616
  383.6 0.0 copy-done
  383.6 0.9 copy.66
  (12 shorter events, 0.1 us)
Async XLA Ops:
  7.2 95.8 %all-gather.2.cloned.1.call-start = ((), (), s32[]{:S(2)}) async-start(), calls=%async_computation.1 | async-start | bytes 6488064 | tf_op jit(solution)/shard_map/all_gather | solution.py:1690
  9.3 0.6 copy-start.8
  10.0 31.5 %copy-start.5 = (f32[2,512]{1,0:T(2,128)S(1)}, f32[2,512]{1,0:T(2,128)}, u32[]{:S(2)}) copy-start(f32[2,512]{1,0:T(2,128)} %param.41) | copy-start | bytes 12292
  10.0 31.5 %copy-start.6 = (f32[2,512]{1,0:T(2,128)S(1)}, f32[2,512]{1,0:T(2,128)}, u32[]{:S(2)}) copy-start(f32[2,512]{1,0:T(2,128)} %param.42) | copy-start | bytes 12292
  10.0 32.1 %copy-start.2 = (bf16[1,4,1,9,12,512]{5,1,4,3,2,0:T(4,128)(2,1)S(1)}, bf16[1,4,1,9,12,512]{5,1,4,3,2,0:T(4,128)(2,1)}, u32[]{:S(2)}) copy-start(bf16[1,4,1,9,12,512]{5,1,4,3,2,0:T(4,128)(2,1)} %param.49) | copy-start | bytes 1327108
  10.0 33.0 %copy-start.3 = (f32[1,3,512]{2,0,1:T(1,128)S(1)}, f32[1,3,512]{2,0,1:T(1,128)}, u32[]{:S(2)}) copy-start(f32[1,3,512]{2,0,1:T(1,128)} %param.46) | copy-start | bytes 18436
  10.0 33.0 %copy-start.4 = (f32[1,3,512]{2,0,1:T(1,128)S(1)}, f32[1,3,512]{2,0,1:T(1,128)}, u32[]{:S(2)}) copy-start(f32[1,3,512]{2,0,1:T(1,128)} %param.45) | copy-start | bytes 18436
  41.2 207.7 %reduce-scatter.2.cloned.1.call-start = ((), (), s32[]{:S(2)}) async-start(), calls=%async_computation.2 | async-start | bytes 3604480 | tf_op jit(solution)/shard_map/reduce_scatter | solution.py:738
  192.4 1.0 copy-start.1
  192.4 2.1 copy-start.7
  226.1 13.1 %copy-start.9 = (f32[1,3,2,512]{3,2,1,0:T(2,128)S(1)}, f32[1,3,2,512]{3,2,1,0:T(2,128)}, u32[]{:S(2)}) copy-start(f32[1,3,2,512]{3,2,1,0:T(2,128)} %param.47) | copy-start | bytes 36868
  226.1 13.1 %copy-start.10 = (f32[1,3,2,512]{3,2,1,0:T(2,128)S(1)}, f32[1,3,2,512]{3,2,1,0:T(2,128)}, u32[]{:S(2)}) copy-start(f32[1,3,2,512]{3,2,1,0:T(2,128)} %param.48) | copy-start | bytes 36868
  248.9 71.1 %copy-start.11 = (f32[2,2,512]{2,1,0:T(2,128)S(1)}, f32[2,2,512]{2,1,0:T(2,128)}, u32[]{:S(2)}) copy-start(f32[2,2,512]{2,1,0:T(2,128)} %param.43) | copy-start | bytes 24580
  248.9 71.1 %copy-start.12 = (f32[2,2,512]{2,1,0:T(2,128)S(1)}, f32[2,2,512]{2,1,0:T(2,128)}, u32[]{:S(2)}) copy-start(f32[2,2,512]{2,1,0:T(2,128)} %param.44) | copy-start | bytes 24580
  321.9 61.7 %copy-start = (f32[432,512]{1,0:T(8,128)S(1)}, f32[432,512]{1,0:T(8,128)}, u32[]{:S(2)}) copy-start(f32[432,512]{1,0:T(8,128)} %get-tuple-element.101) | copy-start | bytes 2654212
Sparse Core Ops, SparseCore 0:
  41.3 61.6 all-gather.1
  192.6 56.2 reduce-scatter.1
where the time goes:
time: 395 us; the launch traced here: 392 us
  Pallas kernels  352 us (89%)
  between operations  15.2 us (4%)
  waiting for transfers between devices  13.2 us (3%)
  local copies, waits for them, and re-layouts  9.6 us (2%)
    pallas_call x5, Pallas kernels, exchange_kernel(): pl.pallas_call(body, out_shape=tuple(outs), in_specs=[SPECS[s] for s in s...  278 us
    pallas_call x1, Pallas kernels, finish(): pl.pallas_call(renew_body, out_shape=tuple(outs), in_specs=[hbm] * 2 + [V...  61.7 us
    pallas_call x1, Pallas kernels, run(): pl.pallas_call(body, out_shape=tuple(outs), in_specs=[SMEM_SPEC if s == '...  13 us
    reduce_scatter x1, waiting for transfers between devices, head(): lax.psum_scatter(grads.reshape(chips * block, channels), 'batch', scatter...  9.08 us
  transfers between devices with their start and end apart: 2, of which 2 were waited for; matrix products, arithmetic and copies ran while one was open for 1% of the time, Pallas kernels for 25%

commit v1 on v0

--- a/solution.py
+++ b/solution.py
@@ -615,7 +615,7 @@
 
         lax.fori_loop(begin, end, tap, 0)
 
-    sums_two = total(4, sums, lambda: taps(0, 4))
+    sums_two = total(4, sums, lambda: taps(0, 3))
 
     def second_back(i, rows, carry):
         valid = valid_of(infos, i, height, breadth)
@@ -634,10 +634,7 @@
 
     def weight_rows():
         grads[pl.ds(channels, channels), :] = dot_tn(hidden[...], out[...]).astype(BF)
-        taps(4, 9)
-        if summing:
-            for chip in range(1, chips):
-                near_copy(chip).start()
+        taps(3, 5)
 
     sums_one = total(5, sums, weight_rows)
 
@@ -662,6 +659,10 @@
         return carry
 
     each_image(geometry, first_back, 0)
+    taps(5, 9)
+    if summing:
+        for chip in range(1, chips):
+            near_copy(chip).start()
     grads[pl.ds(0, channels), :] = dot_tn(features[...], hidden[...]).astype(BF)
     if summing:
         near_copy(0).start()
@@ -1048,14 +1049,18 @@
     return start, middle, relay, end
 
 
-def blocks_in(source, batches, count):
+def blocks_in(source, batches, count, piece=0, pieces=1):
     place, core, chips = pair_place(batches)
+
+    def rows(index):
+        start = (index * pieces + piece) * count
+        return source.at[pl.ds(pl.multiple_of(start, 8), count), :]
 
     def own(step):
         chip = lax.rem(place + step, chips)
-        return block_rows(source, 2 * chip + core, count)[...].astype(F32)
-
-    return (lambda index: block_rows(source, index, count)), own
+        return rows(2 * chip + core)[...].astype(F32)
+
+    return rows, own
 
 
 def pair_scratch(batches, rows, width, kind):
@@ -1319,7 +1324,7 @@
 
 
 def tail_body(
-    tasks, batches, cuts,
+    tasks, batches, cuts, pieces,
     slots, flow, sums, owners, head_grad,
     weight, one, two, head_weight, head_one, head_two, basis, head_basis,
     input_grad, norm_sums, state_new, head_state_new, grams, head_grams,
@@ -1327,8 +1332,9 @@
     flow_in, flow_send, flow_receive, send, receive, sum_send, sum_receive,
     *rest,
 ):
-    row_scratch, gram_scratch, head_scratch = rest[:7], rest[7:14], rest[14:21]
-    chip_send, chip_receive, task_send, task_receive, pair_send, pair_receive, load, save = rest[21:]
+    row_scratch = [rest[7 * k : 7 * k + 7] for k in range(pieces)]
+    gram_scratch, head_scratch, rest = rest[7 * pieces :][:7], rest[7 * pieces + 7 :][:7], rest[7 * pieces + 14 :]
+    chip_send, chip_receive, task_send, task_receive, pair_send, pair_receive, load, save = rest
     task = lax.axis_index("task")
     place, core, chips = pair_place(batches)
     width = part.shape[1]
@@ -1369,11 +1375,11 @@
         return remote(sums, norm_sums.at[:, columns_of(home, width)], sum_send.at[step],
                       sum_receive.at[step], peer, "task")
 
-    def part_copy(step, incoming=False):
+    def part_copy(k, step, incoming=False):
         peer = peer_of(step, incoming)
         home = peer if incoming else task
-        return remote(part, grad.at[:, columns_of(home, width)], send.at[step], receive.at[step],
-                      peer, "task")
+        return remote(part.at[part_rows(k), :], grad.at[part_rows(k), columns_of(home, width)],
+                      send.at[k, step], receive.at[k, step], peer, "task")
 
     def trunk_block(chip, home, which):
         rows = pl.ds(pl.multiple_of((2 * chip + which) * count, 8), count)
@@ -1396,11 +1402,15 @@
         return remote(block, block, pair_send.at[kind, hop], pair_receive.at[kind, hop],
                       2 * place + 1 - core, "batch")
 
-    def sum_of(source, scratch):
+    def sum_of(source, scratch, piece=0, total=1):
         near, paired, far, *sems = scratch
         return pair_sum(
-            batches, *blocks_in(source, batches, near.shape[1]), near, paired, far, sems
+            batches, *blocks_in(source, batches, near.shape[1], piece, total), near, paired, far, sems
         )
+
+    def part_rows(k):
+        size = part.shape[0] // pieces
+        return pl.ds(k * size, size)
 
     moves = [
         (basis, bases.at[pl.ds(0, trunk_total)]),
@@ -1421,27 +1431,33 @@
     ]
 
     greet_pairs(tasks, batches)
-    row_start, row_middle, row_relay, row_end = sum_of(slots, row_scratch)
-    row_start()
+    row_sums = [sum_of(slots, row_scratch[k], k, pieces) for k in range(pieces)]
+    for stages in row_sums:
+        stages[0]()
     for step in range(1, tasks):
         sum_copy(step).start()
         flow_copy(step).start()
     norm_sums[:, columns_of(task, width)] = sums[...]
-    row_middle()
+    row_sums[0][1]()
     put_grams(head_mine, head_grad, head_grad, head_marks(0, head_grad.shape[0]))
     head_start, head_middle, head_relay, head_end = sum_of(head_mine, head_scratch)
+    row_sums[0][2]()
+    for stages in row_sums[1:]:
+        stages[1]()
     head_start()
-    row_relay()
+    for stages in row_sums[1:]:
+        stages[2]()
     head_middle()
     for copy in loads[:5]:
         copy.wait()
     for m in range(trunk_total + head_total):
         low[m] = bases[m].astype(BF)
-    total = row_end().astype(BF)
-    part[...] = total
-    for step in range(1, tasks):
-        part_copy(step).start()
-    grad[:, columns_of(task, width)] = total
+    for k, stages in enumerate(row_sums):
+        total = stages[3]().astype(BF)
+        part[part_rows(k), :] = total
+        for step in range(1, tasks):
+            part_copy(k, step).start()
+        grad[part_rows(k), columns_of(task, width)] = total
     head_relay()
 
     soap_rows(cuts, head_grad, head_marks, head_state, low, trunk_total)
@@ -1460,8 +1476,9 @@
     )
     head_spread[0]()
     pair_copy(tasks, 0).start()
-    for step in range(1, tasks):
-        part_copy(step, True).wait_recv()
+    for k in range(pieces):
+        for step in range(1, tasks):
+            part_copy(k, step, True).wait_recv()
 
     put_grams(mine, grad, part, trunk_marks(0, grad.shape[0]))
     start, middle, relay, end = sum_of(mine, gram_scratch)
@@ -1502,7 +1519,8 @@
         copy.wait()
     for step in range(1, tasks):
         sum_copy(step).wait_send()
-        part_copy(step).wait_send()
+        for k in range(pieces):
+            part_copy(k, step).wait_send()
         flow_copy(step).wait_send()
     for hop in range(chips):
         for kind in range(tasks + 1):
@@ -1517,34 +1535,47 @@
     state, head_state, grams, head_grams, stat, head_stat, basis, head_basis,
     weight_new, one_new, two_new, head_weight_new, head_one_new, head_two_new,
     stat_new, head_stat_new, basis_new, head_basis_new,
-    stats, product, made, held, head_held, load, save, *work,
+    stats, product, made, low_grams, low_head_grams, held, head_held, load, save, *work,
 ):
     trunk_total, head_total = stat.shape[0], head_stat.shape[0]
     channels = stat.shape[1]
     count = trunk_total + head_total
     tables, inverses = work[:count], work[count:]
-    loads = [
-        pltpu.make_async_copy(state, held, load.at[0]),
-        pltpu.make_async_copy(head_state, head_held, load.at[1]),
-    ]
-    for copy in loads:
+    loads = []
+
+    def bring(source, target):
+        copy = pltpu.make_async_copy(source, target, load.at[len(loads)])
         copy.start()
+        loads.append(copy)
+
+    for m in range(count):
+        first = m < trunk_total
+        place = m if first else m - trunk_total
+        rows = pl.ds(place * channels, channels)
+        here, there = (grams, low_grams) if first else (head_grams, low_head_grams)
+        bring(here.at[rows, :], there.at[rows, :])
+        bring((stat if first else head_stat).at[place], stats.at[m])
+        bring((basis if first else head_basis).at[place], made.at[m])
+    bring(state, held)
+    bring(head_state, head_held)
     sources = [held.at[k] for k in range(3)] + [head_held.at[k] for k in range(3)]
     targets = [weight_new, one_new, two_new, head_weight_new, head_one_new, head_two_new]
     saves = [pltpu.make_async_copy(a, b, save.at[k]) for k, (a, b) in enumerate(zip(sources, targets))]
     for m in range(count):
         first = m < trunk_total
         place = m if first else m - trunk_total
-        gram = (grams if first else head_grams)[place * channels : (place + 1) * channels, :]
-        old = (stat if first else head_stat)[place]
-        stats[m] = STAT_DECAY * old + (1.0 - STAT_DECAY) * gram.astype(F32)
-        product[m] = dot3(dot, stats[m], (basis if first else head_basis)[place])
+        for copy in loads[3 * m : 3 * m + 3]:
+            copy.wait()
+        low = low_grams if first else low_head_grams
+        gram = low[place * channels : (place + 1) * channels, :].astype(F32)
+        stats[m] = STAT_DECAY * stats[m] + (1.0 - STAT_DECAY) * gram
+        product[m] = dot3(dot, stats[m], made[m])
     groups = ((0, trunk_total, stat_new, basis_new), (trunk_total, head_total, head_stat_new, head_basis_new))
     for begin, size, out, _ in groups:
         copy = pltpu.make_async_copy(stats.at[pl.ds(begin, size)], out, save.at[len(saves)])
         copy.start()
         saves.append(copy)
-    for copy in loads:
+    for copy in loads[3 * count :]:
         copy.wait()
     for copy in saves[:6]:
         copy.start()
@@ -1572,10 +1603,11 @@
     kind = BF if gram_rows % (16 * batches) == 0 else F32
     head_kind = BF if head_rows % (16 * batches) == 0 else F32
     cuts = 4 if total % 64 == 0 and head_grad.shape[0] % 64 == 0 else 1
+    pieces = 2 if total % 64 == 0 else 1
     square = (trunk_total + head_total, channels, channels)
     pixels = flow.shape[0] // tasks
     input_grad, norm_sums, *made = exchange_kernel(
-        functools.partial(tail_body, tasks, batches, cuts),
+        functools.partial(tail_body, tasks, batches, cuts, pieces),
         [
             shape((pixels, channels), F32),
             shape((8, channels), F32),
@@ -1597,8 +1629,10 @@
             pltpu.VMEM(square, BF),
             pltpu.VMEM((tasks - 1, pixels, channels), BF),
         ]
-        + [pltpu.SemaphoreType.DMA((tasks,))] * 6
-        + pair_scratch(batches, slots.shape[0], width, BF)
+        + [pltpu.SemaphoreType.DMA((tasks,))] * 2
+        + [pltpu.SemaphoreType.DMA((pieces, tasks))] * 2
+        + [pltpu.SemaphoreType.DMA((tasks,))] * 2
+        + pair_scratch(batches, slots.shape[0] // pieces, width, BF) * pieces
         + pair_scratch(batches, gram_rows, width, kind)
         + pair_scratch(batches, head_rows, channels, head_kind)
         + [pltpu.SemaphoreType.DMA((2, max(chips, 4)))] * 2
@@ -1616,11 +1650,12 @@
     results = pl.pallas_call(
         renew_body,
         out_shape=tuple(outs),
-        in_specs=[hbm] * 2 + [VMEM_SPEC] * 6,
+        in_specs=[hbm] * 8,
         out_specs=tuple(hbm for _ in outs),
         scratch_shapes=[pltpu.VMEM(square, F32)] * 3
+        + [pltpu.VMEM(made[2].shape, kind), pltpu.VMEM(made[3].shape, head_kind)]
         + [pltpu.VMEM(made[0].shape, F32), pltpu.VMEM(made[1].shape, F32)]
-        + [pltpu.SemaphoreType.DMA((2,))]
+        + [pltpu.SemaphoreType.DMA((3 * count + 2,))]
         + [pltpu.SemaphoreType.DMA((8 + 2 * (channels // PANEL),))]
         + [pltpu.VMEM((PANEL, 2 * PANEL), F32)] * count
         + [pltpu.VMEM((PANEL, PANEL), F32)] * count,

time: 395 us -> 392 us (level)
  transfers between devices with their start and end apart: 2 -> 2, of which waited for: 2 -> 2; matrix products, arithmetic and copies ran while one was open for 1% -> 1% of each run, Pallas kernels for 25% -> 26%
where the time goes in v1:
time: 392 us; the launch traced here: 389 us
  Pallas kernels  349 us (89%)
  between operations  15.2 us (4%)
  waiting for transfers between devices  13.2 us (3%)
  local copies, waits for them, and re-layouts  9.6 us (2%)
    pallas_call x5, Pallas kernels, exchange_kernel(): pl.pallas_call(body, out_shape=tuple(outs), in_specs=[SPECS[s] for s in s...  274 us
    pallas_call x1, Pallas kernels, finish(): pl.pallas_call(renew_body, out_shape=tuple(outs), in_specs=[hbm] * 8, out...  62.6 us
    pallas_call x1, Pallas kernels, run(): pl.pallas_call(body, out_shape=tuple(outs), in_specs=[SMEM_SPEC if s == '...  13 us
    reduce_scatter x1, waiting for transfers between devices, head(): lax.psum_scatter(grads.reshape(chips * block, channels), 'batch', scatter...  9.03 us
  transfers between devices with their start and end apart: 2, of which 2 were waited for; matrix products, arithmetic and copies ran while one was open for 1% of the time, Pallas kernels for 26%

profile of v1, /device:TPU:0, one launch (start us, length us, event | category | flops | bytes accessed | tf_op | source)
XLA Modules:
  0.0 388.6 jit_solution(7154078162609111448)
XLA Ops:
  7.2 0.0 all-gather.2.cloned.1.call-start
  7.2 0.1 iota_add_fusion
  7.3 0.7 copy.62
  8.0 0.1 broadcast_compare_fusion
  8.1 0.1 eq.36
  8.9 0.1 and.51
  9.0 0.1 and.52
  9.1 0.1 and.54
  9.3 0.1 scatter.14.info
  9.3 0.0 copy-start.8
  9.4 0.6 copy-done.8
  10.0 0.0 copy-start.5
  10.0 0.0 copy-start.6
  10.0 0.0 copy-start.2
  10.0 0.0 copy-start.3
  10.0 0.0 copy-start.4
  10.0 31.2 %shard_map.358 = (bf16[9216,128]{1,0:T(8,128)(2,1)}, bf16[1728,512]{1,0:T(8,128)(2,1)}, f32[32,512]{1,0:T(8,128)}, f32[1152,2]{1,0:T(8,128)}, bf16[704,512]{1,0:T(8,128)(2,1)}) custom-call(bf16[432,512]{1,0:T(8,128)(2,1)} %bitcast.56, f32[8,512]{1,0:T(8,128)} %copy-done.8, s32[72,128]{1,0:T(8,128)} %bitcast.36, f32[1152,512]{1,0:T(8,128)} %weight.3, ...), custom_call_target="tpu_custom_call" | custom-call | flops 20971520000 | bytes 9221120 | tf_op jit(solution)/shard_map/pallas_call | solution.py:232
  41.2 0.0 all-gather.2.cloned.1.call-update
  41.2 0.2 reduce-scatter.2.cloned.1.call-start
  41.5 0.0 copy-done.5
  41.5 0.0 copy-done.6
  41.5 0.6 copy.43
  42.1 0.0 copy-done.2
  42.1 0.8 copy.44.cotangent
  42.9 0.0 copy-done.3
  42.9 0.0 copy-done.4
  42.9 0.6 reshape.259.scales
  43.6 55.3 %shard_map.359 = (f32[8,128]{1,0:T(8,128)}, f32[8,128]{1,0:T(8,128)}, bf16[1728,512]{1,0:T(8,128)(2,1)}, bf16[1728,512]{1,0:T(8,128)(2,1)}, bf16[512,1152]{1,0:T...) custom-call(s32[9216]{0:T(1024)} %index.3, ...), custom_call_target="tpu_custom_call" | custom-call | flops 4076863488 | bytes 13678592 | tf_op jit(solution)/shard_map/pallas_call | solution.py:232
  98.9 4.1 %all-gather.2.cloned.1.call-done.weights = bf16[5632,512]{1,0:T(8,128)(2,1)} async-done(((bf16[704,512]{1,0:T(8,128)(2,1)}), bf16[5632,512]{1,0:T(8,128)(2,1)}) %all-gather.2.cloned.1.call-update) | async-done | bytes 5767184 | tf_op jit(solution)/shard_map/all_gather | solution.py:1725
  103.0 85.3 %shard_map.360 = (bf16[4,108,512]{2,1,0:T(8,128)(2,1)}, f32[1728,128]{1,0:T(8,128)}, f32[8,512]{1,0:T(8,128)}, bf16[4,704,512]{2,1,0:T(8,128)(2,1)}) custom-call(f32[32,512]{1,0:T(8,128)} %get-tuple-element.80.infos, bf16[1728,512]{1,0:T(8,128)(2,1)} %get-tuple-element.83.features, bf16[5632,512]{1,0:T(8,128)(2,1)} %all-gather.2.cloned.1.call-done.weights, ...), custom_call_target="tpu_custom_call" | custom-call | flops 29896998912 | bytes 12288000 | tf_op jit(solution)/shard_map/pallas_call | solution.py:232
  188.3 0.0 copy-start.1
  188.3 0.0 copy-start.7
  188.3 0.0 reduce-scatter.2.cloned.1.call-update
  188.3 1.0 copy-done.1
  189.3 1.1 copy.45
  190.4 0.0 copy-done.7
  190.4 0.2 rev.7
  190.6 31.5 %shard_map.361 = (f32[512,1152]{1,0:T(8,128)}, f32[512,1152]{1,0:T(8,128)}, bf16[1728,512]{1,0:T(8,128)(2,1)}, f32[8,128]{1,0:T(8,128)}) custom-call(f32[32,512]{1,0:T(8,128)} %get-tuple-element.80.infos, f32[1728,128]{1,0:T(8,128)} %get-tuple-element.87.upstream, f32[8,128]{1,0:T(8,128)} %get-tuple-element.85.counts.enc_totals, ...), custom_call_target="tpu_custom_call" | custom-call | flops 8153726976 | bytes 15120384 | tf_op jit(solution)/shard_map/pallas_call | solution.py:232
  222.1 0.0 copy-start.9
  222.1 0.0 copy-start.10
  222.1 13.0 %shard_map.362.slots = bf16[9216,128]{1,0:T(8,128)(2,1)} custom-call(s32[9216]{0:T(1024)} %index.3, f32[512,1152]{1,0:T(8,128)} %get-tuple-element.95.enc, f32[512,1152]{1,0:T(8,128)} %get-tuple-element.96.dec), custom_call_target="tpu_custom_call" | custom-call | bytes 7114752 | tf_op jit(solution)/shard_map/pallas_call | solution.py:32
  235.1 0.0 copy-done.9
  235.1 0.0 copy-done.10
  235.1 0.7 maximum_subtract_fusion
  235.8 9.0 %reduce-scatter.2.cloned.1.call-done.head_grad = bf16[704,512]{1,0:T(8,128)(2,1)} async-done(((bf16[2816,512]{1,0:T(8,128)(2,1)}), bf16[704,512]{1,0:T(8,128)(2,1)}) %reduce-scatter.2.cloned.1.call-update) | async-done | bytes 720912 | tf_op jit(solution)/shard_map/reduce_scatter | solution.py:739
  244.8 0.0 copy-start.11
  244.8 0.0 copy-start.12
  244.8 70.5 %shard_map.363 = (f32[432,512]{1,0:T(8,128)}, f32[8,512]{1,0:T(8,128)}, f32[3,1152,512]{2,1,0:T(8,128)}, f32[3,704,512]{2,1,0:T(8,128)}, bf16[1024,512]{1,0:T(8,128)(2,1)}, /*index=5*/bf16[1536,512]{1,0:T(8,128)(2,1)}) custom-call(bf16[9216,128]{1,0:T(8,128)(2,1)} %shard_map.362.slots, bf16[1728,512]{1,0:T(8,128)(2,1)} %get-tuple-element.97.flow, ...), custom_call_target="tpu_custom_call" | custom-call | flops 52428800000 | bytes 36434944 | tf_op jit(solution)/shard_map/pallas_call | solution.py:232
  315.4 0.7 slice.41
  316.1 0.0 copy-done.11
  316.1 0.0 copy-done.12
  316.2 0.6 copy.49
  316.8 0.6 copy.50
  317.4 0.6 copy.51
  318.0 0.0 copy-start
  318.0 62.6 %shard_map.364 = (f32[1152,512]{1,0:T(8,128)}, f32[1152,512]{1,0:T(8,128)}, f32[1152,512]{1,0:T(8,128)}, f32[704,512]{1,0:T(8,128)}, f32[704,512]{1,0:T(8,128)},...) custom-call(f32[3,1152,512]{2,1,0:T(8,128)} %get-tuple-element.102.s, ...), custom_call_target="tpu_custom_call" | custom-call | flops 62914560000 | bytes 67108864 | tf_op jit(solution)/shard_map/pallas_call | solution.py:1650
  380.6 0.0 copy-done
  380.6 0.9 copy.66
  (12 shorter events, 0.1 us)
Async XLA Ops:
  7.2 95.8 %all-gather.2.cloned.1.call-start = ((), (), s32[]{:S(2)}) async-start(), calls=%async_computation.1 | async-start | bytes 6488064 | tf_op jit(solution)/shard_map/all_gather | solution.py:1725
  9.3 0.6 copy-start.8
  10.0 31.5 %copy-start.5 = (f32[2,512]{1,0:T(2,128)S(1)}, f32[2,512]{1,0:T(2,128)}, u32[]{:S(2)}) copy-start(f32[2,512]{1,0:T(2,128)} %param.41) | copy-start | bytes 12292
  10.0 31.5 %copy-start.6 = (f32[2,512]{1,0:T(2,128)S(1)}, f32[2,512]{1,0:T(2,128)}, u32[]{:S(2)}) copy-start(f32[2,512]{1,0:T(2,128)} %param.42) | copy-start | bytes 12292
  10.0 32.1 %copy-start.2 = (bf16[1,4,1,9,12,512]{5,1,4,3,2,0:T(4,128)(2,1)S(1)}, bf16[1,4,1,9,12,512]{5,1,4,3,2,0:T(4,128)(2,1)}, u32[]{:S(2)}) copy-start(bf16[1,4,1,9,12,512]{5,1,4,3,2,0:T(4,128)(2,1)} %param.49) | copy-start | bytes 1327108
  10.0 33.0 %copy-start.3 = (f32[1,3,512]{2,0,1:T(1,128)S(1)}, f32[1,3,512]{2,0,1:T(1,128)}, u32[]{:S(2)}) copy-start(f32[1,3,512]{2,0,1:T(1,128)} %param.46) | copy-start | bytes 18436
  10.0 33.0 %copy-start.4 = (f32[1,3,512]{2,0,1:T(1,128)S(1)}, f32[1,3,512]{2,0,1:T(1,128)}, u32[]{:S(2)}) copy-start(f32[1,3,512]{2,0,1:T(1,128)} %param.45) | copy-start | bytes 18436
  41.2 203.6 %reduce-scatter.2.cloned.1.call-start = ((), (), s32[]{:S(2)}) async-start(), calls=%async_computation.2 | async-start | bytes 3604480 | tf_op jit(solution)/shard_map/reduce_scatter | solution.py:739
  188.3 1.0 copy-start.1
  188.3 2.1 copy-start.7
  222.1 13.1 %copy-start.9 = (f32[1,3,2,512]{3,2,1,0:T(2,128)S(1)}, f32[1,3,2,512]{3,2,1,0:T(2,128)}, u32[]{:S(2)}) copy-start(f32[1,3,2,512]{3,2,1,0:T(2,128)} %param.47) | copy-start | bytes 36868
  222.1 13.0 %copy-start.10 = (f32[1,3,2,512]{3,2,1,0:T(2,128)S(1)}, f32[1,3,2,512]{3,2,1,0:T(2,128)}, u32[]{:S(2)}) copy-start(f32[1,3,2,512]{3,2,1,0:T(2,128)} %param.48) | copy-start | bytes 36868
  244.8 71.3 %copy-start.11 = (f32[2,2,512]{2,1,0:T(2,128)S(1)}, f32[2,2,512]{2,1,0:T(2,128)}, u32[]{:S(2)}) copy-start(f32[2,2,512]{2,1,0:T(2,128)} %param.43) | copy-start | bytes 24580
  244.8 71.3 %copy-start.12 = (f32[2,2,512]{2,1,0:T(2,128)S(1)}, f32[2,2,512]{2,1,0:T(2,128)}, u32[]{:S(2)}) copy-start(f32[2,2,512]{2,1,0:T(2,128)} %param.44) | copy-start | bytes 24580
  318.0 62.6 %copy-start = (f32[432,512]{1,0:T(8,128)S(1)}, f32[432,512]{1,0:T(8,128)}, u32[]{:S(2)}) copy-start(f32[432,512]{1,0:T(8,128)} %get-tuple-element.101) | copy-start | bytes 2654212
Sparse Core Ops, SparseCore 0:
  41.3 61.6 all-gather.1
  188.5 56.3 reduce-scatter.1

commit v2 on v1

--- a/solution.py
+++ b/solution.py
@@ -1288,6 +1288,10 @@
 PANEL = 128
 
 
+def upper_blocks(size):
+    return [(a, b) for a in range(0, size, PANEL) for b in range(a, size, PANEL)]
+
+
 def renew_panel(k, product, made, tables, inverses):
     count, size = product.shape[0], product.shape[1]
     here = slice(k * PANEL, (k + 1) * PANEL)
@@ -1361,6 +1365,17 @@
                 target.dtype
             )
 
+    def put_packed_grams(target, rows, marks):
+        n = 0
+        for mark in marks:
+            held = (rows[...].astype(F32) * mark).astype(BF)
+            for a, b in upper_blocks(channels):
+                block = dot_tn(held[:, a : a + PANEL], rows[:, b : b + PANEL])
+                target[n : n + PANEL, :] = block.astype(target.dtype)
+                n += PANEL
+        if n < target.shape[0]:
+            target[n:, :] = jnp.zeros((target.shape[0] - n, PANEL), target.dtype)
+
     def peer_of(step, incoming):
         return lax.rem(task + (tasks - step if incoming else step), tasks)
 
@@ -1439,7 +1454,7 @@
         flow_copy(step).start()
     norm_sums[:, columns_of(task, width)] = sums[...]
     row_sums[0][1]()
-    put_grams(head_mine, head_grad, head_grad, head_marks(0, head_grad.shape[0]))
+    put_packed_grams(head_mine, head_grad, head_marks(0, head_grad.shape[0]))
     head_start, head_middle, head_relay, head_end = sum_of(head_mine, head_scratch)
     row_sums[0][2]()
     for stages in row_sums[1:]:
@@ -1532,64 +1547,98 @@
 
 
 def renew_body(
-    state, head_state, grams, head_grams, stat, head_stat, basis, head_basis,
+    core, state, head_state, grams, head_grams, stat, head_stat, basis, head_basis,
     weight_new, one_new, two_new, head_weight_new, head_one_new, head_two_new,
-    stat_new, head_stat_new, basis_new, head_basis_new,
+    stat_new, head_stat_new, low_made,
     stats, product, made, low_grams, low_head_grams, held, head_held, load, save, *work,
 ):
     trunk_total, head_total = stat.shape[0], head_stat.shape[0]
     channels = stat.shape[1]
     count = trunk_total + head_total
-    tables, inverses = work[:count], work[count:]
+    shared = product.shape[0]
+    tables, inverses = work[:shared], work[shared:]
     loads = []
+    blocks = upper_blocks(channels)
+    packed = len(blocks) * PANEL
+
+    def gram_rows(m, start):
+        if m < trunk_total:
+            first = m * channels + start
+            return low_grams[first : first + PANEL, :].astype(F32)
+        parts = []
+        for b in range(0, channels, PANEL):
+            n = blocks.index((min(start, b), max(start, b)))
+            first = (m - trunk_total) * packed + n * PANEL
+            block = low_head_grams[first : first + PANEL, :].astype(F32)
+            parts.append(block if b >= start else block.T)
+        return jnp.concatenate(parts, axis=1)
 
     def bring(source, target):
         copy = pltpu.make_async_copy(source, target, load.at[len(loads)])
-        copy.start()
         loads.append(copy)
+        return copy
 
     for m in range(count):
         first = m < trunk_total
         place = m if first else m - trunk_total
-        rows = pl.ds(place * channels, channels)
+        size = channels if first else packed
+        rows = pl.ds(place * size, size)
         here, there = (grams, low_grams) if first else (head_grams, low_head_grams)
-        bring(here.at[rows, :], there.at[rows, :])
-        bring((stat if first else head_stat).at[place], stats.at[m])
-        bring((basis if first else head_basis).at[place], made.at[m])
-    bring(state, held)
-    bring(head_state, head_held)
+        bring(here.at[rows, :], there.at[rows, :]).start()
+        bring((stat if first else head_stat).at[place], stats.at[m]).start()
+
+    for n in range(shared):
+        both = [
+            basis.at[n] if n < trunk_total else head_basis.at[n - trunk_total],
+            head_basis.at[n],
+        ]
+        copy = bring(both[1], made.at[n])
+        for which, source in enumerate(both):
+
+            @pl.when(core[0] == which)
+            def _():
+                pltpu.make_async_copy(source, made.at[n], load.at[2 * count + n]).start()
+
+    bring(state, held).start()
+    bring(head_state, head_held).start()
     sources = [held.at[k] for k in range(3)] + [head_held.at[k] for k in range(3)]
     targets = [weight_new, one_new, two_new, head_weight_new, head_one_new, head_two_new]
     saves = [pltpu.make_async_copy(a, b, save.at[k]) for k, (a, b) in enumerate(zip(sources, targets))]
     for m in range(count):
-        first = m < trunk_total
-        place = m if first else m - trunk_total
-        for copy in loads[3 * m : 3 * m + 3]:
+        for copy in loads[2 * m : 2 * m + 2]:
             copy.wait()
-        low = low_grams if first else low_head_grams
-        gram = low[place * channels : (place + 1) * channels, :].astype(F32)
-        stats[m] = STAT_DECAY * stats[m] + (1.0 - STAT_DECAY) * gram
-        product[m] = dot3(dot, stats[m], made[m])
-    groups = ((0, trunk_total, stat_new, basis_new), (trunk_total, head_total, head_stat_new, head_basis_new))
-    for begin, size, out, _ in groups:
+        for start in range(0, channels, PANEL):
+            rows = slice(start, start + PANEL)
+            stats[m, rows, :] = STAT_DECAY * stats[m, rows, :] + (1.0 - STAT_DECAY) * gram_rows(m, start)
+    for begin, size, out in ((0, trunk_total, stat_new), (trunk_total, head_total, head_stat_new)):
         copy = pltpu.make_async_copy(stats.at[pl.ds(begin, size)], out, save.at[len(saves)])
         copy.start()
         saves.append(copy)
-    for copy in loads[3 * count :]:
-        copy.wait()
-    for copy in saves[:6]:
-        copy.start()
+    for n in range(shared):
+        loads[2 * count + n].wait()
+        product[n] = dot3(dot, stats[trunk_total * core[0] + n], made[n])
     for k in range(channels // PANEL):
         renew_panel(k, product, made, tables, inverses)
-        cut = pl.ds(k * PANEL, PANEL)
-        for begin, size, _, out in groups:
-            copy = pltpu.make_async_copy(
-                made.at[pl.ds(begin, size), :, cut], out.at[:, :, cut], save.at[len(saves)]
-            )
-            copy.start()
-            saves.append(copy)
+        if k == 0:
+            for copy in loads[2 * count + shared :]:
+                copy.wait()
+            for copy in saves[:6]:
+                copy.start()
+        cut = slice(k * PANEL, (k + 1) * PANEL)
+        low_made[:, :, cut] = made[:, :, cut].astype(BF)
     for copy in saves:
         copy.wait()
+
+
+def swap_body(batches, x, out, sends, receives):
+    place, core, _ = pair_place(batches)
+    other = 2 * place + 1 - core
+    barrier = pltpu.get_barrier_semaphore()
+    pl.semaphore_signal(barrier, inc=1, device_id={"batch": other}, device_id_type=MESH)
+    pl.semaphore_wait(barrier, 1)
+    copy = remote(x, out, sends, receives, other, "batch")
+    copy.start()
+    copy.wait()
 
 
 def finish(tasks, batches, local_grads, rows, matrices):
@@ -1598,10 +1647,11 @@
     total, channels = rows[0].shape
     width = channels // tasks
     trunk_total, head_total = basis.shape[0], head_basis.shape[0]
-    gram_rows, head_rows = trunk_total * channels, head_total * channels
+    gram_rows = trunk_total * channels
+    packed = len(upper_blocks(channels)) * PANEL
+    head_rows = -(-head_total * packed // (16 * batches)) * 16 * batches
     chips = batches // 2
     kind = BF if gram_rows % (16 * batches) == 0 else F32
-    head_kind = BF if head_rows % (16 * batches) == 0 else F32
     cuts = 4 if total % 64 == 0 and head_grad.shape[0] % 64 == 0 else 1
     pieces = 2 if total % 64 == 0 else 1
     square = (trunk_total + head_total, channels, channels)
@@ -1614,7 +1664,7 @@
             shape((3, total, channels), F32),
             shape((3,) + head_grad.shape, F32),
             shape((gram_rows, channels), kind),
-            shape((head_rows, channels), head_kind),
+            shape((head_rows, PANEL), BF),
         ],
         "vvvvvhhhhhhhh",
         (*local_grads, *rows, basis, head_basis),
@@ -1624,7 +1674,7 @@
             pltpu.VMEM((3, total, channels), F32),
             pltpu.VMEM((3,) + head_grad.shape, F32),
             pltpu.VMEM((gram_rows, width), kind),
-            pltpu.VMEM((head_rows, channels), head_kind),
+            pltpu.VMEM((head_rows, PANEL), BF),
             pltpu.VMEM(square, F32),
             pltpu.VMEM(square, BF),
             pltpu.VMEM((tasks - 1, pixels, channels), BF),
@@ -1634,7 +1684,7 @@
         + [pltpu.SemaphoreType.DMA((tasks,))] * 2
         + pair_scratch(batches, slots.shape[0] // pieces, width, BF) * pieces
         + pair_scratch(batches, gram_rows, width, kind)
-        + pair_scratch(batches, head_rows, channels, head_kind)
+        + pair_scratch(batches, head_rows, PANEL, BF)
         + [pltpu.SemaphoreType.DMA((2, max(chips, 4)))] * 2
         + [pltpu.SemaphoreType.DMA((tasks, chips))] * 2
         + [pltpu.SemaphoreType.DMA((tasks + 1, chips))] * 2
@@ -1647,23 +1697,41 @@
     outs = [shape(a.shape, F32) for a in (*rows, *matrices)]
     hbm = pl.BlockSpec(memory_space=pltpu.HBM)
     count = trunk_total + head_total
-    results = pl.pallas_call(
+    shared = max(trunk_total, head_total)
+    core = lax.rem(lax.axis_index("batch"), 2)
+    own = (shared, channels, channels)
+    *results, made_low = pl.pallas_call(
         renew_body,
-        out_shape=tuple(outs),
-        in_specs=[hbm] * 8,
-        out_specs=tuple(hbm for _ in outs),
-        scratch_shapes=[pltpu.VMEM(square, F32)] * 3
-        + [pltpu.VMEM(made[2].shape, kind), pltpu.VMEM(made[3].shape, head_kind)]
+        out_shape=(*outs[:8], shape(own, BF)),
+        in_specs=[SMEM_SPEC] + [hbm] * 8,
+        out_specs=(*(hbm for _ in outs[:8]), VMEM_SPEC),
+        scratch_shapes=[pltpu.VMEM(square, F32)]
+        + [pltpu.VMEM(own, F32)] * 2
+        + [pltpu.VMEM(made[2].shape, kind), pltpu.VMEM(made[3].shape, BF)]
         + [pltpu.VMEM(made[0].shape, F32), pltpu.VMEM(made[1].shape, F32)]
-        + [pltpu.SemaphoreType.DMA((3 * count + 2,))]
-        + [pltpu.SemaphoreType.DMA((8 + 2 * (channels // PANEL),))]
-        + [pltpu.VMEM((PANEL, 2 * PANEL), F32)] * count
-        + [pltpu.VMEM((PANEL, PANEL), F32)] * count,
+        + [pltpu.SemaphoreType.DMA((2 * count + shared + 2,))]
+        + [pltpu.SemaphoreType.DMA((8,))]
+        + [pltpu.VMEM((PANEL, 2 * PANEL), F32)] * shared
+        + [pltpu.VMEM((PANEL, PANEL), F32)] * shared,
         compiler_params=pltpu.CompilerParams(vmem_limit_bytes=60 * MIB),
         cost_estimate=pl.CostEstimate(
-            flops=60000 * MIB, bytes_accessed=64 * MIB, transcendentals=0
+            flops=50000 * MIB, bytes_accessed=64 * MIB, transcendentals=0
         ),
-    )(*made, *matrices)
+    )(core.reshape(1), *made, *matrices)
+    theirs = exchange_kernel(
+        functools.partial(swap_body, batches),
+        [shape(own, BF)],
+        "v",
+        (made_low,),
+        [pltpu.SemaphoreType.DMA] * 2,
+        6,
+        60,
+        flops=5000 * MIB,
+    )[0]
+    results += [
+        jnp.where(core == which, made_low[:total], theirs[:total]).astype(F32)
+        for which, total in enumerate((trunk_total, head_total))
+    ]
     return input_grad, norm_sums, results
 
 

time: 392 us -> 373 us (0.952)
  Pallas kernels: 349 us -> 327 us
  other arithmetic: 0.92 us -> 5.6 us
    pallas_call x1, Pallas kernels: 62.6 us -> 42.9 us  [finish(): pl.pallas_call(renew_body, out_shape=(*outs[:8], shape(own, BF)), in_spec...]
    pallas_call x5 -> x6, Pallas kernels: 274 us -> 271 us  [exchange_kernel(): pl.pallas_call(body, out_shape=tuple(outs), in_specs=[SPECS[s] for s in s...]
  transfers between devices with their start and end apart: 2 -> 2, of which waited for: 2 -> 2; matrix products, arithmetic and copies ran while one was open for 1% -> 1% of each run, Pallas kernels for 26% -> 27%
where the time goes in v2:
time: 373 us; the launch traced here: 370 us
  Pallas kernels  327 us (88%)
  between operations  15.3 us (4%)
  waiting for transfers between devices  12.5 us (3%)
  local copies, waits for them, and re-layouts  8.9 us (2%)
  other arithmetic  5.6 us (2%)
    pallas_call x6, Pallas kernels, exchange_kernel(): pl.pallas_call(body, out_shape=tuple(outs), in_specs=[SPECS[s] for s in s...  271 us
    pallas_call x1, Pallas kernels, finish(): pl.pallas_call(renew_body, out_shape=(*outs[:8], shape(own, BF)), in_spec...  42.9 us
    pallas_call x1, Pallas kernels, run(): pl.pallas_call(body, out_shape=tuple(outs), in_specs=[SMEM_SPEC if s == '...  13.1 us
    reduce_scatter x1, waiting for transfers between devices, head(): lax.psum_scatter(grads.reshape(chips * block, channels), 'batch', scatter...  8.96 us
  transfers between devices with their start and end apart: 2, of which 2 were waited for; matrix products, arithmetic and copies ran while one was open for 1% of the time, Pallas kernels for 27%

profile of v2, /device:TPU:0, one launch (start us, length us, event | category | flops | bytes accessed | tf_op | source)
XLA Modules:
  0.0 369.9 jit_solution(88803849335787959)
XLA Ops:
  7.2 0.0 all-gather.2.cloned.1.call-start
  7.2 0.1 iota_add_fusion
  7.3 0.7 copy.62
  8.0 0.1 broadcast_compare_fusion
  8.1 0.1 eq.42
  8.9 0.1 and.53
  9.0 0.1 and.54
  9.1 0.1 and.56
  9.3 0.1 scatter.14.info
  9.3 0.0 copy-start.12
  9.4 0.6 copy-done.12
  10.0 0.0 copy-start.7
  10.0 0.0 copy-start.6
  10.0 31.2 %shard_map.358 = (bf16[9216,128]{1,0:T(8,128)(2,1)}, bf16[1728,512]{1,0:T(8,128)(2,1)}, f32[32,512]{1,0:T(8,128)}, f32[1152,2]{1,0:T(8,128)}, bf16[704,512]{1,0:T(8,128)(2,1)}) custom-call(bf16[432,512]{1,0:T(8,128)(2,1)} %bitcast.59, f32[8,512]{1,0:T(8,128)} %copy-done.12, s32[72,128]{1,0:T(8,128)} %bitcast.39, f32[1152,512]{1,0:T(8,128)} %weight.3, ...), custom_call_target="tpu_custom_call" | custom-call | flops 20971520000 | bytes 9221120 | tf_op jit(solution)/shard_map/pallas_call | solution.py:232
  41.2 0.0 all-gather.2.cloned.1.call-update
  41.2 0.3 reduce-scatter.2.cloned.1.call-start
  41.5 0.0 copy-done.7
  41.5 0.0 copy-done.9
  41.5 0.6 copy.43
  42.1 0.0 copy-done.4
  42.1 0.8 copy.44.cotangent
  42.9 0.0 copy-done.5
  42.9 0.0 copy-done.6
  43.0 0.6 reshape.262.scales
  43.6 55.9 %shard_map.359 = (f32[8,128]{1,0:T(8,128)}, f32[8,128]{1,0:T(8,128)}, bf16[1728,512]{1,0:T(8,128)(2,1)}, bf16[1728,512]{1,0:T(8,128)(2,1)}, bf16[512,1152]{1,0:T...) custom-call(s32[9216]{0:T(1024)} %index.3, ...), custom_call_target="tpu_custom_call" | custom-call | flops 4076863488 | bytes 13678592 | tf_op jit(solution)/shard_map/pallas_call | solution.py:232
  99.5 3.5 all-gather.2.cloned.1.call-done.weights
  103.0 85.3 %shard_map.360 = (bf16[4,108,512]{2,1,0:T(8,128)(2,1)}, f32[1728,128]{1,0:T(8,128)}, f32[8,512]{1,0:T(8,128)}, bf16[4,704,512]{2,1,0:T(8,128)(2,1)}) custom-call(f32[32,512]{1,0:T(8,128)} %get-tuple-element.79.infos, bf16[1728,512]{1,0:T(8,128)(2,1)} %get-tuple-element.82.features, bf16[5632,512]{1,0:T(8,128)(2,1)} %all-gather.2.cloned.1.call-done.weights, ...), custom_call_target="tpu_custom_call" | custom-call | flops 29896998912 | bytes 12288000 | tf_op jit(solution)/shard_map/pallas_call | solution.py:232
  188.3 0.0 copy-start.3
  188.3 0.0 copy-start.11
  188.3 0.0 reduce-scatter.2.cloned.1.call-update
  188.4 1.0 copy-done.3
  189.3 1.1 copy.45
  190.4 0.0 copy-done.11
  190.5 0.2 rev.7
  190.6 31.5 %shard_map.361 = (f32[512,1152]{1,0:T(8,128)}, f32[512,1152]{1,0:T(8,128)}, bf16[1728,512]{1,0:T(8,128)(2,1)}, f32[8,128]{1,0:T(8,128)}) custom-call(f32[32,512]{1,0:T(8,128)} %get-tuple-element.79.infos, f32[1728,128]{1,0:T(8,128)} %get-tuple-element.86.upstream, f32[8,128]{1,0:T(8,128)} %get-tuple-element.84.counts.enc_totals, ...), custom_call_target="tpu_custom_call" | custom-call | flops 8153726976 | bytes 15120384 | tf_op jit(solution)/shard_map/pallas_call | solution.py:232
  222.1 0.0 copy-start.13
  222.1 0.0 copy-start.14
  222.1 13.1 %shard_map.362.slots = bf16[9216,128]{1,0:T(8,128)(2,1)} custom-call(s32[9216]{0:T(1024)} %index.3, f32[512,1152]{1,0:T(8,128)} %get-tuple-element.94.enc, f32[512,1152]{1,0:T(8,128)} %get-tuple-element.95.dec), custom_call_target="tpu_custom_call" | custom-call | bytes 7114752 | tf_op jit(solution)/shard_map/pallas_call | solution.py:32
  235.2 0.0 copy-done.13
  235.2 0.0 copy-done.14
  235.2 0.7 maximum_subtract_fusion
  235.9 9.0 %reduce-scatter.2.cloned.1.call-done.head_grad = bf16[704,512]{1,0:T(8,128)(2,1)} async-done(((bf16[2816,512]{1,0:T(8,128)(2,1)}), bf16[704,512]{1,0:T(8,128)(2,1)}) %reduce-scatter.2.cloned.1.call-update) | async-done | bytes 720912 | tf_op jit(solution)/shard_map/reduce_scatter | solution.py:739
  244.8 61.3 %shard_map.363 = (f32[432,512]{1,0:T(8,128)}, f32[8,512]{1,0:T(8,128)}, f32[3,1152,512]{2,1,0:T(8,128)}, f32[3,704,512]{2,1,0:T(8,128)}, bf16[1024,512]{1,0:T(8,128)(2,1)}, /*index=5*/bf16[3840,128]{1,0:T(8,128)(2,1)}) custom-call(bf16[9216,128]{1,0:T(8,128)(2,1)} %shard_map.362.slots, bf16[1728,512]{1,0:T(8,128)(2,1)} %get-tuple-element.96.flow, ...), custom_call_target="tpu_custom_call" | custom-call | flops 52428800000 | bytes 35845120 | tf_op jit(solution)/shard_map/pallas_call | solution.py:232
  306.2 42.9 %shard_map.364 = (f32[1152,512]{1,0:T(8,128)}, f32[1152,512]{1,0:T(8,128)}, f32[1152,512]{1,0:T(8,128)}, f32[704,512]{1,0:T(8,128)}, f32[704,512]{1,0:T(8,128)},...) custom-call(s32[1]{0:T(128)} %bitcast.18.core, ...), custom_call_target="tpu_custom_call" | custom-call | flops 52428800000 | bytes 67108864 | tf_op jit(solution)/shard_map/pallas_call | solution.py:1703
  349.0 0.0 copy-start
  349.1 6.2 %shard_map.365 = bf16[3,512,512]{2,1,0:T(8,128)(2,1)} custom-call(bf16[3,512,512]{2,1,0:T(8,128)(2,1)} %get-tuple-element.109.x), custom_call_target="tpu_custom_call" | custom-call | flops 5242880000 | bytes 3145728 | tf_op jit(solution)/shard_map/pallas_call | solution.py:232
  355.3 0.0 copy-done
  355.3 0.0 copy-start.1
  355.3 2.8 select_convert_fusion
  358.1 0.0 copy-done.1
  358.1 0.0 copy-start.15
  358.1 0.0 copy-start.16
  358.1 0.0 copy-start.2
  358.1 1.9 bitcast_convert_fusion
  360.0 0.0 copy-done.17
  360.1 0.0 copy-done.8
  360.1 0.0 copy-done.10
  360.1 0.0 copy-done.15
  360.1 0.0 copy-done.16
  360.1 0.6 copy.49
  360.7 0.6 copy.50
  361.3 0.6 copy.51
  362.0 0.0 copy-done.2
  362.0 0.9 copy.66
  (19 shorter events, 0.2 us)
Async XLA Ops:
  7.2 95.8 %all-gather.2.cloned.1.call-start = ((), (), s32[]{:S(2)}) async-start(), calls=%async_computation.1 | async-start | bytes 6488064 | tf_op jit(solution)/shard_map/all_gather | solution.py:1793
  9.3 0.6 copy-start.12
  10.0 31.5 %copy-start.7 = (f32[2,512]{1,0:T(2,128)S(1)}, f32[2,512]{1,0:T(2,128)}, u32[]{:S(2)}) copy-start(f32[2,512]{1,0:T(2,128)} %param.41) | copy-start | bytes 12292
  10.0 31.5 %copy-start.9 = (f32[2,512]{1,0:T(2,128)S(1)}, f32[2,512]{1,0:T(2,128)}, u32[]{:S(2)}) copy-start(f32[2,512]{1,0:T(2,128)} %param.42) | copy-start | bytes 12292
  10.0 32.1 %copy-start.4 = (bf16[1,4,1,9,12,512]{5,1,4,3,2,0:T(4,128)(2,1)S(1)}, bf16[1,4,1,9,12,512]{5,1,4,3,2,0:T(4,128)(2,1)}, u32[]{:S(2)}) copy-start(bf16[1,4,1,9,12,512]{5,1,4,3,2,0:T(4,128)(2,1)} %param.49) | copy-start | bytes 1327108
  10.0 33.0 %copy-start.5 = (f32[1,3,512]{2,0,1:T(1,128)S(1)}, f32[1,3,512]{2,0,1:T(1,128)}, u32[]{:S(2)}) copy-start(f32[1,3,512]{2,0,1:T(1,128)} %param.46) | copy-start | bytes 18436
  10.0 33.0 %copy-start.6 = (f32[1,3,512]{2,0,1:T(1,128)S(1)}, f32[1,3,512]{2,0,1:T(1,128)}, u32[]{:S(2)}) copy-start(f32[1,3,512]{2,0,1:T(1,128)} %param.45) | copy-start | bytes 18436
  41.2 203.6 %reduce-scatter.2.cloned.1.call-start = ((), (), s32[]{:S(2)}) async-start(), calls=%async_computation.2 | async-start | bytes 3604480 | tf_op jit(solution)/shard_map/reduce_scatter | solution.py:739
  188.3 1.0 copy-start.3
  188.3 2.1 copy-start.11
  222.1 13.1 %copy-start.13 = (f32[1,3,2,512]{3,2,1,0:T(2,128)S(1)}, f32[1,3,2,512]{3,2,1,0:T(2,128)}, u32[]{:S(2)}) copy-start(f32[1,3,2,512]{3,2,1,0:T(2,128)} %param.47) | copy-start | bytes 36868
  222.1 13.1 %copy-start.14 = (f32[1,3,2,512]{3,2,1,0:T(2,128)S(1)}, f32[1,3,2,512]{3,2,1,0:T(2,128)}, u32[]{:S(2)}) copy-start(f32[1,3,2,512]{3,2,1,0:T(2,128)} %param.48) | copy-start | bytes 36868
  349.0 6.2 %copy-start = (bf16[3,512,512]{2,1,0:T(8,128)(2,1)S(1)}, bf16[3,512,512]{2,1,0:T(8,128)(2,1)}, u32[]{:S(2)}) copy-start(bf16[3,512,512]{2,1,0:T(8,128)(2,1)} %get-tuple-element.109.x) | copy-start | bytes 4718596
  355.3 2.8 copy-start.1
  358.1 1.9 copy-start.17
  358.1 2.0 copy-start.8
  358.1 2.0 copy-start.10
  358.1 2.0 copy-start.15
  358.1 2.0 copy-start.16
  358.1 3.8 %copy-start.2 = (f32[432,512]{1,0:T(8,128)S(1)}, f32[432,512]{1,0:T(8,128)}, u32[]{:S(2)}) copy-start(f32[432,512]{1,0:T(8,128)} %get-tuple-element.100) | copy-start | bytes 2654212
Sparse Core Ops, SparseCore 0:
  41.3 61.6 all-gather.1
  188.5 56.3 reduce-scatter.1

commit v3 on v2

--- a/solution.py
+++ b/solution.py
@@ -295,12 +295,12 @@
 
 def trunk_forward_body(
     geometry, tasks, batches,
-    index, infos, x, kernel_slots, scales,
+    index, infos, x_far, kernel_slots, scales,
     enc_totals, dec_totals, features, *rest,
 ):
-    kept, (enc_pre, dec_pre, spread), rest = rest[:6], rest[6:9], rest[9:]
+    kept, (enc_pre, dec_pre, spread), rest = rest[:5], rest[5:8], rest[8:]
     (
-        enc_taps, dec_taps, wide, tap,
+        x, x_loaded, enc_taps, dec_taps, wide, tap,
         work, pooled, pooled_all, part, pool_sends, pool_receives, sends, receives,
     mine, slots, total_sends, total_receives, saved,
     ) = rest
@@ -312,9 +312,10 @@
     choice = pool_choice(height, breadth, windows, True)
     narrow = choice.astype(BF)
 
-    sources = (x, enc_taps, dec_taps, enc_pre, dec_pre, spread)
+    x_load = pltpu.make_async_copy(x_far, x, x_loaded)
+    x_load.start()
+    sources = (enc_taps, dec_taps, enc_pre, dec_pre, spread)
     saves = [pltpu.make_async_copy(a, b, saved.at[k]) for k, (a, b) in enumerate(zip(sources, kept))]
-    saves[0].start()
     channels = x.shape[1]
 
     def widen(i, carry):
@@ -338,7 +339,8 @@
 
     lax.fori_loop(0, wide.shape[0] // channels, widen, 0)
     fetch(enc_taps, 0, 0, 9)
-    saves[1].start()
+    saves[0].start()
+    x_load.wait()
 
     def conv(x, taps, pre):
         def image(i, rows, carry):
@@ -361,7 +363,7 @@
         )
 
     sums = conv(x, enc_taps, enc_pre)
-    saves[3].start()
+    saves[2].start()
     greet((("task", tasks), ("batch", batches)))
     totals = total(0, sums, lambda: fetch(dec_taps, 9, 0, 4))
     put_sums(enc_totals, totals)
@@ -392,7 +394,7 @@
 
     each_image(geometry, pool, 0)
     fetch(dec_taps, 9, 4, 9)
-    saves[2].start()
+    saves[1].start()
 
     def unpool(i, rows, carry):
         for step in range(1, tasks):
@@ -402,9 +404,9 @@
         return carry
 
     each_image(geometry, unpool, 0)
-    saves[5].start()
+    saves[4].start()
     sums = conv(spread, dec_taps, dec_pre)
-    saves[4].start()
+    saves[3].start()
     totals = total(1, sums)
     put_sums(dec_totals, totals)
     scale = rows_of(scales, 2, 2)
@@ -450,18 +452,20 @@
     taps = shape((channels, 9 * width), BF)
     outs = [
         shape((8, width), F32), shape((8, width), F32), shape(x.shape, BF),
-        shape(x.shape, BF), taps, taps,
+        taps, taps,
         tall, tall, shape(x.shape, BF),
     ]
     return exchange_kernel(
         functools.partial(trunk_forward_body, geometry, tasks, batches),
         outs,
-        "svvvv",
+        "svhvv",
         (index, infos, x, kernel_slots, scales),
         [
             pltpu.VMEM(tall.shape, F32),
             pltpu.VMEM(tall.shape, F32),
             pltpu.VMEM(x.shape, BF),
+            pltpu.VMEM(x.shape, BF),
+            pltpu.SemaphoreType.DMA,
             pltpu.VMEM(taps.shape, BF),
             pltpu.VMEM(taps.shape, BF),
             pltpu.VMEM(kernel_slots.shape, F32),
@@ -473,11 +477,11 @@
         ]
         + [pltpu.SemaphoreType.DMA((number, tasks))] * 4
         + total_scratch(2, batches)
-        + [pltpu.SemaphoreType.DMA((6,))],
+        + [pltpu.SemaphoreType.DMA((5,))],
         1,
         60,
         flops=4 * x.size * taps.shape[1],
-        places_out="vvvhhhhhh",
+        places_out="vvvhhhhh",
     )
 
 
@@ -520,7 +524,7 @@
         )
 
     if summing:
-        near, near_sends, near_receives = rest[18:]
+        near, near_sends, near_receives, summed, saved = rest[18:]
         place, core, chips = pair_place(batches)
         block = near.shape[1]
 
@@ -669,7 +673,8 @@
         for chip in (*range(1, chips), 0):
             near_copy(chip).wait_recv()
             own = block_rows(grads, 2 * chip + core, block)[...].astype(F32)
-            grads_out[chip] = (own + near[chip].astype(F32)).astype(BF)
+            summed[chip] = (own + near[chip].astype(F32)).astype(BF)
+            pltpu.make_async_copy(summed.at[chip], grads_out.at[chip], saved.at[chip]).start()
     else:
         grads_out[...] = grads[...]
     put_sums(norm_sums, sums_one + sums_two + sums_three)
@@ -689,6 +694,7 @@
     if summing:
         for chip in range(chips):
             near_copy(chip).wait_send()
+            pltpu.make_async_copy(summed.at[chip], grads_out.at[chip], saved.at[chip]).wait()
 
 
 def head(geometry, tasks, batches, infos, features, weights, cotangent, scales, counts):
@@ -709,6 +715,7 @@
     if summing:
         scratch = [pltpu.VMEM((chips, block, channels), BF)]
         scratch += [pltpu.SemaphoreType.DMA((chips,))] * 2
+        scratch += [pltpu.VMEM((chips, block, channels), BF), pltpu.SemaphoreType.DMA((chips,))]
     pooled, upstream, sums, grads = exchange_kernel(
         functools.partial(head_body, geometry, tasks, batches, summing),
         outs,
@@ -734,6 +741,7 @@
         2,
         61,
         flops=6 * total * channels * weights.shape[0],
+        places_out="vvvh" if summing else "vvvv",
     )
     if summing:
         owned = lax.psum_scatter(
@@ -750,12 +758,17 @@
     infos, upstream, enc_totals, dec_totals, scales, *rest,
 ):
     kept, rest = rest[:6], rest[6:]
-    (enc_grad, dec_grad, flow_out, norm_sums), rest = rest[:4], rest[4:]
+    outs, norm_sums, rest = rest[:3], rest[3], rest[4:]
     (x, enc_taps, dec_taps, enc_pre, dec_pre, spread), rest = rest[:6], rest[6:]
     (
         nine, change, packed, arrived, pooled, sends, receives,
         mine, slots, total_sends, total_receives, loaded,
+        enc_grad, dec_grad, flow_out, saved,
     ) = rest
+    saves = [
+        pltpu.make_async_copy(a, b, saved.at[k])
+        for k, (a, b) in enumerate(zip((enc_grad, dec_grad, flow_out), outs))
+    ]
     targets = (x, enc_taps, dec_taps, enc_pre, dec_pre, spread)
     loads = [pltpu.make_async_copy(a, b, loaded.at[k]) for k, (a, b) in enumerate(zip(kept, targets))]
     for k in (4, 2, 5, 3, 1, 0):
@@ -822,6 +835,7 @@
     back(dec_pre, totals, scale, dec_sums, dec_taps, put_packed)
     loads[5].wait()
     dec_grad[...] = dot_tn(spread[...], nine[...])
+    saves[1].start()
 
     def collect(i, carry):
         for step in range(1, tasks):
@@ -853,8 +867,12 @@
     loads[1].wait()
     back(enc_pre, totals, scale, enc_sums, enc_taps, put_flow)
     loads[0].wait()
+    saves[2].start()
     enc_grad[...] = dot_tn(x[...], nine[...])
+    saves[0].start()
     put_sums(norm_sums, enc_sums + dec_sums)
+    for copy in saves:
+        copy.wait()
 
 
 def trunk_backward(
@@ -886,46 +904,81 @@
         ]
         + [pltpu.SemaphoreType.DMA((number, tasks))] * 2
         + total_scratch(2, batches)
-        + [pltpu.SemaphoreType.DMA((6,))],
+        + [pltpu.SemaphoreType.DMA((6,))]
+        + [pltpu.VMEM(a.shape, a.dtype) for a in outs[:3]]
+        + [pltpu.SemaphoreType.DMA((3,))],
         3,
         60,
         flops=8 * x.size * enc_taps.shape[1],
-    )
-
-
-def to_slots_body(index, enc, dec, slots, wide):
-    count = slots.shape[0]
+        places_out="hhhv",
+    )
+
+
+def to_slots_body(index, enc_far, dec_far, slots, enc, dec, wide, low, load, save):
+    count = wide.shape[0]
     channels = enc.shape[0]
-    width = slots.shape[1]
+    width = wide.shape[1]
     step = 1024
     group = 32
-    for p in range(18):
-        source = enc if p < 9 else dec
-        q = p % 9
-
-        def place(i, carry):
-            base = pl.multiple_of(i * group, group)
-            values = source[pl.ds(base, group), q * width : (q + 1) * width]
-            for u in range(group):
-                wide[pl.ds(index[p * channels + base + u], 1), :] = values[u : u + 1, :]
-            return carry
-
-        lax.fori_loop(0, channels // group, place, 0)
+    loads = [
+        pltpu.make_async_copy(a, b, load.at[k])
+        for k, (a, b) in enumerate(((dec_far, dec), (enc_far, enc)))
+    ]
+    for copy in loads:
+        copy.start()
+    for kernel, copy in ((1, loads[0]), (0, loads[1])):
+        copy.wait()
+        source = dec if kernel else enc
+        for q in range(9):
+
+            def place(i, carry):
+                base = pl.multiple_of(i * group, group)
+                first = (9 * kernel + q) * channels + base
+                values = source[pl.ds(base, group), q * width : (q + 1) * width]
+                for u in range(group):
+                    wide[pl.ds(index[first + u], 1), :] = values[u : u + 1, :]
+                return carry
+
+            lax.fori_loop(0, channels // group, place, 0)
+
+    def out(i):
+        rows = pl.ds(pl.multiple_of(i * step, step), step)
+        return pltpu.make_async_copy(low.at[rows, :], slots.at[rows, :], save.at[i])
 
     def narrow(i, carry):
         rows = pl.ds(pl.multiple_of(i * step, step), step)
-        slots[rows, :] = wide[rows, :].astype(BF)
+        low[rows, :] = wide[rows, :].astype(BF)
+        out(i).start()
         return carry
 
+    def end(i, carry):
+        out(i).wait()
+        return carry
+
     lax.fori_loop(0, count // step, narrow, 0)
+    lax.fori_loop(0, count // step, end, 0)
 
 
 def to_slots(index, enc, dec):
     width = enc.shape[1] // 9
     dims = (index.shape[0], width)
-    return run(
-        to_slots_body, [shape(dims, BF)], "svv", (index, enc, dec), [pltpu.VMEM(dims, F32)], vmem=60
-    )[0]
+    far = pl.BlockSpec(memory_space=pltpu.HBM)
+    return pl.pallas_call(
+        to_slots_body,
+        out_shape=shape(dims, BF),
+        in_specs=[SMEM_SPEC, far, far],
+        out_specs=far,
+        scratch_shapes=[
+            pltpu.VMEM(enc.shape, F32),
+            pltpu.VMEM(dec.shape, F32),
+            pltpu.VMEM(dims, F32),
+            pltpu.VMEM(dims, BF),
+            pltpu.SemaphoreType.DMA((2,)),
+            pltpu.SemaphoreType.DMA((dims[0] // 1024,)),
+        ],
+        compiler_params=pltpu.CompilerParams(vmem_limit_bytes=60 * MIB),
+        cost_estimate=pl.CostEstimate(flops=10000 * MIB, bytes_accessed=8 * MIB, transcendentals=0),
+    )(index, enc, dec)
 
 
 def adam(gradient, moment_one, moment_two):
@@ -1329,10 +1382,10 @@
 
 def tail_body(
     tasks, batches, cuts, pieces,
-    slots, flow, sums, owners, head_grad,
+    slots, flow, sums, owners, head_far,
     weight, one, two, head_weight, head_one, head_two, basis, head_basis,
     input_grad, norm_sums, state_new, head_state_new, grams, head_grams,
-    grad, part, state, head_state, mine, head_mine, bases, low,
+    grad, part, state, head_state, mine, head_mine, bases, low, head_grad, flow_own,
     flow_in, flow_send, flow_receive, send, receive, sum_send, sum_receive,
     *rest,
 ):
@@ -1436,9 +1489,12 @@
         (weight, state.at[0]),
         (one, state.at[1]),
         (two, state.at[2]),
+        (head_far, head_grad),
+        (block_rows(flow, task, pixels), flow_own),
     ]
     loads = [pltpu.make_async_copy(a, b, load.at[k]) for k, (a, b) in enumerate(moves)]
-    for copy in loads:
+    loads[8].start()
+    for copy in (*loads[:8], loads[9]):
         copy.start()
     saves = [
         pltpu.make_async_copy(state, state_new, save.at[0]),
@@ -1454,6 +1510,7 @@
         flow_copy(step).start()
     norm_sums[:, columns_of(task, width)] = sums[...]
     row_sums[0][1]()
+    loads[8].wait()
     put_packed_grams(head_mine, head_grad, head_marks(0, head_grad.shape[0]))
     head_start, head_middle, head_relay, head_end = sum_of(head_mine, head_scratch)
     row_sums[0][2]()
@@ -1477,7 +1534,8 @@
 
     soap_rows(cuts, head_grad, head_marks, head_state, low, trunk_total)
     saves[1].start()
-    total = block_rows(flow, task, pixels)[...].astype(F32)
+    loads[9].wait()
+    total = flow_own[...].astype(F32)
     for step in range(1, tasks):
         flow_copy(step, True).wait_recv()
         total = total + flow_in[step - 1].astype(F32)
@@ -1500,7 +1558,7 @@
     start()
     middle()
     head_spread[1]()
-    for copy in loads[5:]:
+    for copy in loads[5:8]:
         copy.wait()
     relay()
     soap_rows(cuts, grad, trunk_marks, state, low, 0, 0, cuts // 2)
@@ -1666,7 +1724,7 @@
             shape((gram_rows, channels), kind),
             shape((head_rows, PANEL), BF),
         ],
-        "vvvvvhhhhhhhh",
+        "vhvvhhhhhhhhh",
         (*local_grads, *rows, basis, head_basis),
         [
             pltpu.VMEM((total, channels), BF),
@@ -1677,6 +1735,8 @@
             pltpu.VMEM((head_rows, PANEL), BF),
             pltpu.VMEM(square, F32),
             pltpu.VMEM(square, BF),
+            pltpu.VMEM(head_grad.shape, BF),
+            pltpu.VMEM((pixels, channels), BF),
             pltpu.VMEM((tasks - 1, pixels, channels), BF),
         ]
         + [pltpu.SemaphoreType.DMA((tasks,))] * 2
@@ -1688,7 +1748,7 @@
         + [pltpu.SemaphoreType.DMA((2, max(chips, 4)))] * 2
         + [pltpu.SemaphoreType.DMA((tasks, chips))] * 2
         + [pltpu.SemaphoreType.DMA((tasks + 1, chips))] * 2
-        + [pltpu.SemaphoreType.DMA((8,)), pltpu.SemaphoreType.DMA((2,))],
+        + [pltpu.SemaphoreType.DMA((10,)), pltpu.SemaphoreType.DMA((2,))],
         5,
         60,
         flops=50000 * MIB,
@@ -1803,7 +1863,7 @@
     )
     task_features = pooled.reshape(cotangent.shape)
     enc_grad, dec_grad, flow, trunk_sums = trunk_backward(
-        geometry, tasks, batches, infos, upstream, enc_totals, dec_totals, scales, kept
+        geometry, tasks, batches, infos, upstream, enc_totals, dec_totals, scales, (x, *kept)
     )
     input_grad, norm_sums, results = finish(
         tasks, batches,

time: 373 us -> 372 us (level)
  no operation moved by 1% of the time
where the time goes in v3:
time: 372 us; the launch traced here: 368 us
  Pallas kernels  326 us (88%)
  between operations  15.3 us (4%)
  waiting for transfers between devices  12.6 us (3%)
  local copies, waits for them, and re-layouts  8.88 us (2%)
  other arithmetic  5.6 us (2%)
    pallas_call x6, Pallas kernels, exchange_kernel(): pl.pallas_call(body, out_shape=tuple(outs), in_specs=[SPECS[s] for s in s...  270 us
    pallas_call x1, Pallas kernels, finish(): pl.pallas_call(renew_body, out_shape=(*outs[:8], shape(own, BF)), in_spec...  42.9 us
    pallas_call x1, Pallas kernels, to_slots(): pl.pallas_call(to_slots_body, out_shape=shape(dims, BF), in_specs=[SMEM_S...  13.4 us
    reduce_scatter x1, waiting for transfers between devices, head(): lax.psum_scatter(grads.reshape(chips * block, channels), 'batch', scatter...  7.91 us
  transfers between devices with their start and end apart: 2, of which 2 were waited for; matrix products, arithmetic and copies ran while one was open for 1% of the time, Pallas kernels for 27%

profile of v3, /device:TPU:0, one launch (start us, length us, event | category | flops | bytes accessed | tf_op | source)
XLA Modules:
  0.0 368.5 jit_solution(4766067851190791030)
XLA Ops:
  7.2 0.0 all-gather.2.cloned.1.call-start
  7.2 0.1 iota_add_fusion
  7.3 0.7 copy.62
  8.0 0.1 broadcast_compare_fusion
  8.1 0.1 eq.42
  8.9 0.1 and.53
  9.0 0.1 and.54
  9.1 0.1 and.56
  9.3 0.1 scatter.14.info
  9.3 0.0 copy-start.12
  9.4 0.6 copy-done.12
  10.0 0.0 copy-start.7
  10.0 0.0 copy-start.6
  10.0 31.2 %shard_map.358 = (bf16[9216,128]{1,0:T(8,128)(2,1)}, bf16[1728,512]{1,0:T(8,128)(2,1)}, f32[32,512]{1,0:T(8,128)}, f32[1152,2]{1,0:T(8,128)}, bf16[704,512]{1,0:T(8,128)(2,1)}) custom-call(bf16[432,512]{1,0:T(8,128)(2,1)} %bitcast.58, f32[8,512]{1,0:T(8,128)} %copy-done.12, s32[72,128]{1,0:T(8,128)} %bitcast.59, f32[1152,512]{1,0:T(8,128)} %weight.3, ...), custom_call_target="tpu_custom_call" | custom-call | flops 20971520000 | bytes 9221120 | tf_op jit(solution)/shard_map/pallas_call | solution.py:232
  41.2 0.0 all-gather.2.cloned.1.call-update
  41.2 0.3 reduce-scatter.2.cloned.1.call-start
  41.5 0.0 copy-done.7
  41.5 0.0 copy-done.9
  41.5 0.6 copy.43
  42.1 0.0 copy-done.4
  42.1 0.8 copy.44.cotangent
  43.0 0.0 copy-done.5
  43.0 0.0 copy-done.6
  43.0 0.6 reshape.262.scales
  43.6 54.8 %shard_map.359 = (f32[8,128]{1,0:T(8,128)}, f32[8,128]{1,0:T(8,128)}, bf16[1728,512]{1,0:T(8,128)(2,1)}, bf16[512,1152]{1,0:T(8,128)(2,1)}, bf16[512,1152]{1,0:T...) custom-call(s32[9216]{0:T(1024)} %index.3, f32[32,512]{1,0:T(8,128)} %get-tuple-element.78.infos, ...), custom_call_target="tpu_custom_call" | custom-call | flops 4076863488 | bytes 11909120 | tf_op jit(solution)/shard_map/pallas_call | solution.py:232
  98.4 4.6 %all-gather.2.cloned.1.call-done.weights = bf16[5632,512]{1,0:T(8,128)(2,1)} async-done(((bf16[704,512]{1,0:T(8,128)(2,1)}), bf16[5632,512]{1,0:T(8,128)(2,1)}) %all-gather.2.cloned.1.call-update) | async-done | bytes 5767184 | tf_op jit(solution)/shard_map/all_gather | solution.py:1853
  103.0 84.5 %shard_map.360 = (bf16[4,108,512]{2,1,0:T(8,128)(2,1)}, f32[1728,128]{1,0:T(8,128)}, f32[8,512]{1,0:T(8,128)}, bf16[4,704,512]{2,1,0:T(8,128)(2,1)}) custom-call(f32[32,512]{1,0:T(8,128)} %get-tuple-element.78.infos, bf16[1728,512]{1,0:T(8,128)(2,1)} %get-tuple-element.81.features, bf16[5632,512]{1,0:T(8,128)(2,1)} %all-gather.2.cloned.1.call-done.weights, ...), custom_call_target="tpu_custom_call" | custom-call | flops 29896998912 | bytes 12288000 | tf_op jit(solution)/shard_map/pallas_call | solution.py:232
  187.5 0.0 copy-start.3
  187.5 0.0 copy-start.11
  187.5 0.0 copy-start.13
  187.5 0.0 copy-start.14
  187.6 0.0 reduce-scatter.2.cloned.1.call-update
  187.6 0.9 copy-done.3
  188.5 1.1 copy.45
  189.6 0.0 copy-done.11
  189.7 0.2 rev.7
  189.8 0.0 copy-done.13
  189.8 0.0 copy-done.14
  189.8 0.7 maximum_subtract_fusion
  190.5 32.2 %shard_map.361 = (f32[512,1152]{1,0:T(8,128)}, f32[512,1152]{1,0:T(8,128)}, bf16[1728,512]{1,0:T(8,128)(2,1)}, f32[8,128]{1,0:T(8,128)}) custom-call(f32[32,512]{1,0:T(8,128)} %get-tuple-element.78.infos, f32[1728,128]{1,0:T(8,128)} %get-tuple-element.85.upstream, f32[8,128]{1,0:T(8,128)} %get-tuple-element.83.counts.enc_totals, ...), custom_call_target="tpu_custom_call" | custom-call | flops 8153726976 | bytes 15120384 | tf_op jit(solution)/shard_map/pallas_call | solution.py:232
  222.7 13.4 %shard_map.362.slots = bf16[9216,128]{1,0:T(8,128)(2,1)} custom-call(s32[9216]{0:T(1024)} %index.3, f32[512,1152]{1,0:T(8,128)} %get-tuple-element.92.enc_far, f32[512,1152]{1,0:T(8,128)} %get-tuple-element.93.dec_far), custom_call_target="tpu_custom_call" | custom-call | flops 10485760000 | bytes 8388608 | tf_op jit(solution)/shard_map/pallas_call | solution.py:966
  236.1 7.9 %reduce-scatter.2.cloned.1.call-done.head_far = bf16[704,512]{1,0:T(8,128)(2,1)} async-done(((bf16[2816,512]{1,0:T(8,128)(2,1)}), bf16[704,512]{1,0:T(8,128)(2,1)}) %reduce-scatter.2.cloned.1.call-update) | async-done | bytes 720912 | tf_op jit(solution)/shard_map/reduce_scatter | solution.py:747
  244.0 60.7 %shard_map.363 = (f32[432,512]{1,0:T(8,128)}, f32[8,512]{1,0:T(8,128)}, f32[3,1152,512]{2,1,0:T(8,128)}, f32[3,704,512]{2,1,0:T(8,128)}, bf16[1024,512]{1,0:T(8,128)(2,1)}, /*index=5*/bf16[3840,128]{1,0:T(8,128)(2,1)}) custom-call(bf16[9216,128]{1,0:T(8,128)(2,1)} %shard_map.362.slots, bf16[1728,512]{1,0:T(8,128)(2,1)} %get-tuple-element.94.flow, ...), custom_call_target="tpu_custom_call" | custom-call | flops 52428800000 | bytes 35845120 | tf_op jit(solution)/shard_map/pallas_call | solution.py:232
  304.7 42.9 %shard_map.364 = (f32[1152,512]{1,0:T(8,128)}, f32[1152,512]{1,0:T(8,128)}, f32[1152,512]{1,0:T(8,128)}, f32[704,512]{1,0:T(8,128)}, f32[704,512]{1,0:T(8,128)},...) custom-call(s32[1]{0:T(128)} %bitcast.18.core, ...), custom_call_target="tpu_custom_call" | custom-call | flops 52428800000 | bytes 67108864 | tf_op jit(solution)/shard_map/pallas_call | solution.py:1763
  347.6 0.0 copy-start
  347.6 6.2 %shard_map.365 = bf16[3,512,512]{2,1,0:T(8,128)(2,1)} custom-call(bf16[3,512,512]{2,1,0:T(8,128)(2,1)} %get-tuple-element.107.x), custom_call_target="tpu_custom_call" | custom-call | flops 5242880000 | bytes 3145728 | tf_op jit(solution)/shard_map/pallas_call | solution.py:232
  353.8 0.0 copy-done
  353.8 0.0 copy-start.1
  353.8 2.8 select_convert_fusion
  356.6 0.0 copy-done.1
  356.7 0.0 copy-start.15
  356.7 0.0 copy-start.16
  356.7 0.0 copy-start.2
  356.7 1.9 bitcast_convert_fusion
  358.6 0.0 copy-done.17
  358.6 0.0 copy-done.8
  358.6 0.0 copy-done.10
  358.6 0.0 copy-done.15
  358.6 0.0 copy-done.16
  358.7 0.6 copy.49
  359.3 0.6 copy.50
  359.9 0.6 copy.51
  360.5 0.0 copy-done.2
  360.5 0.9 copy.66
  (19 shorter events, 0.2 us)
Async XLA Ops:
  7.2 95.8 %all-gather.2.cloned.1.call-start = ((), (), s32[]{:S(2)}) async-start(), calls=%async_computation.1 | async-start | bytes 6488064 | tf_op jit(solution)/shard_map/all_gather | solution.py:1853
  9.3 0.6 copy-start.12
  10.0 31.5 %copy-start.7 = (f32[2,512]{1,0:T(2,128)S(1)}, f32[2,512]{1,0:T(2,128)}, u32[]{:S(2)}) copy-start(f32[2,512]{1,0:T(2,128)} %param.41) | copy-start | bytes 12292
  10.0 31.5 %copy-start.9 = (f32[2,512]{1,0:T(2,128)S(1)}, f32[2,512]{1,0:T(2,128)}, u32[]{:S(2)}) copy-start(f32[2,512]{1,0:T(2,128)} %param.42) | copy-start | bytes 12292
  10.0 32.2 %copy-start.4 = (bf16[1,4,1,9,12,512]{5,1,4,3,2,0:T(4,128)(2,1)S(1)}, bf16[1,4,1,9,12,512]{5,1,4,3,2,0:T(4,128)(2,1)}, u32[]{:S(2)}) copy-start(bf16[1,4,1,9,12,512]{5,1,4,3,2,0:T(4,128)(2,1)} %param.49) | copy-start | bytes 1327108
  10.0 33.0 %copy-start.5 = (f32[1,3,512]{2,0,1:T(1,128)S(1)}, f32[1,3,512]{2,0,1:T(1,128)}, u32[]{:S(2)}) copy-start(f32[1,3,512]{2,0,1:T(1,128)} %param.46) | copy-start | bytes 18436
  10.0 33.0 %copy-start.6 = (f32[1,3,512]{2,0,1:T(1,128)S(1)}, f32[1,3,512]{2,0,1:T(1,128)}, u32[]{:S(2)}) copy-start(f32[1,3,512]{2,0,1:T(1,128)} %param.45) | copy-start | bytes 18436
  41.2 202.8 %reduce-scatter.2.cloned.1.call-start = ((), (), s32[]{:S(2)}) async-start(), calls=%async_computation.2 | async-start | bytes 3604480 | tf_op jit(solution)/shard_map/reduce_scatter | solution.py:747
  187.5 1.0 copy-start.3
  187.5 2.1 copy-start.11
  187.5 2.3 copy-start.13
  187.5 2.3 copy-start.14
  347.6 6.2 %copy-start = (bf16[3,512,512]{2,1,0:T(8,128)(2,1)S(1)}, bf16[3,512,512]{2,1,0:T(8,128)(2,1)}, u32[]{:S(2)}) copy-start(bf16[3,512,512]{2,1,0:T(8,128)(2,1)} %get-tuple-element.107.x) | copy-start | bytes 4718596
  353.8 2.8 copy-start.1
  356.6 1.9 copy-start.17
  356.6 2.0 copy-start.8
  356.6 2.0 copy-start.10
  356.7 2.0 copy-start.15
  356.7 2.0 copy-start.16
  356.7 3.8 %copy-start.2 = (f32[432,512]{1,0:T(8,128)S(1)}, f32[432,512]{1,0:T(8,128)}, u32[]{:S(2)}) copy-start(f32[432,512]{1,0:T(8,128)} %get-tuple-element.98) | copy-start | bytes 2654212
Sparse Core Ops, SparseCore 0:
  41.3 61.6 all-gather.1
  187.7 56.2 reduce-scatter.1

commit v4 on v3

--- a/solution.py
+++ b/solution.py
@@ -77,8 +77,8 @@
     return row, index - row * breadth
 
 
-def valid_rows(kind, height, breadth):
-    row, col = places(height, breadth)
+def valid_rows(kind, height, breadth, spot):
+    row, col = spot
     shrunk = kind > 0
     row_limit = jnp.where(shrunk, height // 2, height)
     col_limit = jnp.where(shrunk, breadth // 2, breadth)
@@ -120,8 +120,12 @@
     return pair + jnp.where(row % 2 == 0, move(pair, -breadth), move(pair, breadth))
 
 
+def sigmoid(values):
+    return 0.5 * jnp.tanh(0.5 * values) + 0.5
+
+
 def silu_back(scaled):
-    sig = jax.nn.sigmoid(scaled)
+    sig = sigmoid(scaled)
     return sig * (1.0 + scaled * (1.0 - sig))
 
 
@@ -246,28 +250,49 @@
     return infos[pl.ds(pl.multiple_of(i * 8, 8), 8), :]
 
 
-def valid_of(infos, i, height, breadth):
-    return valid_rows(info_rows(infos, i)[1:2, 0:1], height, breadth)
+def valid_of(infos, i, height, breadth, spot):
+    return valid_rows(info_rows(infos, i)[1:2, 0:1], height, breadth, spot)
 
 
 def chosen_cells(narrow, infos, i):
     return (narrow * info_rows(infos, i)[0:1, : narrow.shape[1]]).astype(BF)
 
 
-def norm_with(values, totals, scale):
+def norm_moments(totals):
     total, squares, count = totals
     center = total / count
-    inverse = lax.rsqrt(squares / count - center * center + EPS)
-    normal = (values - center) * inverse
-    return normal, inverse, normal * scale[0] + scale[1]
-
-
-def norm_back_with(upstream, normal, inverse, count, sums, scale, valid):
-    return scale[0] * inverse * (upstream - sums[0] / count - normal * (sums[1] / count)) * valid
+    return center, lax.rsqrt(squares / count - center * center + EPS)
+
+
+def norm_line(totals, scale):
+    center, inverse = norm_moments(totals)
+    slope = inverse * scale[0]
+    return slope, scale[1] - center * slope
+
+
+def norm_sums(totals, sums):
+    center, inverse = norm_moments(totals)
+    return [sums[0], inverse * (sums[1] - center * sums[0])]
+
+
+def norm_back_line(totals, sums, scale):
+    center, inverse = norm_moments(totals)
+    count = totals[2]
+    slope = inverse * scale[0]
+    lean = -slope * inverse * (sums[1] / count)
+    return slope, lean, -slope * (sums[0] / count) - lean * center
+
+
+def on_line(values, line):
+    return values * line[0] + line[1]
+
+
+def back_on_line(upstream, values, line, valid):
+    return (upstream * line[0] + values * line[1] + line[2]) * valid
 
 
 def silu(values):
-    return values * jax.nn.sigmoid(values)
+    return values * sigmoid(values)
 
 
 def window_count(height, breadth):
@@ -308,7 +333,8 @@
     width = enc_pre.shape[1]
     windows = window_count(height, breadth)
     task = lax.axis_index("task")
-    _, col = places(height, breadth)
+    spot = places(height, breadth)
+    _, col = spot
     choice = pool_choice(height, breadth, windows, True)
     narrow = choice.astype(BF)
 
@@ -344,7 +370,7 @@
 
     def conv(x, taps, pre):
         def image(i, rows, carry):
-            valid = valid_of(infos, i, height, breadth)
+            valid = valid_of(infos, i, height, breadth, spot)
             work[...] = dot(x[rows, :], taps[...])
             out = gather_taps(lambda p: work[:, p * width : (p + 1) * width], breadth, col)
             pre[rows, :] = out
@@ -380,9 +406,11 @@
             pooled.at[rows, :], target, pool_sends.at[i, step], pool_receives.at[i, step], peer, "task"
         )
 
+    line = norm_line(totals, scale)
+
     def pool(i, rows, carry):
-        valid = valid_of(infos, i, height, breadth)
-        _, _, scaled = norm_with(enc_pre[rows, :], totals, scale)
+        valid = valid_of(infos, i, height, breadth, spot)
+        scaled = on_line(enc_pre[rows, :], line)
         high, low = split(silu(scaled) * valid)
         mean = ((dot(narrow, high) + dot(narrow, low)) * 0.25).astype(BF)
         here = window_rows(i, windows)
@@ -418,9 +446,11 @@
             part.at[rows, :], target, sends.at[i, step], receives.at[i, step], peer, "task"
         )
 
+    last_line = norm_line(totals, scale)
+
     def finish(i, rows, carry):
-        valid = valid_of(infos, i, height, breadth)
-        _, _, scaled = norm_with(dec_pre[rows, :], totals, scale)
+        valid = valid_of(infos, i, height, breadth, spot)
+        scaled = on_line(dec_pre[rows, :], last_line)
         low = (silu(scaled) * valid).astype(BF)
         part[rows, :] = low
         features[rows, columns_of(task, width)] = low
@@ -488,7 +518,7 @@
 def head_body(
     geometry, tasks, batches, summing,
     infos, features, weights, cotangent, scales, counts,
-    task_out, upstream, norm_sums, *rest,
+    task_out, upstream, sums_out, *rest,
 ):
     grads_out, rest = rest[0], rest[1:]
     (
@@ -501,7 +531,8 @@
     windows = task_out.shape[1]
     task = lax.axis_index("task")
     half = work.shape[2]
-    _, col = places(height, breadth)
+    spot = places(height, breadth)
+    _, col = spot
     widen = pool_choice(height, breadth, windows, False).astype(BF)
     narrow = pool_choice(height, breadth, windows, True).astype(BF)
     count = jnp.broadcast_to(counts[2:3, 0:1], (1, channels))
@@ -545,16 +576,18 @@
     loads[0].wait()
 
     def first_step(i, rows, carry):
-        valid = valid_of(infos, i, height, breadth)
+        valid = valid_of(infos, i, height, breadth, spot)
         return put_stats(pre_one, rows, dot(features[rows, :], first[...]), valid, carry)
 
     sums = each_image(geometry, first_step, nothing)
     greet((("task", tasks), ("batch", batches)))
     totals_one = total(0, sums) + [count]
 
+    line_one = norm_line(totals_one, scale_one)
+
     def second_step(i, rows, carry):
-        valid = valid_of(infos, i, height, breadth)
-        _, _, scaled = norm_with(pre_one[rows, :], totals_one, scale_one)
+        valid = valid_of(infos, i, height, breadth, spot)
+        scaled = on_line(pre_one[rows, :], line_one)
         low = (silu(scaled) * valid).astype(BF)
         hidden[rows, :] = low
         return put_stats(pre_two, rows, dot(low, second[...]), valid, carry)
@@ -562,10 +595,12 @@
     sums = each_image(geometry, second_step, nothing)
     totals_two = total(1, sums) + [count]
 
+    line_two = norm_line(totals_two, scale_two)
+
     def third_step(i, rows, carry):
-        valid = valid_of(infos, i, height, breadth)
-        _, _, scaled = norm_with(pre_two[rows, :], totals_two, scale_two)
-        low = (jax.nn.sigmoid(scaled) * features[rows, :].astype(F32)).astype(BF)
+        valid = valid_of(infos, i, height, breadth, spot)
+        scaled = on_line(pre_two[rows, :], line_two)
+        low = (sigmoid(scaled) * features[rows, :].astype(F32)).astype(BF)
         gated[rows, :] = low
         parts = []
         for j in range(channels // half):
@@ -579,35 +614,39 @@
     sums = each_image(geometry, third_step, nothing)
     totals_three = total(2, sums) + [count]
 
+    line_three = norm_line(totals_three, scale_three)
+
     def out_step(i, rows, carry):
-        valid = valid_of(infos, i, height, breadth)
-        normal, _, scaled = norm_with(pre_three[rows, :], totals_three, scale_three)
+        valid = valid_of(infos, i, height, breadth, spot)
+        values = pre_three[rows, :]
+        scaled = on_line(values, line_three)
         high, low = split(silu(scaled) * valid)
         mean = (dot(narrow, high) + dot(narrow, low)) * 0.25
         task_out[i] = mean.astype(BF)
         dy = silu_back(scaled) * dot(widen, cotangent[i]) * 0.25 * valid
         lower[rows, :] = dy
-        return carry[0] + col_sum(dy), carry[1] + col_sum(dy * normal)
+        return carry[0] + col_sum(dy), carry[1] + col_sum(dy * values)
 
     sums = each_image(geometry, out_step, nothing)
-    sums_three = total(3, sums)
+    sums_three = total(3, norm_sums(totals_three, sums))
+    back_three = norm_back_line(totals_three, sums_three, scale_three)
 
     def third_back(i, rows, carry):
-        valid = valid_of(infos, i, height, breadth)
-        normal, inverse, _ = norm_with(pre_three[rows, :], totals_three, scale_three)
-        dz = norm_back_with(lower[rows, :], normal, inverse, count, sums_three, scale_three, valid)
+        valid = valid_of(infos, i, height, breadth, spot)
+        dz = back_on_line(lower[rows, :], pre_three[rows, :], back_three, valid)
         for p, moved in enumerate(spread_taps(dz, breadth, col)):
             nine[p, rows, :] = moved.astype(BF)
         flow = None
         for p in range(9):
             piece = dot_nt(nine[p, rows, :], grads[kernel_rows(p), :])
             flow = piece if flow is None else flow + piece
+        values = pre_two[rows, :]
+        gate = sigmoid(on_line(values, line_two))
+        flow = flow * gate
         lower[rows, :] = flow
-        normal, _, scaled = norm_with(pre_two[rows, :], totals_two, scale_two)
-        gate = jax.nn.sigmoid(scaled)
-        dy = flow * features[rows, :].astype(F32) * gate * (1.0 - gate) * valid
+        dy = flow * features[rows, :].astype(F32) * (1.0 - gate)
         pre_three[rows, :] = dy
-        return carry[0] + col_sum(dy), carry[1] + col_sum(dy * normal)
+        return carry[0] + col_sum(dy), carry[1] + col_sum(dy * values)
 
     sums = each_image(geometry, third_back, nothing)
 
@@ -619,28 +658,26 @@
 
         lax.fori_loop(begin, end, tap, 0)
 
-    sums_two = total(4, sums, lambda: taps(0, 3))
+    sums_two = total(4, norm_sums(totals_two, sums), lambda: taps(0, 2))
+    back_two = norm_back_line(totals_two, sums_two, scale_two)
 
     def second_back(i, rows, carry):
-        valid = valid_of(infos, i, height, breadth)
-        normal, inverse, scaled = norm_with(pre_two[rows, :], totals_two, scale_two)
-        dz = norm_back_with(
-            pre_three[rows, :], normal, inverse, count, sums_two, scale_two, valid
-        ).astype(BF)
+        valid = valid_of(infos, i, height, breadth, spot)
+        dz = back_on_line(pre_three[rows, :], pre_two[rows, :], back_two, valid).astype(BF)
         out[rows, :] = dz
-        lower[rows, :] = lower[rows, :] * jax.nn.sigmoid(scaled)
-        normal, _, scaled = norm_with(pre_one[rows, :], totals_one, scale_one)
-        dy = silu_back(scaled) * dot_nt(dz, second[...]) * valid
+        values = pre_one[rows, :]
+        dy = silu_back(on_line(values, line_one)) * dot_nt(dz, second[...])
         pre_three[rows, :] = dy
-        return carry[0] + col_sum(dy), carry[1] + col_sum(dy * normal)
+        return carry[0] + col_sum(dy), carry[1] + col_sum(dy * values)
 
     sums = each_image(geometry, second_back, nothing)
 
     def weight_rows():
         grads[pl.ds(channels, channels), :] = dot_tn(hidden[...], out[...]).astype(BF)
-        taps(3, 5)
-
-    sums_one = total(5, sums, weight_rows)
+        taps(2, 3)
+
+    sums_one = total(5, norm_sums(totals_one, sums), weight_rows)
+    back_one = norm_back_line(totals_one, sums_one, scale_one)
 
     def flow_copy(i, rows, step, incoming=False):
         peer = lax.rem(task + (tasks - step if incoming else step), tasks)
@@ -650,11 +687,8 @@
         )
 
     def first_back(i, rows, carry):
-        valid = valid_of(infos, i, height, breadth)
-        normal, inverse, _ = norm_with(pre_one[rows, :], totals_one, scale_one)
-        dz = norm_back_with(
-            pre_three[rows, :], normal, inverse, count, sums_one, scale_one, valid
-        ).astype(BF)
+        valid = valid_of(infos, i, height, breadth, spot)
+        dz = back_on_line(pre_three[rows, :], pre_one[rows, :], back_one, valid).astype(BF)
         hidden[rows, :] = dz
         flow = (lower[rows, :] + dot_nt(dz, first[...])) * valid
         out[rows, :] = flow.astype(BF)
@@ -663,7 +697,7 @@
         return carry
 
     each_image(geometry, first_back, 0)
-    taps(5, 9)
+    taps(3, 9)
     if summing:
         for chip in range(1, chips):
             near_copy(chip).start()
@@ -677,7 +711,7 @@
             pltpu.make_async_copy(summed.at[chip], grads_out.at[chip], saved.at[chip]).start()
     else:
         grads_out[...] = grads[...]
-    put_sums(norm_sums, sums_one + sums_two + sums_three)
+    put_sums(sums_out, sums_one + sums_two + sums_three)
 
     def settle(i, rows, carry):
         for step in range(1, tasks):
@@ -758,7 +792,7 @@
     infos, upstream, enc_totals, dec_totals, scales, *rest,
 ):
     kept, rest = rest[:6], rest[6:]
-    outs, norm_sums, rest = rest[:3], rest[3], rest[4:]
+    outs, sums_out, rest = rest[:3], rest[3], rest[4:]
     (x, enc_taps, dec_taps, enc_pre, dec_pre, spread), rest = rest[:6], rest[6:]
     (
         nine, change, packed, arrived, pooled, sends, receives,
@@ -778,7 +812,8 @@
     width = enc_pre.shape[1]
     windows = window_count(height, breadth)
     task = lax.axis_index("task")
-    _, col = places(height, breadth)
+    spot = places(height, breadth)
+    _, col = spot
     widen = pool_choice(height, breadth, windows, False).astype(BF)
     narrow = pool_choice(height, breadth, windows, True)
     nothing = zero_rows(2, width)
@@ -789,20 +824,23 @@
         )
 
     def change_of(pre, totals, scale, flow):
+        line = norm_line(totals, scale)
+
         def image(i, rows, carry):
-            valid = valid_of(infos, i, height, breadth)
-            normal, _, scaled = norm_with(pre[rows, :], totals, scale)
-            dy = silu_back(scaled) * flow(i, rows) * valid
+            valid = valid_of(infos, i, height, breadth, spot)
+            values = pre[rows, :]
+            dy = silu_back(on_line(values, line)) * flow(i, rows) * valid
             change[rows, :] = dy
-            return carry[0] + col_sum(dy), carry[1] + col_sum(dy * normal)
-
-        return each_image(geometry, image, nothing)
+            return carry[0] + col_sum(dy), carry[1] + col_sum(dy * values)
+
+        return norm_sums(totals, each_image(geometry, image, nothing))
 
     def back(pre, totals, scale, sums, taps, put):
+        line = norm_back_line(totals, sums, scale)
+
         def image(i, rows, carry):
-            valid = valid_of(infos, i, height, breadth)
-            normal, inverse, _ = norm_with(pre[rows, :], totals, scale)
-            dz = norm_back_with(change[rows, :], normal, inverse, totals[2], sums, scale, valid)
+            valid = valid_of(infos, i, height, breadth, spot)
+            dz = back_on_line(change[rows, :], pre[rows, :], line, valid)
             for p, moved in enumerate(spread_taps(dz, breadth, col)):
                 nine[rows, p * width : (p + 1) * width] = moved.astype(BF)
             put(i, rows, dot_nt(nine[rows, :], taps[...]) * valid)
@@ -870,7 +908,7 @@
     saves[2].start()
     enc_grad[...] = dot_tn(x[...], nine[...])
     saves[0].start()
-    put_sums(norm_sums, enc_sums + dec_sums)
+    put_sums(sums_out, enc_sums + dec_sums)
     for copy in saves:
         copy.wait()
 
@@ -1189,7 +1227,9 @@
     number, height, breadth = geometry
     pixels = height * breadth
     for n in range(number):
-        valid = valid_rows(info[8 * n + 1 : 8 * n + 2, 0:1], height, breadth)
+        valid = valid_rows(
+            info[8 * n + 1 : 8 * n + 2, 0:1], height, breadth, places(height, breadth)
+        )
         rows = slice(n * pixels, (n + 1) * pixels)
         image[rows, :] = (image_raw[rows, :].astype(F32) * valid).astype(BF)
     greet_pairs(tasks, batches)
@@ -1355,21 +1395,18 @@
         tables[n][:, :PANEL] = dot3(dot_tn, product[n, :, here], product[n, :, here])
         tables[n][:, PANEL:] = unit
 
-    def group(q, carry):
-        rows = pl.ds(pl.multiple_of(q * GROUP, GROUP), GROUP)
-        turn = lax.rem(PANEL - q * GROUP, PANEL)
+    for first in range(0, PANEL, GROUP):
+        rows, rest = slice(first, first + GROUP), slice(first + GROUP, PANEL)
         done = [
-            factor_rows(tables[n][rows, :PANEL], tables[n][rows, PANEL:], turn)
+            factor_rows(tables[n][rows, :PANEL], tables[n][rows, PANEL:], (PANEL - first) % PANEL)
             for n in range(count)
         ]
         for n in range(count):
             upper, inverse = done[n]
             inverses[n][rows, :] = inverse
-            both = jnp.concatenate([upper, inverse], axis=1)
-            tables[n][...] = tables[n][...] - dot3(dot_tn, upper, both)
-        return carry
-
-    lax.fori_loop(0, PANEL // GROUP, group, 0)
+            if first + GROUP < PANEL:
+                both = jnp.concatenate([upper, inverse], axis=1)
+                tables[n][rest, :] = tables[n][rest, :] - dot3(dot_tn, upper[:, rest], both)
     for n in range(count):
         turned = dot3(dot_nt, product[n, :, here], inverses[n][...])
         made[n, :, here] = turned

time: 372 us -> 365 us (0.981)
  Pallas kernels: 326 us -> 319 us
    pallas_call x1, Pallas kernels: 42.9 us -> 38.9 us  [finish(): pl.pallas_call(renew_body, out_shape=(*outs[:8], shape(own, BF)), in_spec...]
  transfers between devices with their start and end apart: 2 -> 2, of which waited for: 2 -> 2; matrix products, arithmetic and copies ran while one was open for 1% -> 1% of each run, Pallas kernels for 27% -> 28%
where the time goes in v4:
time: 365 us; the launch traced here: 362 us
  Pallas kernels  319 us (87%)
  between operations  15.3 us (4%)
  waiting for transfers between devices  12.6 us (3%)
  local copies, waits for them, and re-layouts  8.88 us (2%)
  other arithmetic  5.6 us (2%)
    pallas_call x6, Pallas kernels, exchange_kernel(): pl.pallas_call(body, out_shape=tuple(outs), in_specs=[SPECS[s] for s in s...  267 us
    pallas_call x1, Pallas kernels, finish(): pl.pallas_call(renew_body, out_shape=(*outs[:8], shape(own, BF)), in_spec...  38.9 us
    pallas_call x1, Pallas kernels, to_slots(): pl.pallas_call(to_slots_body, out_shape=shape(dims, BF), in_specs=[SMEM_S...  13.3 us
    reduce_scatter x1, waiting for transfers between devices, head(): lax.psum_scatter(grads.reshape(chips * block, channels), 'batch', scatter...  7.97 us
  transfers between devices with their start and end apart: 2, of which 2 were waited for; matrix products, arithmetic and copies ran while one was open for 1% of the time, Pallas kernels for 28%

profile of v4, /device:TPU:0, one launch (start us, length us, event | category | flops | bytes accessed | tf_op | source)
XLA Modules:
  0.0 362.1 jit_solution(1742263803215377663)
XLA Ops:
  7.2 0.0 all-gather.2.cloned.1.call-start
  7.2 0.1 iota_add_fusion
  7.3 0.7 copy.62
  8.0 0.1 broadcast_compare_fusion
  8.1 0.1 eq.42
  8.9 0.1 and.53
  9.0 0.1 and.54
  9.1 0.1 and.56
  9.3 0.1 scatter.14.info
  9.3 0.0 copy-start.12
  9.4 0.6 copy-done.12
  10.0 0.0 copy-start.7
  10.0 0.0 copy-start.6
  10.0 31.2 %shard_map.358 = (bf16[9216,128]{1,0:T(8,128)(2,1)}, bf16[1728,512]{1,0:T(8,128)(2,1)}, f32[32,512]{1,0:T(8,128)}, f32[1152,2]{1,0:T(8,128)}, bf16[704,512]{1,0:T(8,128)(2,1)}) custom-call(bf16[432,512]{1,0:T(8,128)(2,1)} %bitcast.58, f32[8,512]{1,0:T(8,128)} %copy-done.12, s32[72,128]{1,0:T(8,128)} %bitcast.59, f32[1152,512]{1,0:T(8,128)} %weight.3, ...), custom_call_target="tpu_custom_call" | custom-call | flops 20971520000 | bytes 9221120 | tf_op jit(solution)/shard_map/pallas_call | solution.py:236
  41.2 0.0 all-gather.2.cloned.1.call-update
  41.2 0.2 reduce-scatter.2.cloned.1.call-start
  41.5 0.0 copy-done.7
  41.5 0.0 copy-done.9
  41.5 0.6 copy.43
  42.1 0.0 copy-done.4
  42.1 0.8 copy.44.cotangent
  42.9 0.0 copy-done.5
  42.9 0.0 copy-done.6
  42.9 0.6 reshape.262.scales
  43.6 54.8 %shard_map.359 = (f32[8,128]{1,0:T(8,128)}, f32[8,128]{1,0:T(8,128)}, bf16[1728,512]{1,0:T(8,128)(2,1)}, bf16[512,1152]{1,0:T(8,128)(2,1)}, bf16[512,1152]{1,0:T...) custom-call(s32[9216]{0:T(1024)} %index.3, f32[32,512]{1,0:T(8,128)} %get-tuple-element.78.infos, ...), custom_call_target="tpu_custom_call" | custom-call | flops 4076863488 | bytes 11909120 | tf_op jit(solution)/shard_map/pallas_call | solution.py:236
  98.4 4.6 %all-gather.2.cloned.1.call-done.weights = bf16[5632,512]{1,0:T(8,128)(2,1)} async-done(((bf16[704,512]{1,0:T(8,128)(2,1)}), bf16[5632,512]{1,0:T(8,128)(2,1)}) %all-gather.2.cloned.1.call-update) | async-done | bytes 5767184 | tf_op jit(solution)/shard_map/all_gather | solution.py:1890
  103.0 82.0 %shard_map.360 = (bf16[4,108,512]{2,1,0:T(8,128)(2,1)}, f32[1728,128]{1,0:T(8,128)}, f32[8,512]{1,0:T(8,128)}, bf16[4,704,512]{2,1,0:T(8,128)(2,1)}) custom-call(f32[32,512]{1,0:T(8,128)} %get-tuple-element.78.infos, bf16[1728,512]{1,0:T(8,128)(2,1)} %get-tuple-element.81.features, bf16[5632,512]{1,0:T(8,128)(2,1)} %all-gather.2.cloned.1.call-done.weights, ...), custom_call_target="tpu_custom_call" | custom-call | flops 29896998912 | bytes 12288000 | tf_op jit(solution)/shard_map/pallas_call | solution.py:236
  185.1 0.0 copy-start.3
  185.1 0.0 copy-start.11
  185.1 0.0 copy-start.13
  185.1 0.0 copy-start.14
  185.1 0.0 reduce-scatter.2.cloned.1.call-update
  185.1 0.9 copy-done.3
  186.1 1.1 copy.45
  187.2 0.0 copy-done.11
  187.2 0.2 rev.7
  187.4 0.0 copy-done.13
  187.4 0.0 copy-done.14
  187.4 0.7 maximum_subtract_fusion
  188.1 32.2 %shard_map.361 = (f32[512,1152]{1,0:T(8,128)}, f32[512,1152]{1,0:T(8,128)}, bf16[1728,512]{1,0:T(8,128)(2,1)}, f32[8,128]{1,0:T(8,128)}) custom-call(f32[32,512]{1,0:T(8,128)} %get-tuple-element.78.infos, f32[1728,128]{1,0:T(8,128)} %get-tuple-element.85.upstream, f32[8,128]{1,0:T(8,128)} %get-tuple-element.83.counts.enc_totals, ...), custom_call_target="tpu_custom_call" | custom-call | flops 8153726976 | bytes 15120384 | tf_op jit(solution)/shard_map/pallas_call | solution.py:236
  220.3 13.3 %shard_map.362.slots = bf16[9216,128]{1,0:T(8,128)(2,1)} custom-call(s32[9216]{0:T(1024)} %index.3, f32[512,1152]{1,0:T(8,128)} %get-tuple-element.92.enc_far, f32[512,1152]{1,0:T(8,128)} %get-tuple-element.93.dec_far), custom_call_target="tpu_custom_call" | custom-call | flops 10485760000 | bytes 8388608 | tf_op jit(solution)/shard_map/pallas_call | solution.py:1004
  233.6 8.0 %reduce-scatter.2.cloned.1.call-done.head_far = bf16[704,512]{1,0:T(8,128)(2,1)} async-done(((bf16[2816,512]{1,0:T(8,128)(2,1)}), bf16[704,512]{1,0:T(8,128)(2,1)}) %reduce-scatter.2.cloned.1.call-update) | async-done | bytes 720912 | tf_op jit(solution)/shard_map/reduce_scatter | solution.py:781
  241.6 60.7 %shard_map.363 = (f32[432,512]{1,0:T(8,128)}, f32[8,512]{1,0:T(8,128)}, f32[3,1152,512]{2,1,0:T(8,128)}, f32[3,704,512]{2,1,0:T(8,128)}, bf16[1024,512]{1,0:T(8,128)(2,1)}, /*index=5*/bf16[3840,128]{1,0:T(8,128)(2,1)}) custom-call(bf16[9216,128]{1,0:T(8,128)(2,1)} %shard_map.362.slots, bf16[1728,512]{1,0:T(8,128)(2,1)} %get-tuple-element.94.flow, ...), custom_call_target="tpu_custom_call" | custom-call | flops 52428800000 | bytes 35845120 | tf_op jit(solution)/shard_map/pallas_call | solution.py:236
  302.3 38.9 %shard_map.364 = (f32[1152,512]{1,0:T(8,128)}, f32[1152,512]{1,0:T(8,128)}, f32[1152,512]{1,0:T(8,128)}, f32[704,512]{1,0:T(8,128)}, f32[704,512]{1,0:T(8,128)},...) custom-call(s32[1]{0:T(128)} %bitcast.18.core, ...), custom_call_target="tpu_custom_call" | custom-call | flops 52428800000 | bytes 67108864 | tf_op jit(solution)/shard_map/pallas_call | solution.py:1800
  341.1 0.0 copy-start
  341.2 6.2 %shard_map.365 = bf16[3,512,512]{2,1,0:T(8,128)(2,1)} custom-call(bf16[3,512,512]{2,1,0:T(8,128)(2,1)} %get-tuple-element.107.x), custom_call_target="tpu_custom_call" | custom-call | flops 5242880000 | bytes 3145728 | tf_op jit(solution)/shard_map/pallas_call | solution.py:236
  347.4 0.0 copy-done
  347.4 0.0 copy-start.1
  347.4 2.8 select_convert_fusion
  350.2 0.0 copy-done.1
  350.2 0.0 copy-start.15
  350.2 0.0 copy-start.16
  350.2 0.0 copy-start.2
  350.2 1.9 bitcast_convert_fusion
  352.1 0.0 copy-done.17
  352.1 0.0 copy-done.8
  352.2 0.0 copy-done.10
  352.2 0.0 copy-done.15
  352.2 0.0 copy-done.16
  352.2 0.6 copy.49
  352.8 0.6 copy.50
  353.4 0.6 copy.51
  354.0 0.0 copy-done.2
  354.0 0.9 copy.66
  (19 shorter events, 0.2 us)
Async XLA Ops:
  7.2 95.8 %all-gather.2.cloned.1.call-start = ((), (), s32[]{:S(2)}) async-start(), calls=%async_computation.1 | async-start | bytes 6488064 | tf_op jit(solution)/shard_map/all_gather | solution.py:1890
  9.3 0.6 copy-start.12
  10.0 31.5 %copy-start.7 = (f32[2,512]{1,0:T(2,128)S(1)}, f32[2,512]{1,0:T(2,128)}, u32[]{:S(2)}) copy-start(f32[2,512]{1,0:T(2,128)} %param.41) | copy-start | bytes 12292
  10.0 31.5 %copy-start.9 = (f32[2,512]{1,0:T(2,128)S(1)}, f32[2,512]{1,0:T(2,128)}, u32[]{:S(2)}) copy-start(f32[2,512]{1,0:T(2,128)} %param.42) | copy-start | bytes 12292
  10.0 32.1 %copy-start.4 = (bf16[1,4,1,9,12,512]{5,1,4,3,2,0:T(4,128)(2,1)S(1)}, bf16[1,4,1,9,12,512]{5,1,4,3,2,0:T(4,128)(2,1)}, u32[]{:S(2)}) copy-start(bf16[1,4,1,9,12,512]{5,1,4,3,2,0:T(4,128)(2,1)} %param.49) | copy-start | bytes 1327108
  10.0 33.0 %copy-start.5 = (f32[1,3,512]{2,0,1:T(1,128)S(1)}, f32[1,3,512]{2,0,1:T(1,128)}, u32[]{:S(2)}) copy-start(f32[1,3,512]{2,0,1:T(1,128)} %param.46) | copy-start | bytes 18436
  10.0 33.0 %copy-start.6 = (f32[1,3,512]{2,0,1:T(1,128)S(1)}, f32[1,3,512]{2,0,1:T(1,128)}, u32[]{:S(2)}) copy-start(f32[1,3,512]{2,0,1:T(1,128)} %param.45) | copy-start | bytes 18436
  41.2 200.4 %reduce-scatter.2.cloned.1.call-start = ((), (), s32[]{:S(2)}) async-start(), calls=%async_computation.2 | async-start | bytes 3604480 | tf_op jit(solution)/shard_map/reduce_scatter | solution.py:781
  185.1 1.0 copy-start.3
  185.1 2.1 copy-start.11
  185.1 2.3 copy-start.13
  185.1 2.3 copy-start.14
  341.1 6.2 %copy-start = (bf16[3,512,512]{2,1,0:T(8,128)(2,1)S(1)}, bf16[3,512,512]{2,1,0:T(8,128)(2,1)}, u32[]{:S(2)}) copy-start(bf16[3,512,512]{2,1,0:T(8,128)(2,1)} %get-tuple-element.107.x) | copy-start | bytes 4718596
  347.4 2.8 copy-start.1
  350.2 1.9 copy-start.17
  350.2 2.0 copy-start.8
  350.2 2.0 copy-start.10
  350.2 2.0 copy-start.15
  350.2 2.0 copy-start.16
  350.2 3.8 %copy-start.2 = (f32[432,512]{1,0:T(8,128)S(1)}, f32[432,512]{1,0:T(8,128)}, u32[]{:S(2)}) copy-start(f32[432,512]{1,0:T(8,128)} %get-tuple-element.98) | copy-start | bytes 2654212
Sparse Core Ops, SparseCore 0:
  41.3 61.6 all-gather.1
  185.3 56.2 reduce-scatter.1

commit v5 on v4

--- a/solution.py
+++ b/solution.py
@@ -797,7 +797,7 @@
     (
         nine, change, packed, arrived, pooled, sends, receives,
         mine, slots, total_sends, total_receives, loaded,
-        enc_grad, dec_grad, flow_out, saved,
+        enc_grad, dec_grad, flow_out, saved, sums_own, sum_sends, sum_receives,
     ) = rest
     saves = [
         pltpu.make_async_copy(a, b, saved.at[k])
@@ -898,6 +898,17 @@
     loads[3].wait()
     sums = change_of(enc_pre, totals, scale, widened)
     enc_sums = total(1, sums)
+    put_sums(sums_own, enc_sums + dec_sums)
+
+    def sum_copy(step, incoming=False):
+        peer = lax.rem(task + (tasks - step if incoming else step), tasks)
+        home = peer if incoming else task
+        return remote(sums_own, sums_out.at[:, columns_of(home, width)], sum_sends.at[step],
+                      sum_receives.at[step], peer, "task")
+
+    for step in range(1, tasks):
+        sum_copy(step).start()
+    sums_out[:, columns_of(task, width)] = sums_own[...]
 
     def put_flow(i, rows, flow):
         flow_out[rows, :] = flow.astype(BF)
@@ -908,9 +919,11 @@
     saves[2].start()
     enc_grad[...] = dot_tn(x[...], nine[...])
     saves[0].start()
-    put_sums(sums_out, enc_sums + dec_sums)
     for copy in saves:
         copy.wait()
+    for step in range(1, tasks):
+        sum_copy(step, True).wait_recv()
+        sum_copy(step).wait_send()
 
 
 def trunk_backward(
@@ -925,7 +938,7 @@
         shape(enc_taps.shape, F32),
         shape(dec_taps.shape, F32),
         shape(x.shape, BF),
-        shape((8, width), F32),
+        shape((8, channels), F32),
     ]
     return exchange_kernel(
         functools.partial(trunk_backward_body, geometry, tasks, batches),
@@ -944,7 +957,8 @@
         + total_scratch(2, batches)
         + [pltpu.SemaphoreType.DMA((6,))]
         + [pltpu.VMEM(a.shape, a.dtype) for a in outs[:3]]
-        + [pltpu.SemaphoreType.DMA((3,))],
+        + [pltpu.SemaphoreType.DMA((3,)), pltpu.VMEM((8, width), F32)]
+        + [pltpu.SemaphoreType.DMA((tasks,))] * 2,
         3,
         60,
         flops=8 * x.size * enc_taps.shape[1],
@@ -1419,11 +1433,11 @@
 
 def tail_body(
     tasks, batches, cuts, pieces,
-    slots, flow, sums, owners, head_far,
+    slots, flow, owners, head_far,
     weight, one, two, head_weight, head_one, head_two, basis, head_basis,
-    input_grad, norm_sums, state_new, head_state_new, grams, head_grams,
+    input_grad, state_new, head_state_new, grams, head_grams,
     grad, part, state, head_state, mine, head_mine, bases, low, head_grad, flow_own,
-    flow_in, flow_send, flow_receive, send, receive, sum_send, sum_receive,
+    flow_in, flow_send, flow_receive, send, receive,
     *rest,
 ):
     row_scratch = [rest[7 * k : 7 * k + 7] for k in range(pieces)]
@@ -1473,12 +1487,6 @@
         peer = peer_of(step, incoming)
         return remote(block_rows(flow, peer, pixels), flow_in.at[step - 1], flow_send.at[step],
                       flow_receive.at[step], peer, "task")
-
-    def sum_copy(step, incoming=False):
-        peer = peer_of(step, incoming)
-        home = peer if incoming else task
-        return remote(sums, norm_sums.at[:, columns_of(home, width)], sum_send.at[step],
-                      sum_receive.at[step], peer, "task")
 
     def part_copy(k, step, incoming=False):
         peer = peer_of(step, incoming)
@@ -1543,9 +1551,7 @@
     for stages in row_sums:
         stages[0]()
     for step in range(1, tasks):
-        sum_copy(step).start()
         flow_copy(step).start()
-    norm_sums[:, columns_of(task, width)] = sums[...]
     row_sums[0][1]()
     loads[8].wait()
     put_packed_grams(head_mine, head_grad, head_marks(0, head_grad.shape[0]))
@@ -1622,13 +1628,9 @@
     for hop in range(chips):
         for kind in range(tasks + 1):
             pair_copy(kind, hop, True).wait_recv()
-    for step in range(1, tasks):
-        sum_copy(step, True).wait_recv()
-
     for copy in saves:
         copy.wait()
     for step in range(1, tasks):
-        sum_copy(step).wait_send()
         for k in range(pieces):
             part_copy(k, step).wait_send()
         flow_copy(step).wait_send()
@@ -1737,7 +1739,7 @@
 
 
 def finish(tasks, batches, local_grads, rows, matrices):
-    slots, flow, sums, owners, head_grad = local_grads
+    slots, flow, owners, head_grad = local_grads
     stat, head_stat, basis, head_basis = matrices
     total, channels = rows[0].shape
     width = channels // tasks
@@ -1751,17 +1753,16 @@
     pieces = 2 if total % 64 == 0 else 1
     square = (trunk_total + head_total, channels, channels)
     pixels = flow.shape[0] // tasks
-    input_grad, norm_sums, *made = exchange_kernel(
+    input_grad, *made = exchange_kernel(
         functools.partial(tail_body, tasks, batches, cuts, pieces),
         [
             shape((pixels, channels), F32),
-            shape((8, channels), F32),
             shape((3, total, channels), F32),
             shape((3,) + head_grad.shape, F32),
             shape((gram_rows, channels), kind),
             shape((head_rows, PANEL), BF),
         ],
-        "vhvvhhhhhhhhh",
+        "vhvhhhhhhhhh",
         (*local_grads, *rows, basis, head_basis),
         [
             pltpu.VMEM((total, channels), BF),
@@ -1778,7 +1779,6 @@
         ]
         + [pltpu.SemaphoreType.DMA((tasks,))] * 2
         + [pltpu.SemaphoreType.DMA((pieces, tasks))] * 2
-        + [pltpu.SemaphoreType.DMA((tasks,))] * 2
         + pair_scratch(batches, slots.shape[0] // pieces, width, BF) * pieces
         + pair_scratch(batches, gram_rows, width, kind)
         + pair_scratch(batches, head_rows, PANEL, BF)
@@ -1789,7 +1789,7 @@
         5,
         60,
         flops=50000 * MIB,
-        places_out="vvhhvv",
+        places_out="vhhvv",
     )
     outs = [shape(a.shape, F32) for a in (*rows, *matrices)]
     hbm = pl.BlockSpec(memory_space=pltpu.HBM)
@@ -1829,7 +1829,7 @@
         jnp.where(core == which, made_low[:total], theirs[:total]).astype(F32)
         for which, total in enumerate((trunk_total, head_total))
     ]
-    return input_grad, norm_sums, results
+    return input_grad, results
 
 
 def local(
@@ -1899,12 +1899,12 @@
         cotangent.reshape(shown, pixels // 4, channels), head_scales, enc_totals,
     )
     task_features = pooled.reshape(cotangent.shape)
-    enc_grad, dec_grad, flow, trunk_sums = trunk_backward(
+    enc_grad, dec_grad, flow, norm_totals = trunk_backward(
         geometry, tasks, batches, infos, upstream, enc_totals, dec_totals, scales, (x, *kept)
     )
-    input_grad, norm_sums, results = finish(
+    input_grad, results = finish(
         tasks, batches,
-        (to_slots(row_slot, enc_grad, dec_grad), flow, trunk_sums, trunk_owners, head_owned),
+        (to_slots(row_slot, enc_grad, dec_grad), flow, trunk_owners, head_owned),
         (trunk_weight, trunk_mean_grad, trunk_mean_square,
          head_weight[0], head_mean_grad[0], head_mean_square[0]),
         (trunk_statistic, head_statistic[0], trunk_basis, head_basis[0]),
@@ -1917,7 +1917,7 @@
     ) = results
 
     trunk_norm = jnp.stack([trunk_gain, trunk_offset], axis=1)
-    trunk_norm_grad = norm_sums[:4].reshape(2, 2, channels)[:, ::-1]
+    trunk_norm_grad = norm_totals[:4].reshape(2, 2, channels)[:, ::-1]
     trunk_norm_one, trunk_norm_two, trunk_direction = adam(
         trunk_norm_grad, trunk_norm_mean_grad, trunk_norm_mean_square
     )

time: 365 us -> 363 us (level)
  transfers between devices with their start and end apart: 2 -> 2, of which waited for: 2 -> 2; matrix products, arithmetic and copies ran while one was open for 1% -> 2% of each run, Pallas kernels for 28% -> 28%
where the time goes in v5:
time: 363 us; the launch traced here: 360 us
  Pallas kernels  319 us (88%)
  between operations  15.3 us (4%)
  waiting for transfers between devices  9.86 us (3%)
  local copies, waits for them, and re-layouts  9.61 us (3%)
  other arithmetic  5.6 us (2%)
    pallas_call x6, Pallas kernels, exchange_kernel(): pl.pallas_call(body, out_shape=tuple(outs), in_specs=[SPECS[s] for s in s...  267 us
    pallas_call x1, Pallas kernels, finish(): pl.pallas_call(renew_body, out_shape=(*outs[:8], shape(own, BF)), in_spec...  38.9 us
    pallas_call x1, Pallas kernels, to_slots(): pl.pallas_call(to_slots_body, out_shape=shape(dims, BF), in_specs=[SMEM_S...  13.3 us
  transfers between devices with their start and end apart: 2, of which 2 were waited for; matrix products, arithmetic and copies ran while one was open for 2% of the time, Pallas kernels for 28%

profile of v5, /device:TPU:0, one launch (start us, length us, event | category | flops | bytes accessed | tf_op | source)
XLA Modules:
  0.0 359.8 jit_solution(2107396286574660525)
XLA Ops:
  7.2 0.0 all-gather.2.cloned.1.call-start
  7.2 0.1 iota_add_fusion
  7.3 0.7 copy.62
  8.0 0.1 broadcast_compare_fusion
  8.1 0.1 eq.42
  8.9 0.1 and.53
  9.0 0.1 and.54
  9.1 0.1 and.56
  9.3 0.1 scatter.14.info
  9.3 0.0 copy-start.10
  9.4 0.6 copy-done.10
  10.0 0.0 copy-start.7
  10.0 0.0 copy-start.8
  10.0 0.0 copy-start.4
  10.0 0.0 copy-start.5
  10.0 0.0 copy-start.6
  10.0 31.2 %shard_map.358 = (bf16[9216,128]{1,0:T(8,128)(2,1)}, bf16[1728,512]{1,0:T(8,128)(2,1)}, f32[32,512]{1,0:T(8,128)}, f32[1152,2]{1,0:T(8,128)}, bf16[704,512]{1,0:T(8,128)(2,1)}) custom-call(bf16[432,512]{1,0:T(8,128)(2,1)} %bitcast.58, f32[8,512]{1,0:T(8,128)} %copy-done.10, s32[72,128]{1,0:T(8,128)} %bitcast.59, f32[1152,512]{1,0:T(8,128)} %weight.3, ...), custom_call_target="tpu_custom_call" | custom-call | flops 20971520000 | bytes 9221120 | tf_op jit(solution)/shard_map/pallas_call | solution.py:236
  41.2 0.0 all-gather.2.cloned.1.call-update
  41.2 0.2 reduce-scatter.2.cloned.1.call-start
  41.5 0.0 copy-done.7
  41.5 0.0 copy-done.8
  41.5 0.6 copy.43
  42.1 0.0 copy-done.4
  42.1 0.8 copy.44.cotangent
  42.9 0.0 copy-done.5
  42.9 0.0 copy-done.6
  42.9 0.6 reshape.262.scales
  43.6 54.8 %shard_map.359 = (f32[8,128]{1,0:T(8,128)}, f32[8,128]{1,0:T(8,128)}, bf16[1728,512]{1,0:T(8,128)(2,1)}, bf16[512,1152]{1,0:T(8,128)(2,1)}, bf16[512,1152]{1,0:T...) custom-call(s32[9216]{0:T(1024)} %index.3, f32[32,512]{1,0:T(8,128)} %get-tuple-element.77.infos, ...), custom_call_target="tpu_custom_call" | custom-call | flops 4076863488 | bytes 11909120 | tf_op jit(solution)/shard_map/pallas_call | solution.py:236
  98.4 4.6 %all-gather.2.cloned.1.call-done.weights = bf16[5632,512]{1,0:T(8,128)(2,1)} async-done(((bf16[704,512]{1,0:T(8,128)(2,1)}), bf16[5632,512]{1,0:T(8,128)(2,1)}) %all-gather.2.cloned.1.call-update) | async-done | bytes 5767184 | tf_op jit(solution)/shard_map/all_gather | solution.py:1890
  103.0 82.0 %shard_map.360 = (bf16[4,108,512]{2,1,0:T(8,128)(2,1)}, f32[1728,128]{1,0:T(8,128)}, f32[8,512]{1,0:T(8,128)}, bf16[4,704,512]{2,1,0:T(8,128)(2,1)}) custom-call(f32[32,512]{1,0:T(8,128)} %get-tuple-element.77.infos, bf16[1728,512]{1,0:T(8,128)(2,1)} %get-tuple-element.80.features, bf16[5632,512]{1,0:T(8,128)(2,1)} %all-gather.2.cloned.1.call-done.weights, ...), custom_call_target="tpu_custom_call" | custom-call | flops 29896998912 | bytes 12288000 | tf_op jit(solution)/shard_map/pallas_call | solution.py:236
  185.1 0.0 copy-start.3
  185.1 0.0 reduce-scatter.2.cloned.1.call-update
  185.1 1.0 copy-done.3
  186.1 1.1 copy.45
  187.2 0.0 copy-start.13
  187.2 0.0 copy-start.14
  187.2 0.0 copy-start.9
  187.2 0.0 copy-start.11
  187.2 0.0 copy-start.12
  187.2 32.3 %shard_map.361 = (f32[512,1152]{1,0:T(8,128)}, f32[512,1152]{1,0:T(8,128)}, bf16[1728,512]{1,0:T(8,128)(2,1)}, f32[8,512]{1,0:T(8,128)}) custom-call(f32[32,512]{1,0:T(8,128)} %get-tuple-element.77.infos, f32[1728,128]{1,0:T(8,128)} %get-tuple-element.84.upstream, f32[8,128]{1,0:T(8,128)} %get-tuple-element.82.counts.enc_totals, ...), custom_call_target="tpu_custom_call" | custom-call | flops 8153726976 | bytes 15132672 | tf_op jit(solution)/shard_map/pallas_call | solution.py:236
  219.5 0.7 slice.49
  220.3 0.0 copy-done.13
  220.3 0.0 copy-done.14
  220.3 0.6 copy.49
  220.9 0.6 copy.50
  221.5 0.6 copy.51
  222.1 0.0 copy-done.9
  222.2 0.2 rev.7
  222.3 0.0 copy-done.11
  222.3 0.0 copy-done.12
  222.3 0.7 maximum_subtract_fusion
  223.0 13.3 %shard_map.362.slots = bf16[9216,128]{1,0:T(8,128)(2,1)} custom-call(s32[9216]{0:T(1024)} %index.3, f32[512,1152]{1,0:T(8,128)} %get-tuple-element.91.enc_far, f32[512,1152]{1,0:T(8,128)} %get-tuple-element.92.dec_far), custom_call_target="tpu_custom_call" | custom-call | flops 10485760000 | bytes 8388608 | tf_op jit(solution)/shard_map/pallas_call | solution.py:1018
  236.3 5.2 %reduce-scatter.2.cloned.1.call-done.head_far = bf16[704,512]{1,0:T(8,128)(2,1)} async-done(((bf16[2816,512]{1,0:T(8,128)(2,1)}), bf16[704,512]{1,0:T(8,128)(2,1)}) %reduce-scatter.2.cloned.1.call-update) | async-done | bytes 720912 | tf_op jit(solution)/shard_map/reduce_scatter | solution.py:781
  241.5 60.5 %shard_map.363 = (f32[432,512]{1,0:T(8,128)}, f32[3,1152,512]{2,1,0:T(8,128)}, f32[3,704,512]{2,1,0:T(8,128)}, bf16[1024,512]{1,0:T(8,128)(2,1)}, bf16[3840,128]{1,0:T(8,128)(2,1)}) custom-call(bf16[9216,128]{1,0:T(8,128)(2,1)} %shard_map.362.slots, bf16[1728,512]{1,0:T(8,128)(2,1)} %get-tuple-element.93.flow, f32[1152,2]{1,0:T(8,128)} %get-tuple-element.94.owners, ...), custom_call_target="tpu_custom_call" | custom-call | flops 52428800000 | bytes 35824640 | tf_op jit(solution)/shard_map/pallas_call | solution.py:236
  302.0 38.9 %shard_map.364 = (f32[1152,512]{1,0:T(8,128)}, f32[1152,512]{1,0:T(8,128)}, f32[1152,512]{1,0:T(8,128)}, f32[704,512]{1,0:T(8,128)}, f32[704,512]{1,0:T(8,128)},...) custom-call(s32[1]{0:T(128)} %bitcast.18.core, ...), custom_call_target="tpu_custom_call" | custom-call | flops 52428800000 | bytes 67108864 | tf_op jit(solution)/shard_map/pallas_call | solution.py:1800
  340.9 0.0 copy-start
  340.9 6.2 %shard_map.365 = bf16[3,512,512]{2,1,0:T(8,128)(2,1)} custom-call(bf16[3,512,512]{2,1,0:T(8,128)(2,1)} %get-tuple-element.105.x), custom_call_target="tpu_custom_call" | custom-call | flops 5242880000 | bytes 3145728 | tf_op jit(solution)/shard_map/pallas_call | solution.py:236
  347.1 0.0 copy-done
  347.1 0.0 copy-start.1
  347.1 2.8 select_convert_fusion
  349.9 0.0 copy-done.1
  349.9 1.9 bitcast_convert_fusion
  351.8 0.0 copy-done.2
  351.8 0.9 copy.66
  (13 shorter events, 0.1 us)
Async XLA Ops:
  7.2 95.8 %all-gather.2.cloned.1.call-start = ((), (), s32[]{:S(2)}) async-start(), calls=%async_computation.1 | async-start | bytes 6488064 | tf_op jit(solution)/shard_map/all_gather | solution.py:1890
  9.3 0.6 copy-start.10
  10.0 31.5 %copy-start.7 = (f32[2,512]{1,0:T(2,128)S(1)}, f32[2,512]{1,0:T(2,128)}, u32[]{:S(2)}) copy-start(f32[2,512]{1,0:T(2,128)} %param.41) | copy-start | bytes 12292
  10.0 31.5 %copy-start.8 = (f32[2,512]{1,0:T(2,128)S(1)}, f32[2,512]{1,0:T(2,128)}, u32[]{:S(2)}) copy-start(f32[2,512]{1,0:T(2,128)} %param.42) | copy-start | bytes 12292
  10.0 32.1 %copy-start.4 = (bf16[1,4,1,9,12,512]{5,1,4,3,2,0:T(4,128)(2,1)S(1)}, bf16[1,4,1,9,12,512]{5,1,4,3,2,0:T(4,128)(2,1)}, u32[]{:S(2)}) copy-start(bf16[1,4,1,9,12,512]{5,1,4,3,2,0:T(4,128)(2,1)} %param.49) | copy-start | bytes 1327108
  10.0 33.0 %copy-start.5 = (f32[1,3,512]{2,0,1:T(1,128)S(1)}, f32[1,3,512]{2,0,1:T(1,128)}, u32[]{:S(2)}) copy-start(f32[1,3,512]{2,0,1:T(1,128)} %param.46) | copy-start | bytes 18436
  10.0 33.0 %copy-start.6 = (f32[1,3,512]{2,0,1:T(1,128)S(1)}, f32[1,3,512]{2,0,1:T(1,128)}, u32[]{:S(2)}) copy-start(f32[1,3,512]{2,0,1:T(1,128)} %param.45) | copy-start | bytes 18436
  41.2 200.3 %reduce-scatter.2.cloned.1.call-start = ((), (), s32[]{:S(2)}) async-start(), calls=%async_computation.2 | async-start | bytes 3604480 | tf_op jit(solution)/shard_map/reduce_scatter | solution.py:781
  185.1 1.0 copy-start.3
  187.2 33.1 %copy-start.13 = (f32[2,2,512]{2,1,0:T(2,128)S(1)}, f32[2,2,512]{2,1,0:T(2,128)}, u32[]{:S(2)}) copy-start(f32[2,2,512]{2,1,0:T(2,128)} %param.43) | copy-start | bytes 24580
  187.2 33.1 %copy-start.14 = (f32[2,2,512]{2,1,0:T(2,128)S(1)}, f32[2,2,512]{2,1,0:T(2,128)}, u32[]{:S(2)}) copy-start(f32[2,2,512]{2,1,0:T(2,128)} %param.44) | copy-start | bytes 24580
  187.2 34.9 %copy-start.9 = (f32[8,512]{1,0:T(8,128)S(1)}, f32[8,512]{1,0:T(8,128)}, u32[]{:S(2)}) copy-start(f32[8,512]{1,0:T(8,128)} %get-tuple-element.111) | copy-start | bytes 49156
  187.2 35.1 %copy-start.11 = (f32[1,3,2,512]{3,2,1,0:T(2,128)S(1)}, f32[1,3,2,512]{3,2,1,0:T(2,128)}, u32[]{:S(2)}) copy-start(f32[1,3,2,512]{3,2,1,0:T(2,128)} %param.47) | copy-start | bytes 36868
  187.2 35.1 %copy-start.12 = (f32[1,3,2,512]{3,2,1,0:T(2,128)S(1)}, f32[1,3,2,512]{3,2,1,0:T(2,128)}, u32[]{:S(2)}) copy-start(f32[1,3,2,512]{3,2,1,0:T(2,128)} %param.48) | copy-start | bytes 36868
  340.9 6.2 %copy-start = (bf16[3,512,512]{2,1,0:T(8,128)(2,1)S(1)}, bf16[3,512,512]{2,1,0:T(8,128)(2,1)}, u32[]{:S(2)}) copy-start(bf16[3,512,512]{2,1,0:T(8,128)(2,1)} %get-tuple-element.105.x) | copy-start | bytes 4718596
  347.1 2.8 copy-start.1
  349.9 1.9 copy-start.2
Sparse Core Ops, SparseCore 0:
  41.3 61.6 all-gather.1
  185.2 56.2 reduce-scatter.1

commit v6 on v5

--- a/solution.py
+++ b/solution.py
@@ -778,9 +778,17 @@
         places_out="vvvh" if summing else "vvvv",
     )
     if summing:
-        owned = lax.psum_scatter(
-            grads.reshape(chips * block, channels), "batch", scatter_dimension=0,
-            axis_index_groups=[list(range(core, batches, 2)) for core in range(2)], tiled=True,
+        groups = [list(range(core, batches, 2)) for core in range(2)]
+        half = channels // 2
+        owned = jnp.concatenate(
+            [
+                lax.psum_scatter(
+                    grads.reshape(chips * block, channels)[:, cut : cut + half], "batch",
+                    scatter_dimension=0, axis_index_groups=groups, tiled=True,
+                )
+                for cut in (0, half)
+            ],
+            axis=1,
         )
     else:
         owned = lax.psum_scatter(grads, "batch", scatter_dimension=0, tiled=True)

time: 363 us -> 381 us (1.050)
  waiting for transfers between devices: 9.86 us -> 23.5 us
    reduce_scatter x1 -> x2, waiting for transfers between devices: 5.2 us -> 18.2 us  [head(): lax.psum_scatter(grads.reshape(chips * block, channels)[:, cut:cut + half...]
  transfers between devices with their start and end apart: 2 -> 3, of which waited for: 2 -> 2; matrix products, arithmetic and copies ran while one was open for 2% -> 2% of each run, Pallas kernels for 28% -> 26%
where the time goes in v6:
time: 381 us; the launch traced here: 378 us
  Pallas kernels  319 us (84%)
  waiting for transfers between devices  23.5 us (6%)
  between operations  15.2 us (4%)
  local copies, waits for them, and re-layouts  12.4 us (3%)
  other arithmetic  7.6 us (2%)
    pallas_call x6, Pallas kernels, exchange_kernel(): pl.pallas_call(body, out_shape=tuple(outs), in_specs=[SPECS[s] for s in s...  267 us
    pallas_call x1, Pallas kernels, finish(): pl.pallas_call(renew_body, out_shape=(*outs[:8], shape(own, BF)), in_spec...  38.9 us
    reduce_scatter x2, waiting for transfers between devices, head(): lax.psum_scatter(grads.reshape(chips * block, channels)[:, cut:cut + half...  18.2 us
    pallas_call x1, Pallas kernels, to_slots(): pl.pallas_call(to_slots_body, out_shape=shape(dims, BF), in_specs=[SMEM_S...  12.9 us
  transfers between devices with their start and end apart: 3, of which 2 were waited for; matrix products, arithmetic and copies ran while one was open for 2% of the time, Pallas kernels for 26%

profile of v6, /device:TPU:0, one launch (start us, length us, event | category | flops | bytes accessed | tf_op | source)
XLA Modules:
  0.0 377.7 jit_solution(7251154257483199169)
XLA Ops:
  7.2 0.0 all-gather.2.cloned.1.call-start
  7.2 0.1 iota_add_fusion
  7.3 0.7 copy.62
  8.0 0.1 broadcast_compare_fusion
  8.1 0.1 eq.42
  8.9 0.1 and.53
  9.0 0.1 and.54
  9.1 0.1 and.56
  9.3 0.1 scatter.14.info
  9.3 0.0 copy-start.10
  9.4 0.6 copy-done.10
  10.0 0.0 copy-start.7
  10.0 0.0 copy-start.8
  10.0 0.0 copy-start.4
  10.0 0.0 copy-start.5
  10.0 0.0 copy-start.6
  10.0 31.2 %shard_map.358 = (bf16[9216,128]{1,0:T(8,128)(2,1)}, bf16[1728,512]{1,0:T(8,128)(2,1)}, f32[32,512]{1,0:T(8,128)}, f32[1152,2]{1,0:T(8,128)}, bf16[704,512]{1,0:T(8,128)(2,1)}) custom-call(bf16[432,512]{1,0:T(8,128)(2,1)} %bitcast.58, f32[8,512]{1,0:T(8,128)} %copy-done.10, s32[72,128]{1,0:T(8,128)} %bitcast.59, f32[1152,512]{1,0:T(8,128)} %weight.3, ...), custom_call_target="tpu_custom_call" | custom-call | flops 20971520000 | bytes 9221120 | tf_op jit(solution)/shard_map/pallas_call | solution.py:236
  41.2 0.0 all-gather.2.cloned.1.call-update
  41.2 0.3 reduce-scatter.5.cloned.1.call-start
  41.5 0.0 copy-done.7
  41.5 0.0 copy-done.8
  41.5 0.6 copy.43
  42.1 0.0 copy-done.4
  42.1 0.8 copy.44.cotangent
  42.9 0.0 copy-done.5
  43.0 0.0 copy-done.6
  43.0 0.6 reshape.263.scales
  43.6 54.8 %shard_map.359 = (f32[8,128]{1,0:T(8,128)}, f32[8,128]{1,0:T(8,128)}, bf16[1728,512]{1,0:T(8,128)(2,1)}, bf16[512,1152]{1,0:T(8,128)(2,1)}, bf16[512,1152]{1,0:T...) custom-call(s32[9216]{0:T(1024)} %index.3, f32[32,512]{1,0:T(8,128)} %get-tuple-element.77.infos, ...), custom_call_target="tpu_custom_call" | custom-call | flops 4076863488 | bytes 11909120 | tf_op jit(solution)/shard_map/pallas_call | solution.py:236
  98.4 4.6 %all-gather.2.cloned.1.call-done.weights = bf16[5632,512]{1,0:T(8,128)(2,1)} async-done(((bf16[704,512]{1,0:T(8,128)(2,1)}), bf16[5632,512]{1,0:T(8,128)(2,1)}) %all-gather.2.cloned.1.call-update) | async-done | bytes 5767184 | tf_op jit(solution)/shard_map/all_gather | solution.py:1898
  103.0 82.3 %shard_map.360 = (bf16[4,108,512]{2,1,0:T(8,128)(2,1)}, f32[1728,128]{1,0:T(8,128)}, f32[8,512]{1,0:T(8,128)}, bf16[4,704,512]{2,1,0:T(8,128)(2,1)}) custom-call(f32[32,512]{1,0:T(8,128)} %get-tuple-element.77.infos, bf16[1728,512]{1,0:T(8,128)(2,1)} %get-tuple-element.80.features, bf16[5632,512]{1,0:T(8,128)(2,1)} %all-gather.2.cloned.1.call-done.weights, ...), custom_call_target="tpu_custom_call" | custom-call | flops 29896998912 | bytes 12288000 | tf_op jit(solution)/shard_map/pallas_call | solution.py:236
  185.3 3.6 fusion.6
  188.9 0.0 reduce-scatter.5.cloned.1.call-update
  188.9 0.0 reduce-scatter.3.cloned.1.call-start
  188.9 0.7 reduce-scatter.3.cloned.1.call-update
  189.6 0.2 copy-done.3
  189.9 1.1 copy.45
  191.0 0.0 copy-start.12
  191.0 31.9 %shard_map.361 = (f32[512,1152]{1,0:T(8,128)}, f32[512,1152]{1,0:T(8,128)}, bf16[1728,512]{1,0:T(8,128)(2,1)}, f32[8,512]{1,0:T(8,128)}) custom-call(f32[32,512]{1,0:T(8,128)} %get-tuple-element.77.infos, f32[1728,128]{1,0:T(8,128)} %get-tuple-element.84.upstream, f32[8,128]{1,0:T(8,128)} %get-tuple-element.82.counts.enc_totals, ...), custom_call_target="tpu_custom_call" | custom-call | flops 8153726976 | bytes 15132672 | tf_op jit(solution)/shard_map/pallas_call | solution.py:236
  222.9 0.7 slice.57
  223.6 0.0 copy-done.13
  223.6 0.0 copy-done.14
  223.7 0.6 copy.49
  224.3 0.6 copy.50
  224.9 0.6 copy.51
  225.5 0.0 copy-done.9
  225.5 0.2 rev.7
  225.7 0.0 copy-done.11
  225.7 0.0 copy-done.12
  225.7 0.7 maximum_subtract_fusion
  226.4 12.9 %shard_map.362.slots = bf16[9216,128]{1,0:T(8,128)(2,1)} custom-call(s32[9216]{0:T(1024)} %index.3, f32[512,1152]{1,0:T(8,128)} %get-tuple-element.91.enc_far, f32[512,1152]{1,0:T(8,128)} %get-tuple-element.92.dec_far), custom_call_target="tpu_custom_call" | custom-call | flops 10485760000 | bytes 8388608 | tf_op jit(solution)/shard_map/pallas_call | solution.py:1026
  239.3 0.0 reduce-scatter.5.cloned.1.call-done
  239.3 18.2 %reduce-scatter.3.cloned.1.call-done = bf16[704,256]{1,0:T(8,128)(2,1)} async-done(((bf16[2816,256]{1,0:T(8,128)(2,1)}), bf16[704,256]{1,0:T(8,128)(2,1)}) %reduce-scatter.3.cloned.1.call-update) | async-done | bytes 360464 | tf_op jit(solution)/shard_map/reduce_scatter | solution.py:785
  257.5 2.0 pad_maximum_fusion.head_far
  259.5 60.5 %shard_map.363 = (f32[432,512]{1,0:T(8,128)}, f32[3,1152,512]{2,1,0:T(8,128)}, f32[3,704,512]{2,1,0:T(8,128)}, bf16[1024,512]{1,0:T(8,128)(2,1)}, bf16[3840,128]{1,0:T(8,128)(2,1)}) custom-call(bf16[9216,128]{1,0:T(8,128)(2,1)} %shard_map.362.slots, bf16[1728,512]{1,0:T(8,128)(2,1)} %get-tuple-element.93.flow, f32[1152,2]{1,0:T(8,128)} %get-tuple-element.94.owners, ...), custom_call_target="tpu_custom_call" | custom-call | flops 52428800000 | bytes 35824640 | tf_op jit(solution)/shard_map/pallas_call | solution.py:236
  320.1 38.9 %shard_map.364 = (f32[1152,512]{1,0:T(8,128)}, f32[1152,512]{1,0:T(8,128)}, f32[1152,512]{1,0:T(8,128)}, f32[704,512]{1,0:T(8,128)}, f32[704,512]{1,0:T(8,128)},...) custom-call(s32[1]{0:T(128)} %bitcast.18.core, ...), custom_call_target="tpu_custom_call" | custom-call | flops 52428800000 | bytes 67108864 | tf_op jit(solution)/shard_map/pallas_call | solution.py:1808
  358.9 0.0 copy-start
  358.9 6.2 %shard_map.365 = bf16[3,512,512]{2,1,0:T(8,128)(2,1)} custom-call(bf16[3,512,512]{2,1,0:T(8,128)(2,1)} %get-tuple-element.105.x), custom_call_target="tpu_custom_call" | custom-call | flops 5242880000 | bytes 3145728 | tf_op jit(solution)/shard_map/pallas_call | solution.py:236
  365.1 0.0 copy-done
  365.1 0.0 copy-start.1
  365.2 2.8 select_convert_fusion
  368.0 0.0 copy-done.1
  368.0 1.9 bitcast_convert_fusion
  369.8 0.0 copy-done.2
  369.8 0.9 copy.66
  (18 shorter events, 0.2 us)
Async XLA Ops:
  7.2 95.8 %all-gather.2.cloned.1.call-start = ((), (), s32[]{:S(2)}) async-start(), calls=%async_computation.2 | async-start | bytes 6488064 | tf_op jit(solution)/shard_map/all_gather | solution.py:1898
  9.3 0.6 copy-start.10
  10.0 31.5 %copy-start.7 = (f32[2,512]{1,0:T(2,128)S(1)}, f32[2,512]{1,0:T(2,128)}, u32[]{:S(2)}) copy-start(f32[2,512]{1,0:T(2,128)} %param.41) | copy-start | bytes 12292
  10.0 31.5 %copy-start.8 = (f32[2,512]{1,0:T(2,128)S(1)}, f32[2,512]{1,0:T(2,128)}, u32[]{:S(2)}) copy-start(f32[2,512]{1,0:T(2,128)} %param.42) | copy-start | bytes 12292
  10.0 32.1 %copy-start.4 = (bf16[1,4,1,9,12,512]{5,1,4,3,2,0:T(4,128)(2,1)S(1)}, bf16[1,4,1,9,12,512]{5,1,4,3,2,0:T(4,128)(2,1)}, u32[]{:S(2)}) copy-start(bf16[1,4,1,9,12,512]{5,1,4,3,2,0:T(4,128)(2,1)} %param.49) | copy-start | bytes 1327108
  10.0 33.0 %copy-start.5 = (f32[1,3,512]{2,0,1:T(1,128)S(1)}, f32[1,3,512]{2,0,1:T(1,128)}, u32[]{:S(2)}) copy-start(f32[1,3,512]{2,0,1:T(1,128)} %param.46) | copy-start | bytes 18436
  10.0 33.0 %copy-start.6 = (f32[1,3,512]{2,0,1:T(1,128)S(1)}, f32[1,3,512]{2,0,1:T(1,128)}, u32[]{:S(2)}) copy-start(f32[1,3,512]{2,0,1:T(1,128)} %param.45) | copy-start | bytes 18436
  41.2 198.1 %reduce-scatter.5.cloned.1.call-start = ((), (), s32[]{:S(2)}) async-start(), calls=%async_computation.4 | async-start | bytes 1802240 | tf_op jit(solution)/shard_map/reduce_scatter | solution.py:785
  188.9 1.0 copy-start.3
  188.9 68.6 %reduce-scatter.3.cloned.1.call-start = ((), (), s32[]{:S(2)}) async-start(), calls=%async_computation.3 | async-start | bytes 1802240 | tf_op jit(solution)/shard_map/reduce_scatter | solution.py:785
  191.0 32.6 %copy-start.13 = (f32[2,2,512]{2,1,0:T(2,128)S(1)}, f32[2,2,512]{2,1,0:T(2,128)}, u32[]{:S(2)}) copy-start(f32[2,2,512]{2,1,0:T(2,128)} %param.43) | copy-start | bytes 24580
  191.0 32.7 %copy-start.14 = (f32[2,2,512]{2,1,0:T(2,128)S(1)}, f32[2,2,512]{2,1,0:T(2,128)}, u32[]{:S(2)}) copy-start(f32[2,2,512]{2,1,0:T(2,128)} %param.44) | copy-start | bytes 24580
  191.0 34.5 %copy-start.9 = (f32[8,512]{1,0:T(8,128)S(1)}, f32[8,512]{1,0:T(8,128)}, u32[]{:S(2)}) copy-start(f32[8,512]{1,0:T(8,128)} %get-tuple-element.111) | copy-start | bytes 49156
  191.0 34.7 %copy-start.11 = (f32[1,3,2,512]{3,2,1,0:T(2,128)S(1)}, f32[1,3,2,512]{3,2,1,0:T(2,128)}, u32[]{:S(2)}) copy-start(f32[1,3,2,512]{3,2,1,0:T(2,128)} %param.47) | copy-start | bytes 36868
  191.0 34.7 %copy-start.12 = (f32[1,3,2,512]{3,2,1,0:T(2,128)S(1)}, f32[1,3,2,512]{3,2,1,0:T(2,128)}, u32[]{:S(2)}) copy-start(f32[1,3,2,512]{3,2,1,0:T(2,128)} %param.48) | copy-start | bytes 36868
  358.9 6.2 %copy-start = (bf16[3,512,512]{2,1,0:T(8,128)(2,1)S(1)}, bf16[3,512,512]{2,1,0:T(8,128)(2,1)}, u32[]{:S(2)}) copy-start(bf16[3,512,512]{2,1,0:T(8,128)(2,1)} %get-tuple-element.105.x) | copy-start | bytes 4718596
  365.1 2.8 copy-start.1
  368.0 1.9 copy-start.2
Sparse Core Ops, SparseCore 0:
  41.3 61.6 all-gather.1
  189.0 33.3 reduce-scatter.4
  225.3 32.1 reduce-scatter.2
